TPU v7x, 256 devices: a whole 4x4x8 slice. The times are simulated.
256 devices in a mesh: dom: 16 (over y, x), feat: 16 (over z, core).
Axes of the slice: x: 4, y: 4, z: 8, core: 2. Of those that a mesh axis runs over, the one named last changes fastest.
Arguments:
- feature_table: float32 [1024, 131072], P('feat', 'dom'), may hold values from -6 to 6
- seed_ids: int32 [16384], P('dom'), may hold values from 0 to 8191
- neighbours: int32 [15, 16384], P(None, 'dom'), may hold values from 0 to 8191
- owners: int32 [1024, 1], P('dom'), may hold values from 0 to 15; in each aligned block of 64 rows (0 to 63, 64 to 127, ...) at most 8 rows name the same one
- blocks: int32 [1024], P('dom'), may hold values from 0 to 63
- counts: int32 [1024], P('dom'), may hold values from 1 to 128
- w_self: float32 [1024, 1024], P('feat'), may hold values from -0.1875 to 0.1875
- w_neigh: float32 [1024, 1024], P('feat'), may hold values from -0.5 to 0.5
- out_bias: float32 [1024], replicated, may hold values from -3 to 3
- cotangent: bfloat16 [16384, 1024], P(('dom', 'feat')), may hold values from -0.046875 to 0.046875
Outputs:
- hidden: bfloat16 [16384, 1024], P(('dom', 'feat'))
- grad_self: float32 [1024, 1024], P('feat')
- grad_neigh: float32 [1024, 1024], P('feat')
Inputs may be any that keep to these rules, and one draw needn't show every extreme that they name: `owners`: among the 64 frontier entries of one partition no owner appears more than 8 times.
All inputs are finite; a program needn't handle non-finite values.
Results may differ from a plain program's by a relative error of at most 0.003.
Values may be sent and summed in bfloat16 or wider, within the bound.
No kernel may reach another device: no remote copies, remote signals or barrier semaphores. Data moves between devices by JAX's collectives and lax.ppermute only.
A program may use at most 128 MiB of HBM per device.

v0:
```python
import jax
import jax.numpy as jnp
from jax import lax
from jax.sharding import PartitionSpec as P

FAN = 15
BLOCK = 128
SLOTS = 8


def silu_slope(preact):
    sigma = jax.nn.sigmoid(preact)
    return sigma * (1.0 + preact * (1.0 - sigma))


def contract(left, right):
    return lax.dot_general(
        left,
        right,
        (((0,), (0,)), ((), ())),
        precision=lax.Precision.HIGHEST,
        preferred_element_type=jnp.float32,
    )


def product(left, right):
    return lax.dot_general(
        left,
        right,
        (((1,), (0,)), ((), ())),
        precision=lax.Precision.HIGHEST,
        preferred_element_type=jnp.float32,
    )


def body(
    feature_table,
    seed_ids,
    neighbours,
    owners,
    blocks,
    counts,
    w_self,
    w_neigh,
    out_bias,
    cotangent,
):
    cols_dev = feature_table.shape[0]
    node_rows = feature_table.shape[1]
    n_dom = lax.axis_size("dom")
    front = owners.shape[0]
    seeds_dev = seed_ids.shape[0]
    fanout = neighbours.shape[0]
    owner_ids = owners[:, 0]
    one_hot = (owner_ids[:, None] == jnp.arange(n_dom, dtype=jnp.int32)[None, :]).astype(jnp.int32)
    slot_rank = jnp.sum(jnp.cumsum(one_hot, axis=0) * one_hot, axis=1) - 1
    outgoing_ids = jnp.zeros((n_dom, SLOTS), jnp.int32).at[owner_ids, slot_rank].set(blocks)
    requested = lax.all_to_all(outgoing_ids, "dom", split_axis=0, concat_axis=0, tiled=True)
    table_rows = jnp.transpose(feature_table)
    block_rows = table_rows.reshape(node_rows // BLOCK, BLOCK, cols_dev)
    outgoing = block_rows[requested.reshape(-1)].reshape(n_dom, SLOTS, BLOCK, cols_dev)
    arrived = lax.all_to_all(outgoing, "dom", split_axis=0, concat_axis=0, tiled=True)
    arrived_flat = arrived.reshape(n_dom * SLOTS, BLOCK, cols_dev)
    frontier = arrived_flat[owner_ids * SLOTS + slot_rank]
    row_valid = jnp.arange(BLOCK, dtype=jnp.int32)[None, :] < counts[:, None]
    frontier = jnp.where(row_valid[:, :, None], frontier, 0.0).reshape(front * BLOCK, cols_dev)
    picked = frontier[neighbours.reshape(-1)].reshape(fanout, seeds_dev, cols_dev)
    neighbour_mean = jnp.sum(picked, axis=0) * (1.0 / FAN)
    self_rows = table_rows[seed_ids]
    stacked = jnp.concatenate([self_rows, neighbour_mean], axis=1)
    weight_cat = jnp.concatenate([w_self, w_neigh], axis=0)
    preact = (
        lax.psum_scatter(product(stacked, weight_cat), "feat", scatter_dimension=0, tiled=True)
        + out_bias[None, :]
    )
    hidden = jax.nn.silu(preact).astype(jnp.bfloat16)
    slope = (cotangent.astype(jnp.float32) * silu_slope(preact)).astype(jnp.bfloat16)
    grad_local = contract(
        stacked, lax.all_gather(slope, "feat", axis=0, tiled=True).astype(jnp.float32)
    )
    grad_total = lax.psum(grad_local, "dom")
    return (hidden, grad_total[:cols_dev], grad_total[cols_dev:])


def solution(mesh):
    return jax.shard_map(
        body,
        mesh=mesh,
        in_specs=(
            P("feat", "dom"),
            P("dom"),
            P(None, "dom"),
            P("dom", None),
            P("dom"),
            P("dom"),
            P("feat", None),
            P("feat", None),
            P(),
            P(("dom", "feat"), None),
        ),
        out_specs=(P(("dom", "feat"), None), P("feat", None), P("feat", None)),
        check_vma=False,
    )
```

profile of v0, /device:TPU:64, one launch (start us, length us, event | category | flops | bytes accessed | tf_op | source)
XLA Modules:
  0.0 395.9 jit_solution(11303320467679522365)
XLA Ops:
  7.2 0.7 fusion.5
  7.9 0.1 reduce_window_sum.11
  8.0 0.8 select_reduce_fusion
  8.8 0.7 fusion.10
  9.5 5.7 %scatter_fusion = s32[16,8]{0,1:T(8,128)S(1)} fusion(s32[16,8]{0,1:T(8,128)S(1)} %broadcast_in_dim.18, s32[64]{0:T(128)S(1)} %get-tuple-element.8, s32[64]{0:T(128)} %param.14), kind=kCustom, calls=%fused_computation.4 | custom fusion | bytes 1280 | tf_op jit(solution)/shard_map/scatter | solution.py:57
  15.3 0.7 copy.24
  15.9 7.0 %all-to-all-start = ((s32[16,1,8]{2,1,0:T(1,128)}), s32[16,1,8]{2,1,0:T(1,128)S(1)}, u32[]{:S(2)}, u32[]{:S(2)}) async-start(s32[16,1,8]{2,1,0:T(1,128)} %copy.24), calls=%async_computation | async-start | bytes 16384 | tf_op jit(solution)/shard_map/all_to_all | solution.py:58
  23.0 0.7 fusion.6
  23.7 3.8 copy.23
  27.5 2.9 all-to-all-done
  30.4 0.5 broadcast.144
  31.0 0.7 reduce.3
  31.6 0.1 reshape.132
  31.7 6.5 %gather_fusion.1 = f32[128,128,64]{2,1,0:T(8,128)} fusion(f32[64,128,64]{2,1,0:T(8,128)} %bitcast.37, s32[1024]{0:T(1024)S(1)} %pad_clamp_fusion.1), kind=kCustom, calls=%fused_computation.1 | custom fusion | bytes 8389120 | tf_op jit(solution)/shard_map/gather | solution.py:61
  38.2 6.8 %copy.25 = f32[128,128,64]{1,2,0:T(8,128)} copy(f32[128,128,64]{2,1,0:T(8,128)} %gather_fusion.1) | data formatting | bytes 8388608 | tf_op jit(solution)/shard_map/gather | solution.py:61
  45.1 4.7 %all-to-all-start.1 = ((f32[16,8,128,64]{2,3,1,0:T(8,128)}), f32[16,8,128,64]{2,3,1,0:T(8,128)}, u32[]{:S(2)}, u32[]{:S(2)}) async-start(f32[16,8,128,64]{2,3,1,0:T(8,128)} %bitcast.40), calls=%async_computation.1 | async-start | bytes 8388608 | tf_op jit(solution)/shard_map/all_to_all | solution.py:62
  49.8 0.1 copy.30
  49.9 5.0 %gather_fusion = f32[1024,64]{1,0:T(8,128)S(1)} fusion(f32[8192,64]{1,0:T(8,128)} %bitcast.38, s32[1024]{0:T(1024)S(1)} %fusion.7), kind=kCustom, calls=%fused_computation | custom fusion | bytes 528384 | tf_op jit(solution)/shard_map/gather | solution.py:69
  54.9 0.1 compare_select_fusion
  55.0 55.8 %all-to-all-done.1 = f32[16,8,128,64]{2,3,1,0:T(8,128)} async-done(((f32[16,8,128,64]{2,3,1,0:T(8,128)}), f32[16,8,128,64]{2,3,1,0:T(8,128)}, u32[]{:S(2)}, u32[]{:S(2)}) %all-to-all-start.1) | async-done | bytes 4194336 | tf_op jit(solution)/shard_map/all_to_all | solution.py:62
  110.8 2.9 gather_fusion.2
  113.7 2.7 copy.28
  116.4 7.4 %bitcast_select_fusion = f32[8192,64]{1,0:T(8,128)} fusion(f32[64,128,64]{2,1,0:T(8,128)} %copy.28, pred[8192]{0:T(1024)(128)(4,1)S(1)} %fusion.6), kind=kLoop, calls=%fused_computation.5 | loop fusion | flops 524288 | bytes 4202496 | tf_op jit(solution)/shard_map/jit(_where)/select_n | solution.py:66
  123.8 53.7 %gather_fusion.3 = f32[15360,64]{1,0:T(8,128)} fusion(f32[8192,64]{1,0:T(8,128)} %bitcast_select_fusion, s32[15360]{0:T(1024)S(1)} %broadcast_clamp_fusion), kind=kCustom, calls=%fused_computation.3 | custom fusion | bytes 7925760 | tf_op jit(solution)/shard_map/gather | solution.py:67
  177.5 3.9 reduce_sum.19
  181.5 5.1 %fusion = f32[1024,1024]{1,0:T(8,128)} fusion(f32[64,1024]{1,0:T(8,128)S(1)} %copy-done, f32[64,1024]{1,0:T(8,128)S(1)} %copy-done.1, f32[1024,64]{1,0:T(8,128)S(1)} %broadcast_multiply_fusion, f32[1024,64]{1,0:T(8,128)S(1)} %gather_fusion), kind=kOutput, calls=%fused_computation.7 | convolution fusion | flops 1610874880 | bytes 5242880 | tf_op jit(solution)/shard_map/dot_general | solution.py:27
  186.6 57.1 %reduce-scatter.2.cloned.1.call-done = f32[64,1024]{1,0:T(8,128)} async-done(((f32[1024,1024]{1,0:T(8,128)}), f32[64,1024]{1,0:T(8,128)}) %reduce-scatter.2.cloned.1.call-update) | async-done | bytes 262160 | tf_op jit(solution)/shard_map/reduce_scatter | solution.py:73
  243.7 1.8 multiply_convert_fusion
  245.5 43.0 %all-gather.2.cloned.1.call-done = bf16[1024,1024]{1,0:T(8,128)(2,1)} async-done(((bf16[64,1024]{1,0:T(8,128)(2,1)}), bf16[1024,1024]{1,0:T(8,128)(2,1)}) %all-gather.2.cloned.1.call-update) | async-done | bytes 2097168 | tf_op jit(solution)/shard_map/all_gather | solution.py:79
  288.5 3.7 fusion.4
  292.2 95.3 %all-reduce.2.cloned.1.call-done = f32[128,1024]{1,0:T(8,128)} async-done(((f32[128,1024]{1,0:T(8,128)}), f32[128,1024]{1,0:T(8,128)}) %all-reduce.2.cloned.1.call-update) | async-done | bytes 524304 | tf_op jit(solution)/shard_map/psum | solution.py:81
  387.5 1.9 fusion.14
  (25 shorter events, 0.3 us)
Async XLA Ops:
  15.9 14.5 %all-to-all-start = ((s32[16,1,8]{2,1,0:T(1,128)}), s32[16,1,8]{2,1,0:T(1,128)S(1)}, u32[]{:S(2)}, u32[]{:S(2)}) async-start(s32[16,1,8]{2,1,0:T(1,128)} %copy.24), calls=%async_computation | async-start | bytes 16384 | tf_op jit(solution)/shard_map/all_to_all | solution.py:58
  45.0 4.7 %copy-start.5 = (s32[1024]{0:T(1024)S(1)}, s32[1024]{0:T(1024)}, u32[]{:S(2)}) copy-start(s32[1024]{0:T(1024)} %param.11) | copy-start | bytes 12292
  45.0 4.7 %copy-start.3 = (s32[15,1024]{1,0:T(8,128)S(1)}, s32[15,1024]{1,0:T(8,128)}, u32[]{:S(2)}) copy-start(s32[15,1024]{1,0:T(8,128)} %param.12) | copy-start | bytes 184324
  45.1 65.7 %all-to-all-start.1 = ((f32[16,8,128,64]{2,3,1,0:T(8,128)}), f32[16,8,128,64]{2,3,1,0:T(8,128)}, u32[]{:S(2)}, u32[]{:S(2)}) async-start(f32[16,8,128,64]{2,3,1,0:T(8,128)} %bitcast.40), calls=%async_computation.1 | async-start | bytes 8388608 | tf_op jit(solution)/shard_map/all_to_all | solution.py:62
  49.7 193.9 %reduce-scatter.2.cloned.1.call-start = ((), (), s32[]{:S(2)}) async-start(), calls=%async_computation.3 | async-start | bytes 4456448 | tf_op jit(solution)/shard_map/reduce_scatter | solution.py:73
  177.5 4.0 copy-start
  177.5 4.0 %copy-start.1 = (f32[64,1024]{1,0:T(8,128)S(1)}, f32[64,1024]{1,0:T(8,128)}, u32[]{:S(2)}) copy-start(f32[64,1024]{1,0:T(8,128)} %param.16) | copy-start | bytes 786436
  181.4 62.2 %copy-start.2 = (bf16[64,1024]{1,0:T(8,128)(2,1)S(1)}, bf16[64,1024]{1,0:T(8,128)(2,1)}, u32[]{:S(2)}) copy-start(bf16[64,1024]{1,0:T(8,128)(2,1)} %param.19) | copy-start | bytes 393220
  181.4 62.2 %copy-start.4 = (f32[1024]{0:T(1024)S(1)}, f32[1024]{0:T(1024)}, u32[]{:S(2)}) copy-start(f32[1024]{0:T(1024)} %param.18) | copy-start | bytes 12292
  186.5 102.0 %all-gather.2.cloned.1.call-start = ((), (), s32[]{:S(2)}) async-start(), calls=%async_computation.4 | async-start | bytes 2228224 | tf_op jit(solution)/shard_map/all_gather | solution.py:79
  245.5 142.0 %all-reduce.2.cloned.1.call-start = ((), (), s32[]{:S(2)}) async-start(), calls=%async_computation.5 | async-start | bytes 1048576 | tf_op jit(solution)/shard_map/psum | solution.py:81
Sparse Core Ops, SparseCore 0:
  186.7 56.9 reduce-scatter.1
  246.1 42.3 all-gather.1
  292.3 95.1 all-reduce.1
where the time goes:
time: 397 us; the launch traced here: 396 us
  waiting for transfers between devices  254 us (64%)
  local copies, waits for them, and re-layouts  90.3 us (23%)
  other arithmetic  17 us (4%)
  between operations  13.9 us (4%)
  starting transfers between devices  11.8 us (3%)
  matrix products  8.71 us (2%)
    psum x1, waiting for transfers between devices, body(): grad_total = lax.psum(grad_local, 'dom')  95.3 us
    reduce_scatter x1, waiting for transfers between devices, body(): lax.psum_scatter(product(stacked, weight_cat), 'feat', scatter_dimension=...  57.1 us
    all_to_all x1, waiting for transfers between devices, body(): lax.all_to_all(outgoing, 'dom', split_axis=0, concat_axis=0, tiled=True)  55.8 us
    gather x1, local copies, waits for them, and re-layouts, body(): frontier[neighbours.reshape(-1)].reshape(fanout, seeds_dev, cols_dev)  53.7 us
    all_gather x1, waiting for transfers between devices, body(): lax.all_gather(slope, 'feat', axis=0, tiled=True).astype(jnp.float32)  43 us
    gather x2, local copies, waits for them, and re-layouts, body(): block_rows[requested.reshape(-1)].reshape(n_dom, SLOTS, BLOCK, cols_dev)  13.3 us
  transfers between devices with their start and end apart: 5, of which 5 were waited for; matrix products, arithmetic and copies ran while one was open for 2% of the time, Pallas kernels for 0%

commit v1 on v0

v1 whole, which is shorter than its diff:
```python
import functools

import jax
import jax.numpy as jnp
from jax import lax
from jax.experimental import pallas as pl
from jax.experimental.pallas import tpu as pltpu
from jax.sharding import PartitionSpec as P

FAN = 15
BLOCK = 128
SLOTS = 8
HALF = BLOCK // 2
F32 = jnp.float32
BF16 = jnp.bfloat16
SMEM = pl.BlockSpec(memory_space=pltpu.SMEM)
VMEM = pl.BlockSpec(memory_space=pltpu.VMEM)


def lane_of(shape):
    return lax.broadcasted_iota(jnp.int32, shape, len(shape) - 1)


def split(value):
    high = value.astype(BF16)
    low = (value - high.astype(F32)).astype(BF16)
    return high, low


def dot(left, right):
    return jnp.dot(left, right, preferred_element_type=F32)


def prepare_kernel(core_ref, seed_ref, table_ref, packed_ref, self_ref, rows):
    core = core_ref[0]
    blocks = table_ref.shape[1] // BLOCK
    first = lane_of((HALF, BLOCK)) < HALF

    def turn(pair, carry):
        start = pl.multiple_of(pair * 2 * BLOCK, 2 * BLOCK)
        left = table_ref[:, pl.ds(start, BLOCK)]
        right = table_ref[:, pl.ds(start + BLOCK, BLOCK)]
        turned = jnp.concatenate([left, right], axis=0).T
        rows[pl.ds(start, BLOCK), :] = turned
        rows[pl.ds(start + BLOCK, BLOCK), :] = pltpu.roll(turned, HALF, 1)
        for which in range(2):
            near = pl.multiple_of(start + which * BLOCK + core * HALF, HALF)
            far = pl.multiple_of(start + (1 - which) * BLOCK + (1 - core) * HALF, HALF)
            both = jnp.where(first, rows[pl.ds(near, HALF), :], rows[pl.ds(far, HALF), :])
            packed_ref[2 * pair + which] = both.astype(BF16)
        return carry

    lax.fori_loop(0, blocks // 2, turn, 0, unroll=2)

    lane = lane_of((1, BLOCK)) < HALF

    def pick(group, carry):
        for step in range(32):
            lead = seed_ref[group * 64 + step + 32 * core]
            trail = seed_ref[group * 64 + step + 32 * (1 - core)]
            low = rows[pl.ds(lead, 1), :]
            high = rows[pl.ds(lax.bitwise_xor(trail, BLOCK), 1), :]
            self_ref[lax.rem(group, 2), lax.div(group, 2), pl.ds(step, 1), :] = jnp.where(lane, low, high)
        return carry

    lax.fori_loop(0, seed_ref.shape[0] // 64, pick, 0)


def pack_kernel(me_ref, request_ref, packed_ref, out_ref, wanted, wanted_smem, sem):
    me = me_ref[0]
    request = request_ref[...]
    parts = request.shape[0]
    lane = lane_of(request.shape)
    mine = jnp.logical_and(request == me, lane < HALF)
    below = lax.broadcasted_iota(jnp.int32, (BLOCK, BLOCK), 0) <= lane_of((BLOCK, BLOCK))
    rank = dot(mine.astype(BF16), below.astype(BF16))
    block = pltpu.roll(request, HALF, 1).astype(F32)
    result = jnp.zeros(request.shape, F32)
    for slot in range(SLOTS):
        hit = jnp.logical_and(mine, rank == slot + 1.0)
        chosen = jnp.sum(jnp.where(hit, block, 0.0), axis=1, keepdims=True)
        result = jnp.where(lane == slot, chosen, result)
    wanted[...] = result.astype(jnp.int32)
    copy = pltpu.make_async_copy(wanted, wanted_smem, sem)
    copy.start()
    copy.wait()

    def send(part, carry):
        for slot in range(SLOTS):
            out_ref[part, slot] = packed_ref[wanted_smem[part, slot]]
        return carry

    lax.fori_loop(0, parts, send, 0)


def gather_kernel(core_ref, owner_ref, count_ref, near_ref, own_ref, other_ref, out_ref, front, seen):
    core = core_ref[0]
    n_dom = own_ref.shape[0] // SLOTS
    for owner in range(n_dom):
        seen[owner] = 0
    lane = lane_of((HALF, BLOCK))
    row = lax.broadcasted_iota(jnp.int32, (HALF, BLOCK), 0)
    straight = (lane < HALF) == (core == 0)

    def place(entry, carry):
        owner = owner_ref[entry]
        rank = seen[owner]
        seen[owner] = rank + 1
        slot = owner * SLOTS + rank
        own = own_ref[slot].astype(F32)
        other = other_ref[slot].astype(F32)
        count = count_ref[entry]
        upper = jnp.where(straight, own, other)
        lower = pltpu.roll(jnp.where(straight, other, own), HALF, 1)
        start = pl.multiple_of(entry * BLOCK, BLOCK)
        front[pl.ds(start, HALF), :] = jnp.where(row < count, upper, 0.0)
        front[pl.ds(start + HALF, HALF), :] = jnp.where(row < count - HALF, lower, 0.0)
        return carry

    lax.fori_loop(0, owner_ref.shape[0], place, 0, unroll=4)

    def average(step, carry):
        group, part = lax.div(step, 4), lax.rem(step, 4)
        base = ((2 * group + core) * 64 + part * 16) * FAN
        for seed in range(16):
            terms = [front[pl.ds(near_ref[base + seed * FAN + k], 1), :] for k in range(FAN)]
            while len(terms) > 1:
                terms = [
                    terms[i] + terms[i + 1] if i + 1 < len(terms) else terms[i]
                    for i in range(0, len(terms), 2)
                ]
            out_ref[group, pl.ds(part * 16 + seed, 1), :] = terms[0] * (1.0 / FAN)
        return carry

    lax.fori_loop(0, 32, average, 0)


def join_kernel(core_ref, own_ref, other_ref, out_ref):
    straight = (lane_of((32, BLOCK)) < HALF) == (core_ref[0] == 0)
    for group in range(8):
        own, other = own_ref[group], other_ref[group]
        out_ref[group, :32] = jnp.where(straight, own, other)
        out_ref[group, 32:] = pltpu.roll(jnp.where(straight, other, own), HALF, 1)


def three(left, right_high, right_low):
    high, low = split(left)
    return dot(high, right_high) + (dot(high, right_low) + dot(low, right_high))


def self_kernel(self_ref, weight_ref, bias_ref, part_ref, high_ref, low_ref):
    part_ref[...] = jnp.broadcast_to(bias_ref[...], part_ref.shape)
    for step in range(4):
        left = jnp.concatenate([self_ref[2 * step], self_ref[2 * step + 1]], axis=1)
        own = jnp.concatenate([weight_ref[4 * step + i, :64] for i in range(4)], axis=0)
        part_ref[...] += three(left, *split(own))
        for i in range(4):
            high, low = split(weight_ref[4 * step + i, 64:])
            start = (4 * step + i) * 64
            high_ref[start : start + 64, :] = high
            low_ref[start : start + 64, :] = low


def forward_kernel(mean_ref, part_ref, high_ref, low_ref, cotangent_ref, hidden_ref, slope_ref):
    left = jnp.concatenate([mean_ref[i] for i in range(8)], axis=1)
    preact = part_ref[...] + three(left, high_ref[...], low_ref[...])
    sigma = 1.0 / (1.0 + jnp.exp(-preact))
    hidden_ref[...] = (preact * sigma).astype(BF16)
    slope = cotangent_ref[...].astype(F32) * (sigma * (1.0 + preact * (1.0 - sigma)))
    slope_ref[...] = slope.astype(BF16)


def gradient_kernel(ring_ref, self_ref, mean_ref, *rest):
    slopes, out_ref = rest[:8], rest[8]
    here = ring_ref[0]
    rows = [lax.rem(here - k + 8, 8) for k in range(8)]
    right = jnp.concatenate([ref[...] for ref in slopes], axis=0)
    for which, ref in enumerate((self_ref, mean_ref)):
        left = jnp.concatenate([ref[r] for r in rows], axis=0)
        total = 0.0
        for piece in split(left):
            total = total + lax.dot_general(
                piece, right, (((0,), (0,)), ((), ())), preferred_element_type=F32
            )
        for core in range(2):
            for chunk in range(8):
                start = core * 64 + chunk * 8
                out_ref[which * 8 + chunk, core] = total[start : start + 8]


def sum_kernel(core_ref, in_ref, keep_ref, send_ref):
    total = in_ref[0]
    for i in range(1, in_ref.shape[0]):
        total = total + in_ref[i]
    mine = core_ref[0] == 0
    keep_ref[...] = jnp.where(mine, total[0], total[1])
    send_ref[...] = jnp.where(mine, total[1], total[0])


def call(kernel, shapes, specs, scratch=(), limit=32, cost=None):
    return pl.pallas_call(
        kernel,
        out_shape=shapes,
        in_specs=specs,
        out_specs=jax.tree.map(lambda _: VMEM, shapes),
        scratch_shapes=list(scratch),
        cost_estimate=cost,
        compiler_params=pltpu.CompilerParams(vmem_limit_bytes=limit << 20),
    )


def cost(flops, size):
    return pl.CostEstimate(flops=flops, bytes_accessed=size, transcendentals=0)


def body(
    feature_table,
    seed_ids,
    neighbours,
    owners,
    blocks,
    counts,
    w_self,
    w_neigh,
    out_bias,
    cotangent,
):
    n_dom = lax.axis_size("dom")
    n_feat = lax.axis_size("feat")
    ring = n_feat // 2
    across = [(i, i ^ 1) for i in range(n_feat)]
    columns = [[2 * z + c for z in range(ring)] for c in range(2)]
    dom = lax.axis_index("dom").astype(jnp.int32).reshape(1)
    feat = lax.axis_index("feat").astype(jnp.int32).reshape(1)
    core, height = feat % 2, feat // 2
    hidden_width = w_self.shape[1]
    owner_ids = owners[:, 0]
    shape = jax.ShapeDtypeStruct

    weights = lax.all_gather(jnp.concatenate([w_self, w_neigh], axis=0), "feat", axis=0, tiled=False)

    request = jnp.concatenate([owner_ids, blocks])
    requests = lax.all_to_all(
        jnp.broadcast_to(request[None, None, :], (n_dom, 1, 2 * owner_ids.shape[0])),
        "dom", split_axis=0, concat_axis=0, tiled=True,
    ).reshape(n_dom, 2 * owner_ids.shape[0])

    packed, self_halves = call(
        prepare_kernel,
        (shape((64, HALF, BLOCK), BF16), shape((2, ring, 32, BLOCK), F32)),
        [SMEM, SMEM, VMEM],
        [pltpu.VMEM((feature_table.shape[1], BLOCK), F32)],
        cost=cost(0, 12 << 20),
    )(core, seed_ids, feature_table)

    outgoing = call(
        pack_kernel,
        shape((n_dom, SLOTS, HALF, BLOCK), BF16),
        [SMEM, VMEM, VMEM],
        [
            pltpu.VMEM((n_dom, BLOCK), jnp.int32),
            pltpu.SMEM((n_dom, BLOCK), jnp.int32),
            pltpu.SemaphoreType.DMA,
        ],
    )(dom, requests, packed)
    arrived = lax.all_to_all(
        outgoing.reshape(n_dom, SLOTS * HALF, BLOCK), "dom", split_axis=0, concat_axis=0, tiled=True
    )
    other = lax.ppermute(arrived, "feat", across)

    kept = lax.dynamic_index_in_dim(self_halves, core[0], 0, keepdims=False)
    given = lax.dynamic_index_in_dim(self_halves, 1 - core[0], 0, keepdims=False)
    self_rows = call(join_kernel, shape((ring, 64, BLOCK), F32), [SMEM, VMEM, VMEM])(
        core, kept, lax.ppermute(given, "feat", across)
    )
    self_seeds = lax.all_to_all(
        self_rows, "feat", split_axis=0, concat_axis=0, tiled=True, axis_index_groups=columns
    )
    part, high, low = call(
        self_kernel,
        (
            shape((64, hidden_width), F32),
            shape((64 * n_feat, hidden_width), BF16),
            shape((64 * n_feat, hidden_width), BF16),
        ),
        [VMEM, VMEM, VMEM],
        limit=40,
        cost=cost(3 << 27, 12 << 20),
    )(self_seeds, weights, out_bias[None, :])

    mean = call(
        gather_kernel,
        shape((ring, 64, BLOCK), F32),
        [SMEM, SMEM, SMEM, SMEM, VMEM, VMEM],
        [pltpu.VMEM((owner_ids.shape[0] * BLOCK, BLOCK), F32), pltpu.SMEM((n_dom,), jnp.int32)],
        cost=cost(0, 30 << 20),
    )(
        core,
        owner_ids,
        counts,
        jnp.transpose(neighbours).reshape(-1),
        arrived.reshape(n_dom * SLOTS, HALF, BLOCK),
        other.reshape(n_dom * SLOTS, HALF, BLOCK),
    )
    mean_seeds = lax.all_to_all(
        mean, "feat", split_axis=0, concat_axis=0, tiled=True, axis_index_groups=columns
    )

    hidden, slope = call(
        forward_kernel,
        (shape((64, hidden_width), BF16), shape((64, hidden_width), BF16)),
        [VMEM] * 5,
    )(mean_seeds, part, high, low, cotangent)

    slopes = [slope]
    for shift in range(1, ring):
        slopes.append(lax.ppermute(slope, "feat", [(i, (i + 2 * shift) % n_feat) for i in range(n_feat)]))

    partial = call(
        gradient_kernel, shape((n_dom, 2, 8, hidden_width), F32), [SMEM] + [VMEM] * 10
    )(height, self_rows, mean, *slopes)
    shares = lax.all_to_all(
        partial.reshape(n_dom, 16, hidden_width), "dom", split_axis=0, concat_axis=0, tiled=True
    )
    keep, send = call(
        sum_kernel,
        (shape((8, hidden_width), F32), shape((8, hidden_width), F32)),
        [SMEM, VMEM],
    )(core, shares.reshape(n_dom, 2, 8, hidden_width))
    total = keep + lax.ppermute(send, "feat", across)
    grads = lax.all_to_all(
        jnp.broadcast_to(total[None], (n_dom, 8, hidden_width)), "dom", split_axis=0, concat_axis=0, tiled=True
    ).reshape(n_dom * 8, hidden_width)
    return hidden, grads[: n_dom * 4], grads[n_dom * 4 :]


def solution(mesh):
    return jax.shard_map(
        body,
        mesh=mesh,
        in_specs=(
            P("feat", "dom"),
            P("dom"),
            P(None, "dom"),
            P("dom", None),
            P("dom"),
            P("dom"),
            P("feat", None),
            P("feat", None),
            P(),
            P(("dom", "feat"), None),
        ),
        out_specs=(P(("dom", "feat"), None), P("feat", None), P("feat", None)),
        check_vma=False,
    )
```

time: 397 us -> 182 us (0.46)
  waiting for transfers between devices: 254 us -> 18.8 us
  local copies, waits for them, and re-layouts: 90.3 us -> 10.6 us
  blocking collectives: 0 us -> 68.7 us
  starting transfers between devices: 11.8 us -> 41.3 us
  Pallas kernels: 0 us -> 22.9 us
  other arithmetic: 17 us -> 2.64 us
  matrix products: 8.71 us -> 0 us
    psum x1 -> x0, waiting for transfers between devices: 95.3 us -> none  [body(): grad_total = lax.psum(grad_local, 'dom')]
    gather x6 -> x0, local copies, waits for them, and re-layouts: 77.5 us -> none  [the longest x1 53.7 us: body(): frontier[neighbours.reshape(-1)].reshape(fanout, seeds_dev, cols_dev)]
    all_to_all x0 -> x3, blocking collectives: none -> 68.7 us  [the longest x1 34.9 us: body(): lax.all_to_all(outgoing.reshape(n_dom, SLOTS * HALF, BLOCK), 'dom', split...]
    reduce_scatter x1 -> x0, waiting for transfers between devices: 57.1 us -> none  [body(): lax.psum_scatter(product(stacked, weight_cat), 'feat', scatter_dimension=...]
    all_to_all x2 -> x3, waiting for transfers between devices: 58.7 us -> 2.56 us  [the longest x1 2.35 us: body(): lax.all_to_all(mean, 'feat', split_axis=0, concat_axis=0, tiled=True, axi...]
    all_gather x1, waiting for transfers between devices: 43 us -> 0.01 us  [body(): lax.all_gather(jnp.concatenate([w_self, w_neigh], axis=0), 'feat', axis=0...]
    pallas_call x0 -> x8, Pallas kernels: none -> 22.9 us  [the longest x1 10.4 us: body(): call(gather_kernel, shape((ring, 64, BLOCK), F32), [SMEM, SMEM, SMEM, SME...]
    ppermute x0 -> x10, starting transfers between devices: none -> 18.5 us  [the longest x7 17.8 us: body(): lax.ppermute(slope, 'feat', [(i, (i + 2 * shift) % n_feat) for i in range...]
  transfers between devices with their start and end apart: 5 -> 14, of which waited for: 5 -> 8; matrix products, arithmetic and copies ran while one was open for 2% -> 1% of each run, Pallas kernels for 0% -> 11%
where the time goes in v1:
time: 182 us; the launch traced here: 179 us
  blocking collectives  68.7 us (38%)
  starting transfers between devices  41.3 us (23%)
  Pallas kernels  22.9 us (13%)
  waiting for transfers between devices  18.8 us (10%)
  between operations  14.2 us (8%)
  local copies, waits for them, and re-layouts  10.6 us (6%)
  other arithmetic  2.64 us (1%)
    all_to_all x1, blocking collectives, body(): lax.all_to_all(outgoing.reshape(n_dom, SLOTS * HALF, BLOCK), 'dom', split...  34.9 us
    all_to_all x1, blocking collectives, body(): lax.all_to_all(partial.reshape(n_dom, 16, hidden_width), 'dom', split_axi...  19.1 us
    ppermute x7, starting transfers between devices, body(): lax.ppermute(slope, 'feat', [(i, (i + 2 * shift) % n_feat) for i in range...  17.8 us
    all_to_all x1, blocking collectives, body(): lax.all_to_all(jnp.broadcast_to(total[None], (n_dom, 8, hidden_width)), '...  14.8 us
    ppermute x7, waiting for transfers between devices, body(): lax.ppermute(slope, 'feat', [(i, (i + 2 * shift) % n_feat) for i in range...  11.9 us
    pallas_call x1, Pallas kernels, body(): call(gather_kernel, shape((ring, 64, BLOCK), F32), [SMEM, SMEM, SMEM, SME...  10.4 us
    unnamed x20, local copies, waits for them, and re-layouts  8.61 us
    all_to_all x1, starting transfers between devices, body(): lax.all_to_all(self_rows, 'feat', split_axis=0, concat_axis=0, tiled=True...  8.52 us
  transfers between devices with their start and end apart: 14, of which 8 were waited for; matrix products, arithmetic and copies ran while one was open for 1% of the time, Pallas kernels for 11%

profile of v1, /device:TPU:64, one launch (start us, length us, event | category | flops | bytes accessed | tf_op | source)
XLA Modules:
  0.0 179.3 jit_solution(13532910651602084225)
XLA Ops:
  7.2 1.9 %pad_maximum_fusion = f32[128,1024]{1,0:T(8,128)} fusion(f32[64,1024]{1,0:T(8,128)} %param.17, f32[64,1024]{1,0:T(8,128)} %param.16), kind=kLoop, calls=%fused_computation | loop fusion | flops 131072 | bytes 1048576 | tf_op jit(solution)/shard_map/concatenate | solution.py:240
  9.1 0.7 pad_add_fusion
  10.5 7.0 %all-to-all-start = ((s32[16,1,128]{2,1,0:T(1,128)}), s32[16,1,128]{2,1,0:T(1,128)S(1)}, u32[]{:S(2)}, u32[]{:S(2)}) async-start(s32[16,1,128]{2,1,0:T(1,128)} %broadcast_in_dim.6), calls=%async_computation | async-start | bytes 16384 | tf_op jit(solution)/shard_map/all_to_all | solution.py:243
  17.5 1.6 copy-done.3
  19.8 5.0 %shard_map.121 = (bf16[64,64,128]{2,1,0:T(8,128)(2,1)S(1)}, f32[2,8,32,128]{3,2,1,0:T(8,128)S(1)}) custom-call(s32[1]{0:T(128)} %select_n.19.core_ref, s32[1024]{0:T(1024)S(1)} %copy-done.5, f32[64,8192]{1,0:T(8,128)S(1)} %copy-done.3), custom_call_target="tpu_custom_call" | custom-call | bytes 12582912 | tf_op jit(solution)/shard_map/pallas_call | solution.py:248
  25.0 1.1 shard_map.122
  26.1 34.9 %all_to_all.30 = bf16[16,512,128]{2,1,0:T(8,128)(2,1)S(1)} all-to-all(bf16[16,512,128]{2,1,0:T(8,128)(2,1)S(1)} %bitcast.23), channel_id=1, replica_groups=mesh['dom'=16,'feat'=16] {'dom'}, dimensions={0} | all-to-all | bytes 4194304 | tf_op jit(solution)/shard_map/all_to_all | solution.py:266
  61.6 3.2 %collective-permute-done.1.other_ref = f32[8,32,128]{2,1,0:T(8,128)S(1)} collective-permute-done((f32[8,32,128]{2,1,0:T(8,128)S(1)}, f32[8,32,128]{2,1,0:T(8,128)S(1)}, u32[]{:S(2)}, u32[]{:S(2)}) %collective-permute-start.1) | collective-permute-done | bytes 131104 | tf_op jit(solution)/shard_map/ppermute | solution.py:274
  64.8 0.8 shard_map.124.self_ref
  65.6 8.5 %all-to-all-start.3 = ((f32[8,64,128]{2,1,0:T(8,128)}), f32[8,64,128]{2,1,0:T(8,128)S(1)}, u32[]{:S(2)}, u32[]{:S(2)}) async-start(f32[8,64,128]{2,1,0:T(8,128)} %shard_map.124.self_ref), calls=%async_computation.3 | async-start | bytes 524288 | tf_op jit(solution)/shard_map/all_to_all | solution.py:276
  74.7 10.4 %shard_map.123.mean_ref = f32[8,64,128]{2,1,0:T(8,128)} custom-call(s32[1]{0:T(128)} %select_n.19.core_ref, s32[64]{0:T(128)S(1)} %bitcast.29, s32[64]{0:T(128)S(1)} %copy-done.8, s32[15360]{0:T(1024)S(1)} %reshape.45.near_ref, bf16[128,64,128]{2,1,0:T(8,128)(2,1)S(1)} %bitcast.22, bf16[128,64,128]{2,1,0:T(8,128)(2,1)} %bitcast.7.other_ref), custom_call_target="tpu_custom_call" | custom-call | bytes 31457280 | tf_op jit(solution)/shard_map/pallas_call | solution.py:291
  85.1 7.2 %all-to-all-start.2 = ((f32[8,64,128]{2,1,0:T(8,128)}), f32[8,64,128]{2,1,0:T(8,128)S(1)}, u32[]{:S(2)}, u32[]{:S(2)}) async-start(f32[8,64,128]{2,1,0:T(8,128)} %shard_map.123.mean_ref), calls=%async_computation.2 | async-start | bytes 524288 | tf_op jit(solution)/shard_map/all_to_all | solution.py:305
  92.3 3.4 %copy-done = f32[2048,1024]{1,0:T(8,128)S(1)} copy-done((f32[2048,1024]{1,0:T(8,128)S(1)}, f32[2048,1024]{1,0:T(8,128)}, u32[]{:S(2)}) %copy-start) | copy-done | bytes 8388632
  95.7 1.9 %shard_map.125 = (f32[64,1024]{1,0:T(8,128)S(1)}, bf16[1024,1024]{1,0:T(8,128)(2,1)S(1)}, bf16[1024,1024]{1,0:T(8,128)(2,1)S(1)}) custom-call(f32[8,64,128]{2,1,0:T(8,128)S(1)} %all-to-all-done.3.self_ref, f32[16,128,1024]{2,1,0:T(8,128)S(1)} %bitcast.21, f32[1,1024]{1,0:T(1,128)S(1)} %bitcast.27), custom_call_target="tpu_custom_call" | custom-call | flops 402653184 | bytes 12582912 | tf_op jit(solution)/shard_map/pallas_call | solution.py:279
  97.6 1.3 copy-done.1
  98.9 2.4 %all-to-all-done.2.mean_ref = f32[8,64,128]{2,1,0:T(8,128)S(1)} async-done(((f32[8,64,128]{2,1,0:T(8,128)}), f32[8,64,128]{2,1,0:T(8,128)S(1)}, u32[]{:S(2)}, u32[]{:S(2)}) %all-to-all-start.2) | async-done | bytes 262176 | tf_op jit(solution)/shard_map/all_to_all | solution.py:305
  101.3 1.6 copy-done.2
  102.9 1.9 %shard_map.126 = (bf16[64,1024]{1,0:T(8,128)(2,1)}, bf16[64,1024]{1,0:T(8,128)(2,1)S(1)}) custom-call(f32[8,64,128]{2,1,0:T(8,128)S(1)} %all-to-all-done.2.mean_ref, f32[64,1024]{1,0:T(8,128)S(1)} %get-tuple-element.14.part_ref, bf16[1024,1024]{1,0:T(8,128)(2,1)S(1)} %get-tuple-element.15.high_ref, bf16[1024,1024]{1,0:T(8,128)(2,1)S(1)} %copy-done.2, ...), custom_call_target="tpu_custom_call" | custom-call | tf_op jit(solution)/shard_map/pallas_call | solution.py:309
  104.8 0.8 collective-permute-start.2
  105.6 1.8 collective-permute-start.3
  107.3 4.5 %collective-permute-start.4 = (bf16[64,1024]{1,0:T(8,128)(2,1)S(1)}, bf16[64,1024]{1,0:T(8,128)(2,1)S(1)}, u32[]{:S(2)}, u32[]{:S(2)}) collective-permute-start(bf16[64,1024]{1,0:T(8,128)(2,1)S(1)} %get-tuple-element.18.rest_0_), channel_id=1, source_target_pairs={{0,6},{1,7},{2,8},{3,9},{4,10},{5,11},{6,12},{7,13},{8,14},{9,15},... | collective-permute-start | bytes 393224 | tf_op jit(solution)/shard_map/ppermute | solution.py:317
  112.5 4.3 %collective-permute-start.6 = (bf16[64,1024]{1,0:T(8,128)(2,1)S(1)}, bf16[64,1024]{1,0:T(8,128)(2,1)S(1)}, u32[]{:S(2)}, u32[]{:S(2)}) collective-permute-start(bf16[64,1024]{1,0:T(8,128)(2,1)S(1)} %get-tuple-element.18.rest_0_), channel_id=1, source_target_pairs={{0,10},{1,11},{2,12},{3,13},{4,14},{5,15},{6,0},{7,1},{8,2},{9,3},... | collective-permute-start | bytes 393224 | tf_op jit(solution)/shard_map/ppermute | solution.py:317
  117.6 1.3 collective-permute-done.3.rest_2_
  118.9 5.1 %collective-permute-start.8 = (bf16[64,1024]{1,0:T(8,128)(2,1)S(1)}, bf16[64,1024]{1,0:T(8,128)(2,1)S(1)}, u32[]{:S(2)}, u32[]{:S(2)}) collective-permute-start(bf16[64,1024]{1,0:T(8,128)(2,1)S(1)} %get-tuple-element.18.rest_0_), channel_id=1, source_target_pairs={{0,14},{1,15},{2,0},{3,1},{4,2},{5,3},{6,4},{7,5},{8,6},{9,7},{10,... | collective-permute-start | bytes 393224 | tf_op jit(solution)/shard_map/ppermute | solution.py:317
  123.9 7.3 %collective-permute-done.4.rest_3_ = bf16[64,1024]{1,0:T(8,128)(2,1)S(1)} collective-permute-done((bf16[64,1024]{1,0:T(8,128)(2,1)S(1)}, bf16[64,1024]{1,0:T(8,128)(2,1)S(1)}, u32[]{:S(2)}, u32[]{:S(2)}) %collective-permute-start.4) | collective-permute-done | bytes 131104 | tf_op jit(solution)/shard_map/ppermute | solution.py:317
  131.3 2.5 %collective-permute-done.7.rest_6_ = bf16[64,1024]{1,0:T(8,128)(2,1)S(1)} collective-permute-done((bf16[64,1024]{1,0:T(8,128)(2,1)S(1)}, bf16[64,1024]{1,0:T(8,128)(2,1)S(1)}, u32[]{:S(2)}, u32[]{:S(2)}) %collective-permute-start.7) | collective-permute-done | bytes 131104 | tf_op jit(solution)/shard_map/ppermute | solution.py:317
  133.8 0.8 collective-permute-done.8.rest_7_
  134.6 1.8 shard_map.127
  136.3 19.1 %all_to_all.31 = f32[16,16,1024]{2,1,0:T(8,128)S(1)} all-to-all(f32[16,16,1024]{2,1,0:T(8,128)S(1)} %bitcast.24), channel_id=1, replica_groups=mesh['dom'=16,'feat'=16] {'dom'}, dimensions={0} | all-to-all | bytes 2097152 | tf_op jit(solution)/shard_map/all_to_all | solution.py:322
  155.6 1.2 collective-permute-done.9
  156.8 14.8 %all_to_all.32 = f32[16,8,1024]{2,1,0:T(8,128)S(1)} all-to-all(f32[16,8,1024]{2,1,0:T(8,128)S(1)} %broadcast_in_dim.8), channel_id=1, replica_groups=mesh['dom'=16,'feat'=16] {'dom'}, dimensions={0} | all-to-all | bytes 1048576 | tf_op jit(solution)/shard_map/all_to_all | solution.py:331
  171.6 0.8 slice_bitcast_fusion
  (37 shorter events, 4.4 us)
Async XLA Ops:
  7.2 85.1 %all-gather.3.cloned.1.call-start = ((), (), s32[]{:S(2)}) async-start(), calls=%async_computation.6 | async-start | bytes 8912896 | tf_op jit(solution)/shard_map/all_gather | solution.py:240
  10.5 14.5 %all-to-all-start = ((s32[16,1,128]{2,1,0:T(1,128)}), s32[16,1,128]{2,1,0:T(1,128)S(1)}, u32[]{:S(2)}, u32[]{:S(2)}) async-start(s32[16,1,128]{2,1,0:T(1,128)} %broadcast_in_dim.6), calls=%async_computation | async-start | bytes 16384 | tf_op jit(solution)/shard_map/all_to_all | solution.py:243
  17.5 1.6 copy-start.3
  19.1 0.7 copy-start.5
  26.1 48.0 %copy-start.9 = (s32[15,1024]{1,0:T(8,128)S(1)}, s32[15,1024]{1,0:T(8,128)}, u32[]{:S(2)}) copy-start(s32[15,1024]{1,0:T(8,128)} %param.12) | copy-start | bytes 184324
  61.0 13.7 %copy-start.7 = (s32[64,1]{0,1:T(1,128)S(1)}, s32[64,1]{0,1:T(1,128)}, u32[]{:S(2)}) copy-start(s32[64,1]{0,1:T(1,128)} %param.13) | copy-start | bytes 772
  61.0 13.7 %copy-start.8 = (s32[64]{0:T(128)S(1)}, s32[64]{0:T(128)}, u32[]{:S(2)}) copy-start(s32[64]{0:T(128)} %count_ref.1) | copy-start | bytes 772
  61.0 13.7 %collective-permute-start = (bf16[16,512,128]{2,1,0:T(8,128)(2,1)S(1)}, bf16[16,512,128]{2,1,0:T(8,128)(2,1)}, u32[]{:S(2)}, u32[]{:S(2)}) collective-permute-start(bf16[16,512,128]{2,1,0:T(8,128)(2,1)S(1)} %all_to_all.30), channel_id=1, source_target_pairs={{0,1},{1,0},{2,3},{3,2},{4,5},{5,4},{6,7},{7,6},{8,9},{9,8},{10,11... | collective-permute-start | bytes 6291464 | tf_op jit(solution)/shard_map/ppermute | solution.py:269
  61.0 3.7 %collective-permute-start.1 = (f32[8,32,128]{2,1,0:T(8,128)S(1)}, f32[8,32,128]{2,1,0:T(8,128)S(1)}, u32[]{:S(2)}, u32[]{:S(2)}) collective-permute-start(f32[8,32,128]{2,1,0:T(8,128)S(1)} %get-tuple-element.23), channel_id=1, source_target_pairs={{0,1},{1,0},{2,3},{3,2},{4,5},{5,4},{6,7},{7,6},{8,9},{9,8},{10,11... | collective-permute-start | bytes 393224 | tf_op jit(solution)/shard_map/ppermute | solution.py:274
  65.6 19.5 %all-to-all-start.3 = ((f32[8,64,128]{2,1,0:T(8,128)}), f32[8,64,128]{2,1,0:T(8,128)S(1)}, u32[]{:S(2)}, u32[]{:S(2)}) async-start(f32[8,64,128]{2,1,0:T(8,128)} %shard_map.124.self_ref), calls=%async_computation.3 | async-start | bytes 524288 | tf_op jit(solution)/shard_map/all_to_all | solution.py:276
  74.7 17.6 %copy-start.6 = (f32[1024]{0:T(1024)S(1)}, f32[1024]{0:T(1024)}, u32[]{:S(2)}) copy-start(f32[1024]{0:T(1024)} %param.18) | copy-start | bytes 12292
  85.1 16.2 %all-to-all-start.2 = ((f32[8,64,128]{2,1,0:T(8,128)}), f32[8,64,128]{2,1,0:T(8,128)S(1)}, u32[]{:S(2)}, u32[]{:S(2)}) async-start(f32[8,64,128]{2,1,0:T(8,128)} %shard_map.123.mean_ref), calls=%async_computation.2 | async-start | bytes 524288 | tf_op jit(solution)/shard_map/all_to_all | solution.py:305
  92.3 3.4 %copy-start = (f32[2048,1024]{1,0:T(8,128)S(1)}, f32[2048,1024]{1,0:T(8,128)}, u32[]{:S(2)}) copy-start(f32[2048,1024]{1,0:T(8,128)} %all-gather.3.cloned.1.call-done) | copy-start | bytes 25165828
  95.7 5.6 %copy-start.4 = (bf16[64,1024]{1,0:T(8,128)(2,1)S(1)}, bf16[64,1024]{1,0:T(8,128)(2,1)}, u32[]{:S(2)}) copy-start(bf16[64,1024]{1,0:T(8,128)(2,1)} %cotangent_ref.1) | copy-start | bytes 393220
  97.6 1.4 copy-start.1
  101.3 1.6 copy-start.2
  104.8 12.0 %collective-permute-start.2 = (bf16[64,1024]{1,0:T(8,128)(2,1)S(1)}, bf16[64,1024]{1,0:T(8,128)(2,1)S(1)}, u32[]{:S(2)}, u32[]{:S(2)}) collective-permute-start(bf16[64,1024]{1,0:T(8,128)(2,1)S(1)} %get-tuple-element.18.rest_0_), channel_id=1, source_target_pairs={{0,2},{1,3},{2,4},{3,5},{4,6},{5,7},{6,8},{7,9},{8,10},{9,11},{10,... | collective-permute-start | bytes 393224 | tf_op jit(solution)/shard_map/ppermute | solution.py:317
  105.6 13.3 %collective-permute-start.3 = (bf16[64,1024]{1,0:T(8,128)(2,1)S(1)}, bf16[64,1024]{1,0:T(8,128)(2,1)S(1)}, u32[]{:S(2)}, u32[]{:S(2)}) collective-permute-start(bf16[64,1024]{1,0:T(8,128)(2,1)S(1)} %get-tuple-element.18.rest_0_), channel_id=1, source_target_pairs={{0,4},{1,5},{2,6},{3,7},{4,8},{5,9},{6,10},{7,11},{8,12},{9,13},{1... | collective-permute-start | bytes 393224 | tf_op jit(solution)/shard_map/ppermute | solution.py:317
  107.3 23.9 %collective-permute-start.4 = (bf16[64,1024]{1,0:T(8,128)(2,1)S(1)}, bf16[64,1024]{1,0:T(8,128)(2,1)S(1)}, u32[]{:S(2)}, u32[]{:S(2)}) collective-permute-start(bf16[64,1024]{1,0:T(8,128)(2,1)S(1)} %get-tuple-element.18.rest_0_), channel_id=1, source_target_pairs={{0,6},{1,7},{2,8},{3,9},{4,10},{5,11},{6,12},{7,13},{8,14},{9,15},... | collective-permute-start | bytes 393224 | tf_op jit(solution)/shard_map/ppermute | solution.py:317
  111.8 19.5 %collective-permute-start.5 = (bf16[64,1024]{1,0:T(8,128)(2,1)S(1)}, bf16[64,1024]{1,0:T(8,128)(2,1)S(1)}, u32[]{:S(2)}, u32[]{:S(2)}) collective-permute-start(bf16[64,1024]{1,0:T(8,128)(2,1)S(1)} %get-tuple-element.18.rest_0_), channel_id=1, source_target_pairs={{0,8},{1,9},{2,10},{3,11},{4,12},{5,13},{6,14},{7,15},{8,0},{9,1},... | collective-permute-start | bytes 393224 | tf_op jit(solution)/shard_map/ppermute | solution.py:317
  112.5 18.7 %collective-permute-start.6 = (bf16[64,1024]{1,0:T(8,128)(2,1)S(1)}, bf16[64,1024]{1,0:T(8,128)(2,1)S(1)}, u32[]{:S(2)}, u32[]{:S(2)}) collective-permute-start(bf16[64,1024]{1,0:T(8,128)(2,1)S(1)} %get-tuple-element.18.rest_0_), channel_id=1, source_target_pairs={{0,10},{1,11},{2,12},{3,13},{4,14},{5,15},{6,0},{7,1},{8,2},{9,3},... | collective-permute-start | bytes 393224 | tf_op jit(solution)/shard_map/ppermute | solution.py:317
  116.8 16.9 %collective-permute-start.7 = (bf16[64,1024]{1,0:T(8,128)(2,1)S(1)}, bf16[64,1024]{1,0:T(8,128)(2,1)S(1)}, u32[]{:S(2)}, u32[]{:S(2)}) collective-permute-start(bf16[64,1024]{1,0:T(8,128)(2,1)S(1)} %get-tuple-element.18.rest_0_), channel_id=1, source_target_pairs={{0,12},{1,13},{2,14},{3,15},{4,0},{5,1},{6,2},{7,3},{8,4},{9,5},{1... | collective-permute-start | bytes 393224 | tf_op jit(solution)/shard_map/ppermute | solution.py:317
  118.9 15.7 %collective-permute-start.8 = (bf16[64,1024]{1,0:T(8,128)(2,1)S(1)}, bf16[64,1024]{1,0:T(8,128)(2,1)S(1)}, u32[]{:S(2)}, u32[]{:S(2)}) collective-permute-start(bf16[64,1024]{1,0:T(8,128)(2,1)S(1)} %get-tuple-element.18.rest_0_), channel_id=1, source_target_pairs={{0,14},{1,15},{2,0},{3,1},{4,2},{5,3},{6,4},{7,5},{8,6},{9,7},{10,... | collective-permute-start | bytes 393224 | tf_op jit(solution)/shard_map/ppermute | solution.py:317
  155.5 1.3 collective-permute-start.9
Sparse Core Ops, SparseCore 0:
  9.8 56.3 all-gather.2

commit v2 on v1

v2 whole, which is shorter than its diff:
```python
import jax
import jax.numpy as jnp
from jax import lax
from jax.experimental import pallas as pl
from jax.experimental.pallas import tpu as pltpu
from jax.sharding import PartitionSpec as P

FAN = 15
BLOCK = 128
SLOTS = 8
HALF = BLOCK // 2
DISTANCES = (0, 1, -1, 2, -2, 3, -3, 4)
F32 = jnp.float32
BF16 = jnp.bfloat16
SMEM = pl.BlockSpec(memory_space=pltpu.SMEM)
VMEM = pl.BlockSpec(memory_space=pltpu.VMEM)
ANY = pl.BlockSpec(memory_space=pl.ANY)


def lane_of(shape):
    return lax.broadcasted_iota(jnp.int32, shape, len(shape) - 1)


def split(value):
    high = value.astype(BF16)
    low = (value - high.astype(F32)).astype(BF16)
    return high, low


def dot(left, right):
    return jnp.dot(left, right, preferred_element_type=F32)


def prepare_kernel(
    core_ref, seed_hbm, table_hbm, packed_ref, keep_ref, send_ref,
    rows, table, seed_ref, packed, sems, seed_sem, out_sems,
):
    core = core_ref[0]
    parts = sems.shape[0]
    width = table.shape[1] // parts
    pairs = width // (2 * BLOCK)
    first = lane_of((HALF, BLOCK)) < HALF

    def fetch(part):
        window = pl.ds(part * width, width)
        return pltpu.make_async_copy(table_hbm.at[:, window], table.at[:, window], sems.at[part])

    seeds = pltpu.make_async_copy(seed_hbm, seed_ref, seed_sem)
    seeds.start()
    for part in range(parts):
        fetch(part).start()

    def turn(pair, carry):
        start = pl.multiple_of(pair * 2 * BLOCK, 2 * BLOCK)
        left = table[:, pl.ds(start, BLOCK)]
        right = table[:, pl.ds(start + BLOCK, BLOCK)]
        turned = jnp.concatenate([left, right], axis=0).T
        rows[pl.ds(start, BLOCK), :] = turned
        rows[pl.ds(start + BLOCK, BLOCK), :] = pltpu.roll(turned, HALF, 1)
        for which in range(2):
            near = pl.multiple_of(start + which * BLOCK + core * HALF, HALF)
            far = pl.multiple_of(start + (1 - which) * BLOCK + (1 - core) * HALF, HALF)
            both_halves = jnp.where(first, rows[pl.ds(near, HALF), :], rows[pl.ds(far, HALF), :])
            packed[2 * pair + which] = both_halves.astype(BF16)
        return carry

    outs = []
    for part in range(parts):
        fetch(part).wait()
        lax.fori_loop(part * pairs, (part + 1) * pairs, turn, 0, unroll=2)
        window = pl.ds(2 * pairs * part, 2 * pairs)
        outs.append(pltpu.make_async_copy(packed.at[window], packed_ref.at[window], out_sems.at[part]))
        outs[-1].start()
    lane = lane_of((1, BLOCK)) < HALF
    seeds.wait()

    def pick(chip, carry):
        for mine, ref in ((True, keep_ref), (False, send_ref)):
            group = 2 * chip + (core if mine else 1 - core)
            for step in range(32):
                lead = seed_ref[group * 64 + step + 32 * core]
                trail = seed_ref[group * 64 + step + 32 * (1 - core)]
                low = rows[pl.ds(lead, 1), :]
                high = rows[pl.ds(lax.bitwise_xor(trail, BLOCK), 1), :]
                ref[chip, pl.ds(step, 1), :] = jnp.where(lane, low, high)
        return carry

    lax.fori_loop(0, keep_ref.shape[0], pick, 0)
    for copy in outs:
        copy.wait()


def pack_kernel(me_ref, request_ref, packed_hbm, out_hbm, wanted, wanted_smem, packed_ref, out_ref, sem, in_sem, out_sems):
    fetch = pltpu.make_async_copy(packed_hbm, packed_ref, in_sem)
    fetch.start()
    me = me_ref[0]
    request = request_ref[...]
    parts = request.shape[0]
    lane = lane_of(request.shape)
    mine = jnp.logical_and(request == me, lane < HALF)
    below = lax.broadcasted_iota(jnp.int32, (BLOCK, BLOCK), 0) <= lane_of((BLOCK, BLOCK))
    rank = dot(mine.astype(BF16), below.astype(BF16))
    block = pltpu.roll(request, HALF, 1).astype(F32)
    result = jnp.zeros(request.shape, F32)
    for slot in range(SLOTS):
        hit = jnp.logical_and(mine, rank == slot + 1.0)
        chosen = jnp.sum(jnp.where(hit, block, 0.0), axis=1, keepdims=True)
        result = jnp.where(lane == slot, chosen, result)
    wanted[...] = result.astype(jnp.int32)
    copy = pltpu.make_async_copy(wanted, wanted_smem, sem)
    copy.start()
    copy.wait()

    fetch.wait()
    copies = []
    for part in range(parts):
        for slot in range(SLOTS):
            out_ref[part, slot] = packed_ref[wanted_smem[part, slot]]
        copies.append(pltpu.make_async_copy(out_ref.at[part], out_hbm.at[part], out_sems.at[part]))
        copies[-1].start()
    for copy in copies:
        copy.wait()


def collect_kernel(owner_ref, arrived_ref, *rest):
    out_ref, seen = rest[-2:]
    for owner in range(arrived_ref.shape[0] // SLOTS):
        seen[owner] = 0

    def place(entry, carry):
        owner = owner_ref[entry]
        rank = seen[owner]
        seen[owner] = rank + 1
        out_ref[entry] = arrived_ref[owner * SLOTS + rank]
        return carry

    lax.fori_loop(0, out_ref.shape[0], place, 0, unroll=4)


def gather_kernel(core_ref, count_ref, near_ref, own_ref, other_ref, out_ref, front):
    core = core_ref[0]
    lane = lane_of((HALF, BLOCK))
    row = lax.broadcasted_iota(jnp.int32, (HALF, BLOCK), 0)
    straight = (lane < HALF) == (core == 0)

    def place(entry, carry):
        own = own_ref[entry].astype(F32)
        other = other_ref[entry].astype(F32)
        count = count_ref[entry]
        upper = jnp.where(straight, own, other)
        lower = pltpu.roll(jnp.where(straight, other, own), HALF, 1)
        start = pl.multiple_of(entry * BLOCK, BLOCK)
        front[pl.ds(start, HALF), :] = jnp.where(row < count, upper, 0.0)
        front[pl.ds(start + HALF, HALF), :] = jnp.where(row < count - HALF, lower, 0.0)
        return carry

    lax.fori_loop(0, own_ref.shape[0], place, 0, unroll=4)

    def average(step, carry):
        group, part = lax.div(step, 4), lax.rem(step, 4)
        base = ((2 * group + core) * 64 + part * 16) * FAN
        for seed in range(16):
            terms = [front[pl.ds(near_ref[base + seed * FAN + k], 1), :] for k in range(FAN)]
            while len(terms) > 1:
                terms = [
                    terms[i] + terms[i + 1] if i + 1 < len(terms) else terms[i]
                    for i in range(0, len(terms), 2)
                ]
            out_ref[group, pl.ds(part * 16 + seed, 1), :] = terms[0] * (1.0 / FAN)
        return carry

    lax.fori_loop(0, 32, average, 0)


def join_kernel(place_ref, own_ref, other_ref, *rest):
    out_ref, sends = rest[0], rest[1:]
    straight = (lane_of((32, BLOCK)) < HALF) == (place_ref[0] == 0)
    ring = own_ref.shape[0]
    for shift in range(ring):
        group = lax.rem(place_ref[1] + shift, ring)
        own, other = own_ref[group], other_ref[group]
        upper = jnp.where(straight, own, other)
        lower = pltpu.roll(jnp.where(straight, other, own), HALF, 1)
        out_ref[group, :32] = upper
        out_ref[group, 32:] = lower
        target = sends[shift]
        target[:32] = upper
        target[32:] = lower


def weight_kernel(self_hbm, neigh_hbm, out_ref, both, sems):
    copies = [
        pltpu.make_async_copy(ref, both.at[which], sems.at[which])
        for which, ref in enumerate((self_hbm, neigh_hbm))
    ]
    for copy in copies:
        copy.start()
    copies[0].wait()
    high, low = split(both[0])
    out_ref[0] = high
    out_ref[1] = low
    copies[1].wait()
    out_ref[2] = both[1].astype(BF16)


def three(left, right_high, right_low):
    high, low = split(left)
    return dot(high, right_high) + (dot(high, right_low) + dot(low, right_high))


def self_kernel(place_ref, bias_ref, weight_hbm, *rest):
    pieces = rest[:8]
    part_ref, neigh_ref, held, rows, sems, row_sems = rest[8:]
    row_copies = [
        pltpu.make_async_copy(piece, rows.at[index], row_sems.at[index]) for index, piece in enumerate(pieces)
    ]
    for copy in row_copies:
        copy.start()
    chips = [lax.rem(place_ref[1] + 8 - distance, 8) for distance in DISTANCES]
    copies = []
    for index, chip in enumerate(chips):
        pair = weight_hbm.at[pl.ds(2 * chip, 2), pl.ds(0, 2)]
        copies.append(pltpu.make_async_copy(pair, held.at[index], sems.at[index]))
        copies[-1].start()
    neigh_copies = []
    for core in range(16):
        target = neigh_ref.at[core]
        neigh_copies.append(pltpu.make_async_copy(weight_hbm.at[core, 2], target, sems.at[8 + core]))
        neigh_copies[-1].start()
    part_ref[...] = jnp.broadcast_to(bias_ref[...], part_ref.shape)
    for step in range(4):
        pair = (2 * step, 2 * step + 1)
        for index in pair:
            copies[index].wait()
            row_copies[index].wait()
        left = jnp.concatenate([rows[index] for index in pair], axis=1)
        high, low = [
            jnp.concatenate([held[index, core, which] for index in pair for core in range(2)], axis=0)
            for which in range(2)
        ]
        part_ref[...] += three(left, high, low)
    for copy in neigh_copies:
        copy.wait()


def forward_kernel(mean_ref, part_ref, weight_ref, cotangent_ref, hidden_ref, slope_ref):
    preact = part_ref[...]
    left = jnp.concatenate([mean_ref[chip] for chip in range(8)], axis=1)
    right = weight_ref[...]
    for piece in split(left):
        preact += dot(piece, right)
    sigma = 1.0 / (1.0 + jnp.exp(-preact))
    hidden_ref[...] = (preact * sigma).astype(BF16)
    slope = cotangent_ref[...].astype(F32) * (sigma * (1.0 + preact * (1.0 - sigma)))
    slope_ref[...] = slope.astype(BF16)


def gradient_kernel(place_ref, self_ref, mean_ref, near_ref, *rest):
    slopes, (keep_ref, send_ref) = rest[:-2], rest[-2:]
    here = place_ref[1]
    rows = [lax.rem(here - k + 8, 8) for k in DISTANCES]
    right = jnp.concatenate([near_ref[...]] + [ref[...] for ref in slopes], axis=0)
    first = place_ref[0] == 0
    for which, ref in enumerate((self_ref, mean_ref)):
        left = jnp.concatenate([ref[r] for r in rows], axis=0)
        total = 0.0
        for piece in split(left):
            total = total + lax.dot_general(
                piece, right, (((0,), (0,)), ((), ())), preferred_element_type=F32
            )
        for chunk in range(8):
            start = chunk * 8
            one, two = total[start : start + 8], total[64 + start : 64 + start + 8]
            keep_ref[which * 8 + chunk] = jnp.where(first, one, two)
            send_ref[which * 8 + chunk] = jnp.where(first, two, one)


def add_kernel(left_ref, right_ref, out_ref):
    out_ref[...] = left_ref[...] + right_ref[...]


def sum_kernel(in_ref, out_ref):
    total = in_ref[0]
    for i in range(1, in_ref.shape[0]):
        total = total + in_ref[i]
    for i in range(out_ref.shape[0]):
        out_ref[i] = total


def call(kernel, shapes, specs, scratch=(), limit=8, cost=None, outs=None, aliases={}):
    return pl.pallas_call(
        kernel,
        out_shape=shapes,
        in_specs=specs,
        out_specs=outs or jax.tree.map(lambda _: VMEM, shapes),
        input_output_aliases=aliases,
        scratch_shapes=list(scratch),
        cost_estimate=cost,
        compiler_params=pltpu.CompilerParams(vmem_limit_bytes=limit << 20),
    )


def cost(flops, size):
    return pl.CostEstimate(flops=flops, bytes_accessed=size, transcendentals=0)


def body(
    feature_table,
    seed_ids,
    neighbours,
    owners,
    blocks,
    counts,
    w_self,
    w_neigh,
    out_bias,
    cotangent,
):
    n_dom = lax.axis_size("dom")
    n_feat = lax.axis_size("feat")
    ring = n_feat // 2
    across = [(i, i ^ 1) for i in range(n_feat)]
    columns = [[2 * z + c for z in range(ring)] for c in range(2)]
    dom = lax.axis_index("dom").astype(jnp.int32).reshape(1)
    feat = lax.axis_index("feat").astype(jnp.int32).reshape(1)
    core = feat % 2
    place = jnp.concatenate([core, feat // 2])
    hidden_width = w_self.shape[1]

    def climb(value, chips):
        pairs = [(i, (i + 2 * chips) % n_feat) for i in range(n_feat)]
        return lax.ppermute(value, "feat", pairs)

    owner_ids = owners[:, 0]
    shape = jax.ShapeDtypeStruct

    request = jnp.concatenate([owner_ids, blocks])
    requests = lax.all_to_all(
        jnp.broadcast_to(request[None, None, :], (n_dom, 1, 2 * owner_ids.shape[0])),
        "dom", split_axis=0, concat_axis=0, tiled=True,
    ).reshape(n_dom, 2 * owner_ids.shape[0])
    near = jnp.transpose(neighbours).reshape(-1)
    weights = lax.all_gather(
        call(
            weight_kernel, shape((3, 64, hidden_width), BF16), [ANY, ANY],
            [pltpu.VMEM((2, 64, hidden_width), F32), pltpu.SemaphoreType.DMA((2,))], limit=60,
        )(w_self, w_neigh),
        "feat", axis=0, tiled=False,
    )

    packed, kept, given = call(
        prepare_kernel,
        (
            shape((feature_table.shape[1] // BLOCK, HALF, BLOCK), BF16),
            shape((ring, 32, BLOCK), F32),
            shape((ring, 32, BLOCK), F32),
        ),
        [SMEM, ANY, ANY],
        [
            pltpu.VMEM((feature_table.shape[1], BLOCK), F32),
            pltpu.VMEM(feature_table.shape, F32),
            pltpu.SMEM(seed_ids.shape, jnp.int32),
            pltpu.VMEM((feature_table.shape[1] // BLOCK, HALF, BLOCK), BF16),
            pltpu.SemaphoreType.DMA((4,)),
            pltpu.SemaphoreType.DMA,
            pltpu.SemaphoreType.DMA((4,)),
        ],
        limit=60, cost=cost(0, 10 << 20), outs=(ANY, VMEM, VMEM),
    )(core, seed_ids, feature_table)

    outgoing = call(
        pack_kernel,
        shape((n_dom, SLOTS, HALF, BLOCK), BF16),
        [SMEM, VMEM, ANY],
        [
            pltpu.VMEM((n_dom, BLOCK), jnp.int32),
            pltpu.SMEM((n_dom, BLOCK), jnp.int32),
            pltpu.VMEM(packed.shape, BF16),
            pltpu.VMEM((n_dom, SLOTS, HALF, BLOCK), BF16),
            pltpu.SemaphoreType.DMA,
            pltpu.SemaphoreType.DMA,
            pltpu.SemaphoreType.DMA((n_dom,)),
        ],
        limit=60, outs=ANY,
    )(dom, requests, packed)
    arrived = lax.all_to_all(
        outgoing.reshape(n_dom, SLOTS * HALF, BLOCK), "dom", split_axis=0, concat_axis=0, tiled=True
    )
    self_rows, *sends = call(
        join_kernel,
        (shape((ring, 64, BLOCK), F32),) + (shape((64, BLOCK), F32),) * ring,
        [SMEM, VMEM, VMEM],
        limit=60, cost=cost(0, 1 << 20),
    )(place, kept, lax.ppermute(given, "feat", across))
    moved = [climb(sends[k % ring], k) for k in DISTANCES[1:]]
    pieces = [sends[0]] + moved

    entries = call(
        collect_kernel, shape((owner_ids.shape[0], HALF, BLOCK), BF16),
        [SMEM, VMEM] + [ANY] * 8, [pltpu.SMEM((n_dom,), jnp.int32)], limit=2, cost=cost(0, 2 << 20),
    )(owner_ids, arrived.reshape(n_dom * SLOTS, HALF, BLOCK), *moved, near)
    mean = call(
        gather_kernel,
        shape((ring, 64, BLOCK), F32),
        [SMEM, SMEM, SMEM, VMEM, VMEM],
        [pltpu.VMEM((owner_ids.shape[0] * BLOCK, BLOCK), F32)],
        cost=cost(0, 30 << 20),
    )(core, counts, near, entries, lax.ppermute(entries, "feat", across))

    part, neigh_weight = call(
        self_kernel,
        (shape((64, hidden_width), F32), shape((n_feat, 64, hidden_width), BF16)),
        [SMEM, VMEM] + [ANY] * 9,
        [
            pltpu.VMEM((ring, 2, 2, 64, hidden_width), BF16),
            pltpu.VMEM((ring, 64, BLOCK), F32),
            pltpu.SemaphoreType.DMA((24,)),
            pltpu.SemaphoreType.DMA((ring,)),
        ],
        limit=56, cost=cost(3 << 27, 9 << 20),
    )(place, out_bias[None, :], weights, *pieces)
    mean_seeds = lax.all_to_all(
        mean, "feat", split_axis=0, concat_axis=0, tiled=True, axis_index_groups=columns
    )

    hidden, slope = call(
        forward_kernel,
        (shape((64, hidden_width), BF16), shape((64, hidden_width), BF16)),
        [VMEM] * 4, limit=8, cost=cost(2 << 27, 4 << 20),
    )(mean_seeds, part, neigh_weight.reshape(-1, hidden_width), cotangent)

    up, down = climb(slope, 1), climb(slope, -1)
    up_two, down_two = climb(slope, 2), climb(slope, -2)
    up_three, down_three = climb(up_two, 1), climb(down_two, -1)
    up_four, down_four = climb(up_two[:32], 2), climb(down_two[32:], -2)
    slopes = [up, down, up_two, down_two, up_three, down_three, up_four, down_four]

    keep, send = call(
        gradient_kernel, (shape((n_dom, 8, hidden_width), F32),) * 2, [SMEM] + [VMEM] * 11, limit=16
    )(place, self_rows, mean, slope, *slopes)
    partial = call(add_kernel, shape(keep.shape, F32), [VMEM, VMEM], limit=4)(
        keep, lax.ppermute(send, "feat", across)
    )
    shares = lax.all_to_all(partial, "dom", split_axis=0, concat_axis=0, tiled=True)
    total = call(sum_kernel, shape(shares.shape, F32), [VMEM], limit=4)(shares)
    grads = lax.all_to_all(
        total, "dom", split_axis=0, concat_axis=0, tiled=True
    ).reshape(n_dom * 8, hidden_width)
    return hidden, grads[: n_dom * 4], grads[n_dom * 4 :]


def solution(mesh):
    return jax.shard_map(
        body,
        mesh=mesh,
        in_specs=(
            P("feat", "dom"),
            P("dom"),
            P(None, "dom"),
            P("dom", None),
            P("dom"),
            P("dom"),
            P("feat", None),
            P("feat", None),
            P(),
            P(("dom", "feat"), None),
        ),
        out_specs=(P(("dom", "feat"), None), P("feat", None), P("feat", None)),
        check_vma=False,
    )
```

time: 182 us -> 163 us (0.90); the launches traced: 179 us -> 162 us
  blocking collectives: 68.7 us -> 28.7 us
  Pallas kernels: 22.9 us -> 34.1 us
  waiting for transfers between devices: 18.8 us -> 27.9 us
  starting transfers between devices: 41.3 us -> 50.2 us
  local copies, waits for them, and re-layouts: 10.6 us -> 5.84 us
    all_to_all x3 -> x2, blocking collectives: 68.7 us -> 28.7 us  [the longest x1 14.7 us: body(): lax.all_to_all(partial, 'dom', split_axis=0, concat_axis=0, tiled=True)]
    ppermute x9 -> x17, starting transfers between devices: 17.9 us -> 28.8 us  [the longest x15 28.6 us: climb(): return lax.ppermute(value, 'feat', pairs)]
    pallas_call x6 -> x9, Pallas kernels: 19.9 us -> 29.1 us  [the longest x1 10.3 us: body(): call(gather_kernel, shape((ring, 64, BLOCK), F32), [SMEM, SMEM, SMEM, VME...]
    ppermute x9 -> x17, waiting for transfers between devices: 13.1 us -> 18.5 us  [the longest x15 13.9 us: climb(): return lax.ppermute(value, 'feat', pairs)]
    unnamed x20 -> x36, local copies, waits for them, and re-layouts: 8.61 us -> 3.86 us
    all_to_all x1, waiting for transfers between devices: 0.01 us -> 4.55 us  [body(): lax.all_to_all(outgoing.reshape(n_dom, SLOTS * HALF, BLOCK), 'dom', split...]
    all_to_all x1, starting transfers between devices: 8.52 us -> 6.04 us  [body(): lax.all_to_all(outgoing.reshape(n_dom, SLOTS * HALF, BLOCK), 'dom', split...]
    ppermute x1, waiting for transfers between devices: 3.15 us -> 0.68 us  [body(): lax.ppermute(given, 'feat', across)]
  transfers between devices with their start and end apart: 14 -> 22, of which waited for: 8 -> 12; matrix products, arithmetic and copies ran while one was open for 1% -> 2% of each run, Pallas kernels for 11% -> 18%
where the time goes in v2:
time: 163 us; the launch traced here: 162 us
  starting transfers between devices  50.2 us (31%)
  Pallas kernels  34.1 us (21%)
  blocking collectives  28.7 us (18%)
  waiting for transfers between devices  27.9 us (17%)
  between operations  14.3 us (9%)
  local copies, waits for them, and re-layouts  5.84 us (4%)
    ppermute x15, starting transfers between devices, climb(): return lax.ppermute(value, 'feat', pairs)  28.6 us
    all_to_all x1, blocking collectives, body(): lax.all_to_all(partial, 'dom', split_axis=0, concat_axis=0, tiled=True)  14.7 us
    all_to_all x1, blocking collectives, body(): lax.all_to_all(total, 'dom', split_axis=0, concat_axis=0, tiled=True)  14 us
    ppermute x15, waiting for transfers between devices, climb(): return lax.ppermute(value, 'feat', pairs)  13.9 us
    pallas_call x1, Pallas kernels, body(): call(gather_kernel, shape((ring, 64, BLOCK), F32), [SMEM, SMEM, SMEM, VME...  10.3 us
    all_to_all x1, starting transfers between devices, body(): lax.all_to_all(mean, 'feat', split_axis=0, concat_axis=0, tiled=True, axi...  8.15 us
    all_to_all x1, starting transfers between devices, body(): lax.all_to_all(jnp.broadcast_to(request[None, None, :], (n_dom, 1, 2 * ow...  7.03 us
    pallas_call x1, Pallas kernels, body(): call(self_kernel, (shape((64, hidden_width), F32), shape((n_feat, 64, hid...  6.23 us
  transfers between devices with their start and end apart: 22, of which 12 were waited for; matrix products, arithmetic and copies ran while one was open for 2% of the time, Pallas kernels for 18%

profile of v2, /device:TPU:64, one launch (start us, length us, event | category | flops | bytes accessed | tf_op | source)
XLA Modules:
  0.0 162.5 jit_solution(330865787462148222)
XLA Ops:
  7.2 1.8 %shard_map.126 = bf16[3,64,1024]{2,1,0:T(8,128)(2,1)} custom-call(f32[64,1024]{1,0:T(8,128)} %self_hbm.1, f32[64,1024]{1,0:T(8,128)} %neigh_hbm.1), custom_call_target="tpu_custom_call" | custom-call | tf_op jit(solution)/shard_map/pallas_call | solution.py:344
  10.4 7.0 %all-to-all-start = ((s32[16,1,128]{2,1,0:T(1,128)}), s32[16,1,128]{2,1,0:T(1,128)S(1)}, u32[]{:S(2)}, u32[]{:S(2)}) async-start(s32[16,1,128]{2,1,0:T(1,128)} %broadcast_in_dim.4), calls=%async_computation | async-start | bytes 16384 | tf_op jit(solution)/shard_map/all_to_all | solution.py:338
  17.5 6.1 %shard_map.121 = (bf16[64,64,128]{2,1,0:T(8,128)(2,1)}, f32[8,32,128]{2,1,0:T(8,128)}, f32[8,32,128]{2,1,0:T(8,128)}) custom-call(s32[1]{0:T(128)S(6)} %select_n.12.core_ref, s32[1024]{0:T(1024)} %seed_hbm.1, f32[64,8192]{1,0:T(8,128)} %table_hbm.1), custom_call_target="tpu_custom_call" | custom-call | bytes 10485760 | tf_op jit(solution)/shard_map/pallas_call | solution.py:351
  25.5 3.5 %shard_map.122 = bf16[16,8,64,128]{3,2,1,0:T(8,128)(2,1)} custom-call(s32[1]{0:T(128)} %bitcast.3.me_ref, s32[16,128]{1,0:T(8,128)} %bitcast.21, bf16[64,64,128]{2,1,0:T(8,128)(2,1)} %get-tuple-element.21.packed_hbm), custom_call_target="tpu_custom_call" | custom-call | tf_op jit(solution)/shard_map/pallas_call | solution.py:371
  29.1 6.0 %all-to-all-start.1 = ((bf16[16,512,128]{2,1,0:T(8,128)(2,1)}), bf16[16,512,128]{2,1,0:T(8,128)(2,1)S(1)}, u32[]{:S(2)}, u32[]{:S(2)}) async-start(bf16[16,512,128]{2,1,0:T(8,128)(2,1)} %bitcast.18), calls=%async_computation.1 | async-start | bytes 4194304 | tf_op jit(solution)/shard_map/all_to_all | solution.py:386
  37.2 1.8 %shard_map.123 = (f32[8,64,128]{2,1,0:T(8,128)}, f32[64,128]{1,0:T(8,128)}, f32[64,128]{1,0:T(8,128)}, f32[64,128]{1,0:T(8,128)}, f32[64,128]{1,0:T(8,128)}, /*i...) custom-call(s32[2]{0:T(128)} %pad_add_fusion.1.place_ref, ...), custom_call_target="tpu_custom_call" | custom-call | bytes 1048576 | tf_op jit(solution)/shard_map/pallas_call | solution.py:389
  39.1 2.0 %collective-permute-start.1 = (f32[64,128]{1,0:T(8,128)}, f32[64,128]{1,0:T(8,128)S(1)}, u32[]{:S(2)}, u32[]{:S(2)}) collective-permute-start(f32[64,128]{1,0:T(8,128)} %get-tuple-element.24), channel_id=1, source_target_pairs={{0,2},{1,3},{2,4},{3,5},{4,6},{5,7},{6,8},{7,9},{8,10},{9,11},{10,... | collective-permute-start | bytes 98312 | tf_op jit(solution)/shard_map/ppermute | solution.py:332
  41.2 5.7 %collective-permute-start.3 = (f32[64,128]{1,0:T(8,128)}, f32[64,128]{1,0:T(8,128)S(1)}, u32[]{:S(2)}, u32[]{:S(2)}) collective-permute-start(f32[64,128]{1,0:T(8,128)} %get-tuple-element.26), channel_id=1, source_target_pairs={{0,4},{1,5},{2,6},{3,7},{4,8},{5,9},{6,10},{7,11},{8,12},{9,13},{1... | collective-permute-start | bytes 98312 | tf_op jit(solution)/shard_map/ppermute | solution.py:332
  46.9 3.4 %collective-permute-start.5 = (f32[64,128]{1,0:T(8,128)}, f32[64,128]{1,0:T(8,128)S(1)}, u32[]{:S(2)}, u32[]{:S(2)}) collective-permute-start(f32[64,128]{1,0:T(8,128)} %get-tuple-element.28), channel_id=1, source_target_pairs={{0,6},{1,7},{2,8},{3,9},{4,10},{5,11},{6,12},{7,13},{8,14},{9,15},... | collective-permute-start | bytes 98312 | tf_op jit(solution)/shard_map/ppermute | solution.py:332
  50.3 1.7 %collective-permute-start.6 = (f32[64,128]{1,0:T(8,128)}, f32[64,128]{1,0:T(8,128)S(1)}, u32[]{:S(2)}, u32[]{:S(2)}) collective-permute-start(f32[64,128]{1,0:T(8,128)} %get-tuple-element.29), channel_id=1, source_target_pairs={{0,10},{1,11},{2,12},{3,13},{4,14},{5,15},{6,0},{7,1},{8,2},{9,3},... | collective-permute-start | bytes 98312 | tf_op jit(solution)/shard_map/ppermute | solution.py:332
  52.0 2.6 %collective-permute-start.7 = (f32[64,128]{1,0:T(8,128)}, f32[64,128]{1,0:T(8,128)S(1)}, u32[]{:S(2)}, u32[]{:S(2)}) collective-permute-start(f32[64,128]{1,0:T(8,128)} %get-tuple-element.30), channel_id=1, source_target_pairs={{0,8},{1,9},{2,10},{3,11},{4,12},{5,13},{6,14},{7,15},{8,0},{9,1},... | collective-permute-start | bytes 98312 | tf_op jit(solution)/shard_map/ppermute | solution.py:332
  55.2 3.9 %collective-permute-done.6.rest_5_.rest_6_ = f32[64,128]{1,0:T(8,128)S(1)} collective-permute-done((f32[64,128]{1,0:T(8,128)}, f32[64,128]{1,0:T(8,128)S(1)}, u32[]{:S(2)}, u32[]{:S(2)}) %collective-permute-start.6) | collective-permute-done | bytes 32800 | tf_op jit(solution)/shard_map/ppermute | solution.py:332
  59.1 1.7 %collective-permute-done.7.rest_6_.rest_7_ = f32[64,128]{1,0:T(8,128)S(1)} collective-permute-done((f32[64,128]{1,0:T(8,128)}, f32[64,128]{1,0:T(8,128)S(1)}, u32[]{:S(2)}, u32[]{:S(2)}) %collective-permute-start.7) | collective-permute-done | bytes 32800 | tf_op jit(solution)/shard_map/ppermute | solution.py:332
  60.8 4.6 %all-to-all-done.1 = bf16[16,512,128]{2,1,0:T(8,128)(2,1)S(1)} async-done(((bf16[16,512,128]{2,1,0:T(8,128)(2,1)}), bf16[16,512,128]{2,1,0:T(8,128)(2,1)S(1)}, u32[]{:S(2)}, u32[]{:S(2)}) %all-to-all-start.1) | async-done | bytes 2097184 | tf_op jit(solution)/shard_map/all_to_all | solution.py:386
  66.4 2.6 %collective-permute-done.8.other_ref = bf16[64,64,128]{2,1,0:T(8,128)(2,1)S(1)} collective-permute-done((bf16[64,64,128]{2,1,0:T(8,128)(2,1)S(1)}, bf16[64,64,128]{2,1,0:T(8,128)(2,1)S(1)}, u32[]{:S(2)}, u32[]{:S(2)}) %collective-permute-start.8) | collective-permute-done | bytes 1048608 | tf_op jit(solution)/shard_map/ppermute | solution.py:408
  69.0 10.3 %shard_map.125.mean_ref = f32[8,64,128]{2,1,0:T(8,128)} custom-call(s32[1]{0:T(128)S(6)} %select_n.12.core_ref, s32[64]{0:T(128)S(1)} %copy-done.13, s32[15360]{0:T(1024)S(1)} %reshape.38.rest_7_.near_ref, bf16[64,64,128]{2,1,0:T(8,128)(2,1)S(1)} %shard_map.124.own_ref, bf16[64,64,128]{2,1,0:T(8,128)(2,1)S(1)} %collective-permute-done.8.other_ref), custom_call_target="tpu_custom_call" | custom-call | bytes 31457280 | tf_op jit(solution)/shard_map/pallas_call | solution.py:402
  79.4 8.1 %all-to-all-start.2 = ((f32[8,64,128]{2,1,0:T(8,128)}), f32[8,64,128]{2,1,0:T(8,128)S(1)}, u32[]{:S(2)}, u32[]{:S(2)}) async-start(f32[8,64,128]{2,1,0:T(8,128)} %shard_map.125.mean_ref), calls=%async_computation.2 | async-start | bytes 524288 | tf_op jit(solution)/shard_map/all_to_all | solution.py:422
  87.5 6.2 %shard_map.127 = (f32[64,1024]{1,0:T(8,128)}, bf16[16,64,1024]{2,1,0:T(8,128)(2,1)}) custom-call(s32[2]{0:T(128)} %pad_add_fusion.1.place_ref, f32[1,1024]{1,0:T(1,128)} %bitcast.22, bf16[16,3,64,1024]{3,2,1,0:T(8,128)(2,1)} %bitcast.19, f32[64,128]{1,0:T(8,128)} %get-tuple-element.31.rest_0_, f32[64,128]{1,0:T(8,128)} %copy-done.3, f32[64,128]{1,0:T(8,128)} %copy-done.4, ...), custom_call_target="tpu_custom_call" | custom-call | flops 402653184 | bytes 9437184 | tf_op jit(solution)/shard_map/pallas_call | solution.py:410
  93.8 2.9 %all-to-all-done.2.mean_ref = f32[8,64,128]{2,1,0:T(8,128)S(1)} async-done(((f32[8,64,128]{2,1,0:T(8,128)}), f32[8,64,128]{2,1,0:T(8,128)S(1)}, u32[]{:S(2)}, u32[]{:S(2)}) %all-to-all-start.2) | async-done | bytes 262176 | tf_op jit(solution)/shard_map/all_to_all | solution.py:422
  96.6 1.6 copy-done
  99.2 1.6 shard_map.128
  102.0 1.8 %collective-permute-start.12 = (bf16[64,1024]{1,0:T(8,128)(2,1)S(1)}, bf16[64,1024]{1,0:T(8,128)(2,1)S(1)}, u32[]{:S(2)}, u32[]{:S(2)}) collective-permute-start(bf16[64,1024]{1,0:T(8,128)(2,1)S(1)} %get-tuple-element.36.near_ref), channel_id=1, source_target_pairs={{0,12},{1,13},{2,14},{3,15},{4,0},{5,1},{6,2},{7,3},{8,4},{9,5},{1... | collective-permute-start | bytes 393224 | tf_op jit(solution)/shard_map/ppermute | solution.py:332
  104.6 2.5 %collective-permute-start.10 = (bf16[64,1024]{1,0:T(8,128)(2,1)S(1)}, bf16[64,1024]{1,0:T(8,128)(2,1)S(1)}, u32[]{:S(2)}, u32[]{:S(2)}) collective-permute-start(bf16[64,1024]{1,0:T(8,128)(2,1)S(1)} %get-tuple-element.36.near_ref), channel_id=1, source_target_pairs={{0,14},{1,15},{2,0},{3,1},{4,2},{5,3},{6,4},{7,5},{8,6},{9,7},{10,... | collective-permute-start | bytes 393224 | tf_op jit(solution)/shard_map/ppermute | solution.py:332
  107.0 1.3 collective-permute-done.11.rest_2_
  108.4 2.4 %collective-permute-start.13 = (bf16[64,1024]{1,0:T(8,128)(2,1)S(1)}, bf16[64,1024]{1,0:T(8,128)(2,1)S(1)}, u32[]{:S(2)}, u32[]{:S(2)}) collective-permute-start(bf16[64,1024]{1,0:T(8,128)(2,1)S(1)} %collective-permute-done.11.rest_2_), channel_id=1, source_target_pairs={{0,2},{1,3},{2,4},{3,5},{4,6},{5,7},{6,8},{7,9},{8,10},{9,11},{10,... | collective-permute-start | bytes 393224 | tf_op jit(solution)/shard_map/ppermute | solution.py:332
  112.7 3.0 %collective-permute-start.15 = (bf16[32,1024]{1,0:T(8,128)(2,1)S(1)}, bf16[32,1024]{1,0:T(8,128)(2,1)S(1)}, u32[]{:S(2)}, u32[]{:S(2)}) collective-permute-start(bf16[32,1024]{1,0:T(8,128)(2,1)S(1)} %slice.24), channel_id=1, source_target_pairs={{0,4},{1,5},{2,6},{3,7},{4,8},{5,9},{6,10},{7,11},{8,12},{9,13},{1... | collective-permute-start | bytes 196616 | tf_op jit(solution)/shard_map/ppermute | solution.py:332
  116.4 2.1 %collective-permute-done.15.rest_6_ = bf16[32,1024]{1,0:T(8,128)(2,1)S(1)} collective-permute-done((bf16[32,1024]{1,0:T(8,128)(2,1)S(1)}, bf16[32,1024]{1,0:T(8,128)(2,1)S(1)}, u32[]{:S(2)}, u32[]{:S(2)}) %collective-permute-start.15) | collective-permute-done | bytes 65568 | tf_op jit(solution)/shard_map/ppermute | solution.py:332
  118.6 3.6 %collective-permute-done.16.rest_7_ = bf16[32,1024]{1,0:T(8,128)(2,1)S(1)} collective-permute-done((bf16[32,1024]{1,0:T(8,128)(2,1)S(1)}, bf16[32,1024]{1,0:T(8,128)(2,1)S(1)}, u32[]{:S(2)}, u32[]{:S(2)}) %collective-permute-start.16) | collective-permute-done | bytes 65568 | tf_op jit(solution)/shard_map/ppermute | solution.py:332
  122.2 1.7 %shard_map.129 = (f32[16,8,1024]{2,1,0:T(8,128)S(1)}, f32[16,8,1024]{2,1,0:T(8,128)S(1)}) custom-call(s32[2]{0:T(128)S(1)} %copy-done.11, f32[8,64,128]{2,1,0:T(8,128)S(1)} %copy-done.1, f32[8,64,128]{2,1,0:T(8,128)} %shard_map.125.mean_ref, bf16[64,1024]{1,0:T(8,128)(2,1)S(1)} %get-tuple-element.36.near_ref, ...), custom_call_target="tpu_custom_call" | custom-call | tf_op jit(solution)/shard_map/pallas_call | solution.py:438
  124.0 1.9 %collective-permute-done.17.right_ref = f32[16,8,1024]{2,1,0:T(8,128)S(1)} collective-permute-done((f32[16,8,1024]{2,1,0:T(8,128)S(1)}, f32[16,8,1024]{2,1,0:T(8,128)S(1)}, u32[]{:S(2)}, u32[]{:S(2)}) %collective-permute-start.17) | collective-permute-done | bytes 524320 | tf_op jit(solution)/shard_map/ppermute | solution.py:442
  126.0 14.7 %all_to_all.25.in_ref = f32[16,8,1024]{2,1,0:T(8,128)S(1)} all-to-all(f32[16,8,1024]{2,1,0:T(8,128)S(1)} %shard_map.130), channel_id=1, replica_groups=mesh['dom'=16,'feat'=16] {'dom'}, dimensions={0} | all-to-all | bytes 1048576 | tf_op jit(solution)/shard_map/all_to_all | solution.py:444
  140.8 14.0 %all_to_all.26 = f32[16,8,1024]{2,1,0:T(8,128)S(1)} all-to-all(f32[16,8,1024]{2,1,0:T(8,128)S(1)} %shard_map.131), channel_id=1, replica_groups=mesh['dom'=16,'feat'=16] {'dom'}, dimensions={0} | all-to-all | bytes 1048576 | tf_op jit(solution)/shard_map/all_to_all | solution.py:446
  (70 shorter events, 13.7 us)
Async XLA Ops:
  7.2 80.3 %all-gather.3.cloned.1.call-start = ((), (), s32[]{:S(2)}) async-start(), calls=%async_computation.5 | async-start | bytes 6684672 | tf_op jit(solution)/shard_map/all_gather | solution.py:343
  10.4 14.5 %all-to-all-start = ((s32[16,1,128]{2,1,0:T(1,128)}), s32[16,1,128]{2,1,0:T(1,128)S(1)}, u32[]{:S(2)}, u32[]{:S(2)}) async-start(s32[16,1,128]{2,1,0:T(1,128)} %broadcast_in_dim.4), calls=%async_computation | async-start | bytes 16384 | tf_op jit(solution)/shard_map/all_to_all | solution.py:338
  29.0 25.5 %copy-start.15 = (s32[15,1024]{1,0:T(8,128)S(1)}, s32[15,1024]{1,0:T(8,128)}, u32[]{:S(2)}) copy-start(s32[15,1024]{1,0:T(8,128)} %param.12) | copy-start | bytes 184324
  29.1 36.3 %copy-start.12 = (s32[64,1]{0,1:T(1,128)S(1)}, s32[64,1]{0,1:T(1,128)}, u32[]{:S(2)}) copy-start(s32[64,1]{0,1:T(1,128)} %param.13) | copy-start | bytes 772
  29.1 36.3 %all-to-all-start.1 = ((bf16[16,512,128]{2,1,0:T(8,128)(2,1)}), bf16[16,512,128]{2,1,0:T(8,128)(2,1)S(1)}, u32[]{:S(2)}, u32[]{:S(2)}) async-start(bf16[16,512,128]{2,1,0:T(8,128)(2,1)} %bitcast.18), calls=%async_computation.1 | async-start | bytes 4194304 | tf_op jit(solution)/shard_map/all_to_all | solution.py:386
  35.1 1.4 collective-permute-start
  39.1 11.2 %collective-permute-start.1 = (f32[64,128]{1,0:T(8,128)}, f32[64,128]{1,0:T(8,128)S(1)}, u32[]{:S(2)}, u32[]{:S(2)}) collective-permute-start(f32[64,128]{1,0:T(8,128)} %get-tuple-element.24), channel_id=1, source_target_pairs={{0,2},{1,3},{2,4},{3,5},{4,6},{5,7},{6,8},{7,9},{8,10},{9,11},{10,... | collective-permute-start | bytes 98312 | tf_op jit(solution)/shard_map/ppermute | solution.py:332
  41.1 10.8 %collective-permute-start.2 = (f32[64,128]{1,0:T(8,128)}, f32[64,128]{1,0:T(8,128)S(1)}, u32[]{:S(2)}, u32[]{:S(2)}) collective-permute-start(f32[64,128]{1,0:T(8,128)} %get-tuple-element.25), channel_id=1, source_target_pairs={{0,14},{1,15},{2,0},{3,1},{4,2},{5,3},{6,4},{7,5},{8,6},{9,7},{10,... | collective-permute-start | bytes 98312 | tf_op jit(solution)/shard_map/ppermute | solution.py:332
  41.2 14.0 %collective-permute-start.3 = (f32[64,128]{1,0:T(8,128)}, f32[64,128]{1,0:T(8,128)S(1)}, u32[]{:S(2)}, u32[]{:S(2)}) collective-permute-start(f32[64,128]{1,0:T(8,128)} %get-tuple-element.26), channel_id=1, source_target_pairs={{0,4},{1,5},{2,6},{3,7},{4,8},{5,9},{6,10},{7,11},{8,12},{9,13},{1... | collective-permute-start | bytes 98312 | tf_op jit(solution)/shard_map/ppermute | solution.py:332
  46.9 8.2 %collective-permute-start.4 = (f32[64,128]{1,0:T(8,128)}, f32[64,128]{1,0:T(8,128)S(1)}, u32[]{:S(2)}, u32[]{:S(2)}) collective-permute-start(f32[64,128]{1,0:T(8,128)} %get-tuple-element.27), channel_id=1, source_target_pairs={{0,12},{1,13},{2,14},{3,15},{4,0},{5,1},{6,2},{7,3},{8,4},{9,5},{1... | collective-permute-start | bytes 98312 | tf_op jit(solution)/shard_map/ppermute | solution.py:332
  46.9 8.3 %collective-permute-start.5 = (f32[64,128]{1,0:T(8,128)}, f32[64,128]{1,0:T(8,128)S(1)}, u32[]{:S(2)}, u32[]{:S(2)}) collective-permute-start(f32[64,128]{1,0:T(8,128)} %get-tuple-element.28), channel_id=1, source_target_pairs={{0,6},{1,7},{2,8},{3,9},{4,10},{5,11},{6,12},{7,13},{8,14},{9,15},... | collective-permute-start | bytes 98312 | tf_op jit(solution)/shard_map/ppermute | solution.py:332
  50.3 16.0 %copy-start.3 = (f32[64,128]{1,0:T(8,128)}, f32[64,128]{1,0:T(8,128)S(1)}, u32[]{:S(2)}) copy-start(f32[64,128]{1,0:T(8,128)S(1)} %collective-permute-done.1.rest_0_.rest_1_) | copy-start | bytes 98308
  50.3 8.8 %collective-permute-start.6 = (f32[64,128]{1,0:T(8,128)}, f32[64,128]{1,0:T(8,128)S(1)}, u32[]{:S(2)}, u32[]{:S(2)}) collective-permute-start(f32[64,128]{1,0:T(8,128)} %get-tuple-element.29), channel_id=1, source_target_pairs={{0,10},{1,11},{2,12},{3,13},{4,14},{5,15},{6,0},{7,1},{8,2},{9,3},... | collective-permute-start | bytes 98312 | tf_op jit(solution)/shard_map/ppermute | solution.py:332
  52.0 8.8 %collective-permute-start.7 = (f32[64,128]{1,0:T(8,128)}, f32[64,128]{1,0:T(8,128)S(1)}, u32[]{:S(2)}, u32[]{:S(2)}) collective-permute-start(f32[64,128]{1,0:T(8,128)} %get-tuple-element.30), channel_id=1, source_target_pairs={{0,8},{1,9},{2,10},{3,11},{4,12},{5,13},{6,14},{7,15},{8,0},{9,1},... | collective-permute-start | bytes 98312 | tf_op jit(solution)/shard_map/ppermute | solution.py:332
  55.1 24.2 %copy-start.5 = (f32[64,128]{1,0:T(8,128)}, f32[64,128]{1,0:T(8,128)S(1)}, u32[]{:S(2)}) copy-start(f32[64,128]{1,0:T(8,128)S(1)} %collective-permute-done.3.rest_2_.rest_3_) | copy-start | bytes 98308
  55.2 24.2 %copy-start.6 = (f32[64,128]{1,0:T(8,128)}, f32[64,128]{1,0:T(8,128)S(1)}, u32[]{:S(2)}) copy-start(f32[64,128]{1,0:T(8,128)S(1)} %collective-permute-done.4.rest_3_.rest_4_) | copy-start | bytes 98308
  55.2 24.1 %copy-start.7 = (f32[64,128]{1,0:T(8,128)}, f32[64,128]{1,0:T(8,128)S(1)}, u32[]{:S(2)}) copy-start(f32[64,128]{1,0:T(8,128)S(1)} %collective-permute-done.5.rest_4_.rest_5_) | copy-start | bytes 98308
  59.1 20.3 %copy-start.8 = (f32[64,128]{1,0:T(8,128)}, f32[64,128]{1,0:T(8,128)S(1)}, u32[]{:S(2)}) copy-start(f32[64,128]{1,0:T(8,128)S(1)} %collective-permute-done.6.rest_5_.rest_6_) | copy-start | bytes 98308
  60.8 18.6 %copy-start.9 = (f32[64,128]{1,0:T(8,128)}, f32[64,128]{1,0:T(8,128)S(1)}, u32[]{:S(2)}) copy-start(f32[64,128]{1,0:T(8,128)S(1)} %collective-permute-done.7.rest_6_.rest_7_) | copy-start | bytes 98308
  66.3 2.7 %collective-permute-start.8 = (bf16[64,64,128]{2,1,0:T(8,128)(2,1)S(1)}, bf16[64,64,128]{2,1,0:T(8,128)(2,1)S(1)}, u32[]{:S(2)}, u32[]{:S(2)}) collective-permute-start(bf16[64,64,128]{2,1,0:T(8,128)(2,1)S(1)} %shard_map.124.own_ref), channel_id=1, source_target_pairs={{0,1},{1,0},{2,3},{3,2},{4,5},{5,4},{6,7},{7,6},{8,9},{9,8},{10,11... | collective-permute-start | bytes 3145736 | tf_op jit(solution)/shard_map/ppermute | solution.py:408
  79.4 17.3 %all-to-all-start.2 = ((f32[8,64,128]{2,1,0:T(8,128)}), f32[8,64,128]{2,1,0:T(8,128)S(1)}, u32[]{:S(2)}, u32[]{:S(2)}) async-start(f32[8,64,128]{2,1,0:T(8,128)} %shard_map.125.mean_ref), calls=%async_computation.2 | async-start | bytes 524288 | tf_op jit(solution)/shard_map/all_to_all | solution.py:422
  87.5 34.7 %copy-start.1 = (f32[8,64,128]{2,1,0:T(8,128)S(1)}, f32[8,64,128]{2,1,0:T(8,128)}, u32[]{:S(2)}) copy-start(f32[8,64,128]{2,1,0:T(8,128)} %get-tuple-element.35.self_ref) | copy-start | bytes 786436
  93.8 28.5 %copy-start.11 = (s32[2]{0:T(128)S(1)}, s32[2]{0:T(128)}, u32[]{:S(2)}) copy-start(s32[2]{0:T(128)} %pad_add_fusion.1.place_ref) | copy-start | bytes 28
  100.7 7.7 %collective-permute-start.11 = (bf16[64,1024]{1,0:T(8,128)(2,1)S(1)}, bf16[64,1024]{1,0:T(8,128)(2,1)S(1)}, u32[]{:S(2)}, u32[]{:S(2)}) collective-permute-start(bf16[64,1024]{1,0:T(8,128)(2,1)S(1)} %get-tuple-element.36.near_ref), channel_id=1, source_target_pairs={{0,4},{1,5},{2,6},{3,7},{4,8},{5,9},{6,10},{7,11},{8,12},{9,13},{1... | collective-permute-start | bytes 393224 | tf_op jit(solution)/shard_map/ppermute | solution.py:332
  102.0 10.0 %collective-permute-start.12 = (bf16[64,1024]{1,0:T(8,128)(2,1)S(1)}, bf16[64,1024]{1,0:T(8,128)(2,1)S(1)}, u32[]{:S(2)}, u32[]{:S(2)}) collective-permute-start(bf16[64,1024]{1,0:T(8,128)(2,1)S(1)} %get-tuple-element.36.near_ref), channel_id=1, source_target_pairs={{0,12},{1,13},{2,14},{3,15},{4,0},{5,1},{6,2},{7,3},{8,4},{9,5},{1... | collective-permute-start | bytes 393224 | tf_op jit(solution)/shard_map/ppermute | solution.py:332
  103.8 11.9 %collective-permute-start.9 = (bf16[64,1024]{1,0:T(8,128)(2,1)S(1)}, bf16[64,1024]{1,0:T(8,128)(2,1)S(1)}, u32[]{:S(2)}, u32[]{:S(2)}) collective-permute-start(bf16[64,1024]{1,0:T(8,128)(2,1)S(1)} %get-tuple-element.36.near_ref), channel_id=1, source_target_pairs={{0,2},{1,3},{2,4},{3,5},{4,6},{5,7},{6,8},{7,9},{8,10},{9,11},{10,... | collective-permute-start | bytes 393224 | tf_op jit(solution)/shard_map/ppermute | solution.py:332
  104.6 11.9 %collective-permute-start.10 = (bf16[64,1024]{1,0:T(8,128)(2,1)S(1)}, bf16[64,1024]{1,0:T(8,128)(2,1)S(1)}, u32[]{:S(2)}, u32[]{:S(2)}) collective-permute-start(bf16[64,1024]{1,0:T(8,128)(2,1)S(1)} %get-tuple-element.36.near_ref), channel_id=1, source_target_pairs={{0,14},{1,15},{2,0},{3,1},{4,2},{5,3},{6,4},{7,5},{8,6},{9,7},{10,... | collective-permute-start | bytes 393224 | tf_op jit(solution)/shard_map/ppermute | solution.py:332
  108.4 13.8 %collective-permute-start.13 = (bf16[64,1024]{1,0:T(8,128)(2,1)S(1)}, bf16[64,1024]{1,0:T(8,128)(2,1)S(1)}, u32[]{:S(2)}, u32[]{:S(2)}) collective-permute-start(bf16[64,1024]{1,0:T(8,128)(2,1)S(1)} %collective-permute-done.11.rest_2_), channel_id=1, source_target_pairs={{0,2},{1,3},{2,4},{3,5},{4,6},{5,7},{6,8},{7,9},{8,10},{9,11},{10,... | collective-permute-start | bytes 393224 | tf_op jit(solution)/shard_map/ppermute | solution.py:332
  112.0 10.2 %collective-permute-start.14 = (bf16[64,1024]{1,0:T(8,128)(2,1)S(1)}, bf16[64,1024]{1,0:T(8,128)(2,1)S(1)}, u32[]{:S(2)}, u32[]{:S(2)}) collective-permute-start(bf16[64,1024]{1,0:T(8,128)(2,1)S(1)} %collective-permute-done.12.rest_3_), channel_id=1, source_target_pairs={{0,14},{1,15},{2,0},{3,1},{4,2},{5,3},{6,4},{7,5},{8,6},{9,7},{10,... | collective-permute-start | bytes 393224 | tf_op jit(solution)/shard_map/ppermute | solution.py:332
  112.7 5.9 %collective-permute-start.15 = (bf16[32,1024]{1,0:T(8,128)(2,1)S(1)}, bf16[32,1024]{1,0:T(8,128)(2,1)S(1)}, u32[]{:S(2)}, u32[]{:S(2)}) collective-permute-start(bf16[32,1024]{1,0:T(8,128)(2,1)S(1)} %slice.24), channel_id=1, source_target_pairs={{0,4},{1,5},{2,6},{3,7},{4,8},{5,9},{6,10},{7,11},{8,12},{9,13},{1... | collective-permute-start | bytes 196616 | tf_op jit(solution)/shard_map/ppermute | solution.py:332
  115.7 6.5 %collective-permute-start.16 = (bf16[32,1024]{1,0:T(8,128)(2,1)S(1)}, bf16[32,1024]{1,0:T(8,128)(2,1)S(1)}, u32[]{:S(2)}, u32[]{:S(2)}) collective-permute-start(bf16[32,1024]{1,0:T(8,128)(2,1)S(1)} %slice.25), channel_id=1, source_target_pairs={{0,12},{1,13},{2,14},{3,15},{4,0},{5,1},{6,2},{7,3},{8,4},{9,5},{1... | collective-permute-start | bytes 196616 | tf_op jit(solution)/shard_map/ppermute | solution.py:332
  123.9 2.0 %collective-permute-start.17 = (f32[16,8,1024]{2,1,0:T(8,128)S(1)}, f32[16,8,1024]{2,1,0:T(8,128)S(1)}, u32[]{:S(2)}, u32[]{:S(2)}) collective-permute-start(f32[16,8,1024]{2,1,0:T(8,128)S(1)} %get-tuple-element.38), channel_id=1, source_target_pairs={{0,1},{1,0},{2,3},{3,2},{4,5},{5,4},{6,7},{7,6},{8,9},{9,8},{10,11... | collective-permute-start | bytes 1572872 | tf_op jit(solution)/shard_map/ppermute | solution.py:442
  (8 other events, 47.5 us)
Sparse Core Ops, SparseCore 0:
  9.8 53.2 all-gather.2

commit v3 on v2

--- a/solution.py
+++ b/solution.py
@@ -71,18 +71,13 @@
         window = pl.ds(2 * pairs * part, 2 * pairs)
         outs.append(pltpu.make_async_copy(packed.at[window], packed_ref.at[window], out_sems.at[part]))
         outs[-1].start()
-    lane = lane_of((1, BLOCK)) < HALF
     seeds.wait()
 
     def pick(chip, carry):
         for mine, ref in ((True, keep_ref), (False, send_ref)):
-            group = 2 * chip + (core if mine else 1 - core)
-            for step in range(32):
-                lead = seed_ref[group * 64 + step + 32 * core]
-                trail = seed_ref[group * 64 + step + 32 * (1 - core)]
-                low = rows[pl.ds(lead, 1), :]
-                high = rows[pl.ds(lax.bitwise_xor(trail, BLOCK), 1), :]
-                ref[chip, pl.ds(step, 1), :] = jnp.where(lane, low, high)
+            base = (2 * chip + (core if mine else 1 - core)) * 64
+            for step in range(64):
+                ref[chip, pl.ds(step, 1), :] = rows[pl.ds(seed_ref[base + step], 1), :]
         return carry
 
     lax.fori_loop(0, keep_ref.shape[0], pick, 0)
@@ -90,9 +85,18 @@
         copy.wait()
 
 
-def pack_kernel(me_ref, request_ref, packed_hbm, out_hbm, wanted, wanted_smem, packed_ref, out_ref, sem, in_sem, out_sems):
+def pack_kernel(
+    me_ref, request_ref, packed_hbm, self_hbm, neigh_hbm, out_hbm, weight_ref,
+    wanted, wanted_smem, packed_ref, both, out_ref, sem, in_sem, out_sems, weight_sems,
+):
     fetch = pltpu.make_async_copy(packed_hbm, packed_ref, in_sem)
     fetch.start()
+    weights = [
+        pltpu.make_async_copy(ref, both.at[which], weight_sems.at[which])
+        for which, ref in enumerate((self_hbm, neigh_hbm))
+    ]
+    for copy in weights:
+        copy.start()
     me = me_ref[0]
     request = request_ref[...]
     parts = request.shape[0]
@@ -109,8 +113,13 @@
     wanted[...] = result.astype(jnp.int32)
     copy = pltpu.make_async_copy(wanted, wanted_smem, sem)
     copy.start()
+    for held in weights:
+        held.wait()
+    high, low = split(both[0])
+    weight_ref[0] = high
+    weight_ref[1] = low
+    weight_ref[2] = both[1].astype(BF16)
     copy.wait()
-
     fetch.wait()
     copies = []
     for part in range(parts):
@@ -174,33 +183,22 @@
 
 def join_kernel(place_ref, own_ref, other_ref, *rest):
     out_ref, sends = rest[0], rest[1:]
-    straight = (lane_of((32, BLOCK)) < HALF) == (place_ref[0] == 0)
+    lane = lane_of((64, BLOCK)) < HALF
+    first = place_ref[0] == 0
     ring = own_ref.shape[0]
     for shift in range(ring):
         group = lax.rem(place_ref[1] + shift, ring)
         own, other = own_ref[group], other_ref[group]
-        upper = jnp.where(straight, own, other)
-        lower = pltpu.roll(jnp.where(straight, other, own), HALF, 1)
-        out_ref[group, :32] = upper
-        out_ref[group, 32:] = lower
-        target = sends[shift]
-        target[:32] = upper
-        target[32:] = lower
-
-
-def weight_kernel(self_hbm, neigh_hbm, out_ref, both, sems):
-    copies = [
-        pltpu.make_async_copy(ref, both.at[which], sems.at[which])
-        for which, ref in enumerate((self_hbm, neigh_hbm))
-    ]
-    for copy in copies:
-        copy.start()
-    copies[0].wait()
-    high, low = split(both[0])
-    out_ref[0] = high
-    out_ref[1] = low
-    copies[1].wait()
-    out_ref[2] = both[1].astype(BF16)
+        left, right = jnp.where(first, own, other), jnp.where(first, other, own)
+        joined = jnp.where(lane, left, pltpu.roll(right, HALF, 1))
+        out_ref[group] = joined
+        sends[shift][...] = joined
+
+
+def open_kernel(owner_ref, block_ref, request_ref):
+    request = jnp.concatenate([owner_ref[...], block_ref[...]], axis=1)
+    for part in range(request_ref.shape[0]):
+        request_ref[part] = request
 
 
 def three(left, right_high, right_low):
@@ -211,23 +209,22 @@
 def self_kernel(place_ref, bias_ref, weight_hbm, *rest):
     pieces = rest[:8]
     part_ref, neigh_ref, held, rows, sems, row_sems = rest[8:]
-    row_copies = [
-        pltpu.make_async_copy(piece, rows.at[index], row_sems.at[index]) for index, piece in enumerate(pieces)
-    ]
-    for copy in row_copies:
-        copy.start()
     chips = [lax.rem(place_ref[1] + 8 - distance, 8) for distance in DISTANCES]
-    copies = []
-    for index, chip in enumerate(chips):
+    copies, row_copies = [], []
+    for index, (piece, chip) in enumerate(zip(pieces, chips)):
+        row_copies.append(pltpu.make_async_copy(piece, rows.at[index], row_sems.at[index]))
+        row_copies[-1].start()
         pair = weight_hbm.at[pl.ds(2 * chip, 2), pl.ds(0, 2)]
         copies.append(pltpu.make_async_copy(pair, held.at[index], sems.at[index]))
         copies[-1].start()
     neigh_copies = []
-    for core in range(16):
-        target = neigh_ref.at[core]
-        neigh_copies.append(pltpu.make_async_copy(weight_hbm.at[core, 2], target, sems.at[8 + core]))
+    for step in range(4):
+        window = pl.ds(4 * step, 4)
+        neigh_copies.append(
+            pltpu.make_async_copy(weight_hbm.at[window, 2], neigh_ref.at[window], sems.at[8 + step])
+        )
         neigh_copies[-1].start()
-    part_ref[...] = jnp.broadcast_to(bias_ref[...], part_ref.shape)
+    total = jnp.broadcast_to(bias_ref[...], part_ref.shape)
     for step in range(4):
         pair = (2 * step, 2 * step + 1)
         for index in pair:
@@ -238,36 +235,40 @@
             jnp.concatenate([held[index, core, which] for index in pair for core in range(2)], axis=0)
             for which in range(2)
         ]
-        part_ref[...] += three(left, high, low)
+        total = total + three(left, high, low)
+    part_ref[...] = total
     for copy in neigh_copies:
         copy.wait()
 
 
 def forward_kernel(mean_ref, part_ref, weight_ref, cotangent_ref, hidden_ref, slope_ref):
     preact = part_ref[...]
-    left = jnp.concatenate([mean_ref[chip] for chip in range(8)], axis=1)
-    right = weight_ref[...]
-    for piece in split(left):
-        preact += dot(piece, right)
+    for step in range(4):
+        left = jnp.concatenate([mean_ref[2 * step], mean_ref[2 * step + 1]], axis=1)
+        right = weight_ref[4 * step : 4 * step + 4].reshape(256, weight_ref.shape[2])
+        for piece in split(left):
+            preact = preact + dot(piece, right)
     sigma = 1.0 / (1.0 + jnp.exp(-preact))
     hidden_ref[...] = (preact * sigma).astype(BF16)
     slope = cotangent_ref[...].astype(F32) * (sigma * (1.0 + preact * (1.0 - sigma)))
     slope_ref[...] = slope.astype(BF16)
 
 
-def gradient_kernel(place_ref, self_ref, mean_ref, near_ref, *rest):
+def turn_kernel(place_ref, self_ref, mean_ref, high_ref, low_ref):
+    rows = [lax.rem(place_ref[1] + 8 - k, 8) for k in DISTANCES]
+    for which, ref in enumerate((self_ref, mean_ref)):
+        turned = jnp.concatenate([ref[r] for r in rows], axis=0).T
+        window = slice(which * BLOCK, (which + 1) * BLOCK)
+        high_ref[window], low_ref[window] = split(turned)
+
+
+def gradient_kernel(place_ref, high_ref, low_ref, near_ref, *rest):
     slopes, (keep_ref, send_ref) = rest[:-2], rest[-2:]
-    here = place_ref[1]
-    rows = [lax.rem(here - k + 8, 8) for k in DISTANCES]
     right = jnp.concatenate([near_ref[...]] + [ref[...] for ref in slopes], axis=0)
     first = place_ref[0] == 0
-    for which, ref in enumerate((self_ref, mean_ref)):
-        left = jnp.concatenate([ref[r] for r in rows], axis=0)
-        total = 0.0
-        for piece in split(left):
-            total = total + lax.dot_general(
-                piece, right, (((0,), (0,)), ((), ())), preferred_element_type=F32
-            )
+    for which in range(2):
+        window = slice(which * BLOCK, (which + 1) * BLOCK)
+        total = dot(high_ref[window], right) + dot(low_ref[window], right)
         for chunk in range(8):
             start = chunk * 8
             one, two = total[start : start + 8], total[64 + start : 64 + start + 8]
@@ -296,7 +297,7 @@
         input_output_aliases=aliases,
         scratch_shapes=list(scratch),
         cost_estimate=cost,
-        compiler_params=pltpu.CompilerParams(vmem_limit_bytes=limit << 20),
+        compiler_params=pltpu.CompilerParams(vmem_limit_bytes=int(limit * (1 << 20))),
     )
 
 
@@ -334,26 +335,20 @@
     owner_ids = owners[:, 0]
     shape = jax.ShapeDtypeStruct
 
-    request = jnp.concatenate([owner_ids, blocks])
-    requests = lax.all_to_all(
-        jnp.broadcast_to(request[None, None, :], (n_dom, 1, 2 * owner_ids.shape[0])),
-        "dom", split_axis=0, concat_axis=0, tiled=True,
-    ).reshape(n_dom, 2 * owner_ids.shape[0])
+    entries_here = owner_ids.shape[0]
+    request = call(
+        open_kernel, shape((n_dom, 1, 2 * entries_here), jnp.int32), [VMEM, VMEM], limit=60
+    )(owner_ids[None, :], blocks[None, :])
+    requests = lax.all_to_all(request, "dom", split_axis=0, concat_axis=0, tiled=True).reshape(
+        n_dom, 2 * entries_here
+    )
     near = jnp.transpose(neighbours).reshape(-1)
-    weights = lax.all_gather(
-        call(
-            weight_kernel, shape((3, 64, hidden_width), BF16), [ANY, ANY],
-            [pltpu.VMEM((2, 64, hidden_width), F32), pltpu.SemaphoreType.DMA((2,))], limit=60,
-        )(w_self, w_neigh),
-        "feat", axis=0, tiled=False,
-    )
-
     packed, kept, given = call(
         prepare_kernel,
         (
             shape((feature_table.shape[1] // BLOCK, HALF, BLOCK), BF16),
-            shape((ring, 32, BLOCK), F32),
-            shape((ring, 32, BLOCK), F32),
+            shape((ring, 64, BLOCK), F32),
+            shape((ring, 64, BLOCK), F32),
         ),
         [SMEM, ANY, ANY],
         [
@@ -361,28 +356,31 @@
             pltpu.VMEM(feature_table.shape, F32),
             pltpu.SMEM(seed_ids.shape, jnp.int32),
             pltpu.VMEM((feature_table.shape[1] // BLOCK, HALF, BLOCK), BF16),
-            pltpu.SemaphoreType.DMA((4,)),
+            pltpu.SemaphoreType.DMA((8,)),
             pltpu.SemaphoreType.DMA,
-            pltpu.SemaphoreType.DMA((4,)),
+            pltpu.SemaphoreType.DMA((8,)),
         ],
         limit=60, cost=cost(0, 10 << 20), outs=(ANY, VMEM, VMEM),
     )(core, seed_ids, feature_table)
 
-    outgoing = call(
+    outgoing, weight = call(
         pack_kernel,
-        shape((n_dom, SLOTS, HALF, BLOCK), BF16),
-        [SMEM, VMEM, ANY],
+        (shape((n_dom, SLOTS, HALF, BLOCK), BF16), shape((3, 64, hidden_width), BF16)),
+        [SMEM, VMEM, ANY, ANY, ANY],
         [
             pltpu.VMEM((n_dom, BLOCK), jnp.int32),
             pltpu.SMEM((n_dom, BLOCK), jnp.int32),
             pltpu.VMEM(packed.shape, BF16),
+            pltpu.VMEM((2, 64, hidden_width), F32),
             pltpu.VMEM((n_dom, SLOTS, HALF, BLOCK), BF16),
             pltpu.SemaphoreType.DMA,
             pltpu.SemaphoreType.DMA,
             pltpu.SemaphoreType.DMA((n_dom,)),
+            pltpu.SemaphoreType.DMA((2,)),
         ],
-        limit=60, outs=ANY,
-    )(dom, requests, packed)
+        limit=59, outs=(ANY, VMEM),
+    )(dom, requests, packed, w_self, w_neigh)
+    weights = lax.all_gather(weight, "feat", axis=0, tiled=False)
     arrived = lax.all_to_all(
         outgoing.reshape(n_dom, SLOTS * HALF, BLOCK), "dom", split_axis=0, concat_axis=0, tiled=True
     )
@@ -414,10 +412,10 @@
         [
             pltpu.VMEM((ring, 2, 2, 64, hidden_width), BF16),
             pltpu.VMEM((ring, 64, BLOCK), F32),
-            pltpu.SemaphoreType.DMA((24,)),
+            pltpu.SemaphoreType.DMA((12,)),
             pltpu.SemaphoreType.DMA((ring,)),
         ],
-        limit=56, cost=cost(3 << 27, 9 << 20),
+        limit=24, cost=cost(3 << 27, 9 << 20),
     )(place, out_bias[None, :], weights, *pieces)
     mean_seeds = lax.all_to_all(
         mean, "feat", split_axis=0, concat_axis=0, tiled=True, axis_index_groups=columns
@@ -427,7 +425,7 @@
         forward_kernel,
         (shape((64, hidden_width), BF16), shape((64, hidden_width), BF16)),
         [VMEM] * 4, limit=8, cost=cost(2 << 27, 4 << 20),
-    )(mean_seeds, part, neigh_weight.reshape(-1, hidden_width), cotangent)
+    )(mean_seeds, part, neigh_weight, cotangent)
 
     up, down = climb(slope, 1), climb(slope, -1)
     up_two, down_two = climb(slope, 2), climb(slope, -2)
@@ -435,9 +433,12 @@
     up_four, down_four = climb(up_two[:32], 2), climb(down_two[32:], -2)
     slopes = [up, down, up_two, down_two, up_three, down_three, up_four, down_four]
 
+    turned = call(
+        turn_kernel, (shape((2 * BLOCK, ring * 64), BF16),) * 2, [SMEM, VMEM, VMEM], limit=8
+    )(place, self_rows, mean)
     keep, send = call(
         gradient_kernel, (shape((n_dom, 8, hidden_width), F32),) * 2, [SMEM] + [VMEM] * 11, limit=16
-    )(place, self_rows, mean, slope, *slopes)
+    )(place, *turned, slope, *slopes)
     partial = call(add_kernel, shape(keep.shape, F32), [VMEM, VMEM], limit=4)(
         keep, lax.ppermute(send, "feat", across)
     )

time: 163 us -> 159 us (0.975)
  Pallas kernels: 34.1 us -> 31.8 us
    pallas_call x1, Pallas kernels: 6.23 us -> 2.81 us  [body(): call(self_kernel, (shape((64, hidden_width), F32), shape((n_feat, 64, hid...]
    pallas_call x2 -> x3, Pallas kernels: 5.3 us -> 6.97 us  [the longest x1 4.46 us: body(): call(pack_kernel, (shape((n_dom, SLOTS, HALF, BLOCK), BF16), shape((3, 64...]
    unnamed x36 -> x24, local copies, waits for them, and re-layouts: 3.86 us -> 4.13 us
  transfers between devices with their start and end apart: 22 -> 22, of which waited for: 12 -> 12; matrix products, arithmetic and copies ran while one was open for 2% -> 1% of each run, Pallas kernels for 18% -> 15%
where the time goes in v3:
time: 159 us
  starting transfers between devices  50.3 us (32%)
  Pallas kernels  31.8 us (20%)
  blocking collectives  28.9 us (18%)
  waiting for transfers between devices  27.2 us (17%)
  between operations  14.3 us (9%)
  local copies, waits for them, and re-layouts  5.51 us (3%)
    ppermute x15, starting transfers between devices, climb(): return lax.ppermute(value, 'feat', pairs)  28.9 us
    all_to_all x1, blocking collectives, body(): lax.all_to_all(partial, 'dom', split_axis=0, concat_axis=0, tiled=True)  14.9 us
    all_to_all x1, blocking collectives, body(): lax.all_to_all(total, 'dom', split_axis=0, concat_axis=0, tiled=True)  14 us
    ppermute x15, waiting for transfers between devices, climb(): return lax.ppermute(value, 'feat', pairs)  12.5 us
    pallas_call x1, Pallas kernels, body(): call(gather_kernel, shape((ring, 64, BLOCK), F32), [SMEM, SMEM, SMEM, VME...  10.3 us
    all_to_all x1, starting transfers between devices, body(): lax.all_to_all(mean, 'feat', split_axis=0, concat_axis=0, tiled=True, axi...  8.09 us
    all_to_all x1, starting transfers between devices, body(): lax.all_to_all(request, 'dom', split_axis=0, concat_axis=0, tiled=True)  7.03 us
    pallas_call x1, Pallas kernels, body(): call(prepare_kernel, (shape((feature_table.shape[1] // BLOCK, HALF, BLOCK...  5.96 us
  transfers between devices with their start and end apart: 22, of which 12 were waited for; matrix products, arithmetic and copies ran while one was open for 1% of the time, Pallas kernels for 15%

profile of v3, /device:TPU:64, one launch (start us, length us, event | category | flops | bytes accessed | tf_op | source)
XLA Modules:
  0.0 158.6 jit_solution(17870774248987849627)
XLA Ops:
  7.2 1.3 shard_map.121
  8.5 7.0 %all-to-all-start = ((s32[16,1,128]{2,1,0:T(1,128)}), s32[16,1,128]{2,1,0:T(1,128)S(1)}, u32[]{:S(2)}, u32[]{:S(2)}) async-start(s32[16,1,128]{2,1,0:T(1,128)} %shard_map.121), calls=%async_computation | async-start | bytes 16384 | tf_op jit(solution)/shard_map/all_to_all | solution.py:342
  15.6 6.0 %shard_map.122 = (bf16[64,64,128]{2,1,0:T(8,128)(2,1)}, f32[8,64,128]{2,1,0:T(8,128)}, f32[8,64,128]{2,1,0:T(8,128)}) custom-call(s32[1]{0:T(128)S(6)} %select_n.12.core_ref, s32[1024]{0:T(1024)} %seed_hbm.1, f32[64,8192]{1,0:T(8,128)} %table_hbm.1), custom_call_target="tpu_custom_call" | custom-call | bytes 10485760 | tf_op jit(solution)/shard_map/pallas_call | solution.py:346
  21.6 1.4 all-to-all-done
  23.6 4.5 %shard_map.123 = (bf16[16,8,64,128]{3,2,1,0:T(8,128)(2,1)}, bf16[3,64,1024]{2,1,0:T(8,128)(2,1)}) custom-call(s32[1]{0:T(128)} %bitcast.3.me_ref, s32[16,128]{1,0:T(8,128)} %bitcast.22, bf16[64,64,128]{2,1,0:T(8,128)(2,1)} %get-tuple-element.25.packed_hbm, f32[64,1024]{1,0:T(8,128)} %self_hbm.1, f32[64,1024]{1,0:T(8,128)} %neigh_hbm.1), custom_call_target="tpu_custom_call" | custom-call | tf_op jit(solution)/shard_map/pallas_call | solution.py:366
  28.2 5.9 %all-to-all-start.1 = ((bf16[16,512,128]{2,1,0:T(8,128)(2,1)}), bf16[16,512,128]{2,1,0:T(8,128)(2,1)S(1)}, u32[]{:S(2)}, u32[]{:S(2)}) async-start(bf16[16,512,128]{2,1,0:T(8,128)(2,1)} %bitcast.20), calls=%async_computation.1 | async-start | bytes 4194304 | tf_op jit(solution)/shard_map/all_to_all | solution.py:384
  36.4 1.9 %shard_map.124 = (f32[8,64,128]{2,1,0:T(8,128)}, f32[64,128]{1,0:T(8,128)}, f32[64,128]{1,0:T(8,128)}, f32[64,128]{1,0:T(8,128)}, f32[64,128]{1,0:T(8,128)}, /*i...) custom-call(s32[2]{0:T(128)} %pad_add_fusion.place_ref, ...), custom_call_target="tpu_custom_call" | custom-call | bytes 1048576 | tf_op jit(solution)/shard_map/pallas_call | solution.py:387
  38.3 2.0 %collective-permute-start.1 = (f32[64,128]{1,0:T(8,128)}, f32[64,128]{1,0:T(8,128)S(1)}, u32[]{:S(2)}, u32[]{:S(2)}) collective-permute-start(f32[64,128]{1,0:T(8,128)} %get-tuple-element.29), channel_id=1, source_target_pairs={{0,2},{1,3},{2,4},{3,5},{4,6},{5,7},{6,8},{7,9},{8,10},{9,11},{10,... | collective-permute-start | bytes 98312 | tf_op jit(solution)/shard_map/ppermute | solution.py:333
  40.4 5.7 %collective-permute-start.3 = (f32[64,128]{1,0:T(8,128)}, f32[64,128]{1,0:T(8,128)S(1)}, u32[]{:S(2)}, u32[]{:S(2)}) collective-permute-start(f32[64,128]{1,0:T(8,128)} %get-tuple-element.31), channel_id=1, source_target_pairs={{0,4},{1,5},{2,6},{3,7},{4,8},{5,9},{6,10},{7,11},{8,12},{9,13},{1... | collective-permute-start | bytes 98312 | tf_op jit(solution)/shard_map/ppermute | solution.py:333
  46.1 3.4 %collective-permute-start.5 = (f32[64,128]{1,0:T(8,128)}, f32[64,128]{1,0:T(8,128)S(1)}, u32[]{:S(2)}, u32[]{:S(2)}) collective-permute-start(f32[64,128]{1,0:T(8,128)} %get-tuple-element.33), channel_id=1, source_target_pairs={{0,6},{1,7},{2,8},{3,9},{4,10},{5,11},{6,12},{7,13},{8,14},{9,15},... | collective-permute-start | bytes 98312 | tf_op jit(solution)/shard_map/ppermute | solution.py:333
  49.5 1.7 %collective-permute-start.6 = (f32[64,128]{1,0:T(8,128)}, f32[64,128]{1,0:T(8,128)S(1)}, u32[]{:S(2)}, u32[]{:S(2)}) collective-permute-start(f32[64,128]{1,0:T(8,128)} %get-tuple-element.34), channel_id=1, source_target_pairs={{0,10},{1,11},{2,12},{3,13},{4,14},{5,15},{6,0},{7,1},{8,2},{9,3},... | collective-permute-start | bytes 98312 | tf_op jit(solution)/shard_map/ppermute | solution.py:333
  51.2 2.6 %collective-permute-start.7 = (f32[64,128]{1,0:T(8,128)}, f32[64,128]{1,0:T(8,128)S(1)}, u32[]{:S(2)}, u32[]{:S(2)}) collective-permute-start(f32[64,128]{1,0:T(8,128)} %get-tuple-element.35), channel_id=1, source_target_pairs={{0,8},{1,9},{2,10},{3,11},{4,12},{5,13},{6,14},{7,15},{8,0},{9,1},... | collective-permute-start | bytes 98312 | tf_op jit(solution)/shard_map/ppermute | solution.py:333
  54.4 3.8 %collective-permute-done.6.rest_5_.rest_6_ = f32[64,128]{1,0:T(8,128)S(1)} collective-permute-done((f32[64,128]{1,0:T(8,128)}, f32[64,128]{1,0:T(8,128)S(1)}, u32[]{:S(2)}, u32[]{:S(2)}) %collective-permute-start.6) | collective-permute-done | bytes 32800 | tf_op jit(solution)/shard_map/ppermute | solution.py:333
  58.2 1.8 %collective-permute-done.7.rest_6_.rest_7_ = f32[64,128]{1,0:T(8,128)S(1)} collective-permute-done((f32[64,128]{1,0:T(8,128)}, f32[64,128]{1,0:T(8,128)S(1)}, u32[]{:S(2)}, u32[]{:S(2)}) %collective-permute-start.7) | collective-permute-done | bytes 32800 | tf_op jit(solution)/shard_map/ppermute | solution.py:333
  60.0 4.3 %all-to-all-done.1 = bf16[16,512,128]{2,1,0:T(8,128)(2,1)S(1)} async-done(((bf16[16,512,128]{2,1,0:T(8,128)(2,1)}), bf16[16,512,128]{2,1,0:T(8,128)(2,1)S(1)}, u32[]{:S(2)}, u32[]{:S(2)}) %all-to-all-start.1) | async-done | bytes 2097184 | tf_op jit(solution)/shard_map/all_to_all | solution.py:384
  65.4 2.7 %collective-permute-done.8.other_ref = bf16[64,64,128]{2,1,0:T(8,128)(2,1)S(1)} collective-permute-done((bf16[64,64,128]{2,1,0:T(8,128)(2,1)S(1)}, bf16[64,64,128]{2,1,0:T(8,128)(2,1)S(1)}, u32[]{:S(2)}, u32[]{:S(2)}) %collective-permute-start.8) | collective-permute-done | bytes 1048608 | tf_op jit(solution)/shard_map/ppermute | solution.py:406
  68.0 10.3 %shard_map.126.mean_ref = f32[8,64,128]{2,1,0:T(8,128)} custom-call(s32[1]{0:T(128)S(6)} %select_n.12.core_ref, s32[64]{0:T(128)S(1)} %copy-done.7, s32[15360]{0:T(1024)S(1)} %reshape.32.rest_7_.near_ref, bf16[64,64,128]{2,1,0:T(8,128)(2,1)S(1)} %shard_map.125.own_ref, bf16[64,64,128]{2,1,0:T(8,128)(2,1)S(1)} %collective-permute-done.8.other_ref), custom_call_target="tpu_custom_call" | custom-call | bytes 31457280 | tf_op jit(solution)/shard_map/pallas_call | solution.py:400
  78.3 8.1 %all-to-all-start.2 = ((f32[8,64,128]{2,1,0:T(8,128)}), f32[8,64,128]{2,1,0:T(8,128)S(1)}, u32[]{:S(2)}, u32[]{:S(2)}) async-start(f32[8,64,128]{2,1,0:T(8,128)} %shard_map.126.mean_ref), calls=%async_computation.2 | async-start | bytes 524288 | tf_op jit(solution)/shard_map/all_to_all | solution.py:420
  86.5 2.8 %copy-done = bf16[48,64,1024]{2,1,0:T(8,128)(2,1)S(1)} copy-done((bf16[48,64,1024]{2,1,0:T(8,128)(2,1)S(1)}, bf16[48,64,1024]{2,1,0:T(8,128)(2,1)}, u32[]{:S(2)}) %copy-start) | copy-done | bytes 6291480
  89.2 2.8 %shard_map.127 = (f32[64,1024]{1,0:T(8,128)S(1)}, bf16[16,64,1024]{2,1,0:T(8,128)(2,1)S(1)}) custom-call(s32[2]{0:T(128)S(1)} %copy-done.4, f32[1,1024]{1,0:T(1,128)S(1)} %bitcast.17, bf16[16,3,64,1024]{3,2,1,0:T(8,128)(2,1)S(1)} %bitcast.16, f32[64,128]{1,0:T(8,128)S(1)} %copy-done.3, f32[64,128]{1,0:T(8,128)S(1)} %collective-permute-done.1.rest_0_.rest_1_, ...), custom_call_target="tpu_custom_call" | custom-call | flops 402653184 | bytes 9437184 | tf_op jit(solution)/shard_map/pallas_call | solution.py:408
  92.1 3.5 %all-to-all-done.2.mean_ref = f32[8,64,128]{2,1,0:T(8,128)S(1)} async-done(((f32[8,64,128]{2,1,0:T(8,128)}), f32[8,64,128]{2,1,0:T(8,128)S(1)}, u32[]{:S(2)}, u32[]{:S(2)}) %all-to-all-start.2) | async-done | bytes 262176 | tf_op jit(solution)/shard_map/all_to_all | solution.py:420
  95.6 1.6 shard_map.128
  98.4 1.8 %collective-permute-start.12 = (bf16[64,1024]{1,0:T(8,128)(2,1)S(1)}, bf16[64,1024]{1,0:T(8,128)(2,1)S(1)}, u32[]{:S(2)}, u32[]{:S(2)}) collective-permute-start(bf16[64,1024]{1,0:T(8,128)(2,1)S(1)} %get-tuple-element.44.near_ref), channel_id=1, source_target_pairs={{0,12},{1,13},{2,14},{3,15},{4,0},{5,1},{6,2},{7,3},{8,4},{9,5},{1... | collective-permute-start | bytes 393224 | tf_op jit(solution)/shard_map/ppermute | solution.py:333
  100.2 3.2 %collective-permute-start.10 = (bf16[64,1024]{1,0:T(8,128)(2,1)S(1)}, bf16[64,1024]{1,0:T(8,128)(2,1)S(1)}, u32[]{:S(2)}, u32[]{:S(2)}) collective-permute-start(bf16[64,1024]{1,0:T(8,128)(2,1)S(1)} %get-tuple-element.44.near_ref), channel_id=1, source_target_pairs={{0,14},{1,15},{2,0},{3,1},{4,2},{5,3},{6,4},{7,5},{8,6},{9,7},{10,... | collective-permute-start | bytes 393224 | tf_op jit(solution)/shard_map/ppermute | solution.py:333
  104.2 2.7 %collective-permute-start.13 = (bf16[64,1024]{1,0:T(8,128)(2,1)S(1)}, bf16[64,1024]{1,0:T(8,128)(2,1)S(1)}, u32[]{:S(2)}, u32[]{:S(2)}) collective-permute-start(bf16[64,1024]{1,0:T(8,128)(2,1)S(1)} %collective-permute-done.11.rest_2_), channel_id=1, source_target_pairs={{0,2},{1,3},{2,4},{3,5},{4,6},{5,7},{6,8},{7,9},{8,10},{9,11},{10,... | collective-permute-start | bytes 393224 | tf_op jit(solution)/shard_map/ppermute | solution.py:333
  106.8 1.3 collective-permute-done.12.rest_3_
  108.7 3.5 %collective-permute-start.15 = (bf16[32,1024]{1,0:T(8,128)(2,1)S(1)}, bf16[32,1024]{1,0:T(8,128)(2,1)S(1)}, u32[]{:S(2)}, u32[]{:S(2)}) collective-permute-start(bf16[32,1024]{1,0:T(8,128)(2,1)S(1)} %slice.24), channel_id=1, source_target_pairs={{0,4},{1,5},{2,6},{3,7},{4,8},{5,9},{6,10},{7,11},{8,12},{9,13},{1... | collective-permute-start | bytes 196616 | tf_op jit(solution)/shard_map/ppermute | solution.py:333
  114.8 3.9 %collective-permute-done.16.rest_7_ = bf16[32,1024]{1,0:T(8,128)(2,1)S(1)} collective-permute-done((bf16[32,1024]{1,0:T(8,128)(2,1)S(1)}, bf16[32,1024]{1,0:T(8,128)(2,1)S(1)}, u32[]{:S(2)}, u32[]{:S(2)}) %collective-permute-start.16) | collective-permute-done | bytes 65568 | tf_op jit(solution)/shard_map/ppermute | solution.py:333
  118.7 1.3 shard_map.130
  120.1 1.9 %collective-permute-done.17.right_ref = f32[16,8,1024]{2,1,0:T(8,128)S(1)} collective-permute-done((f32[16,8,1024]{2,1,0:T(8,128)S(1)}, f32[16,8,1024]{2,1,0:T(8,128)S(1)}, u32[]{:S(2)}, u32[]{:S(2)}) %collective-permute-start.17) | collective-permute-done | bytes 524320 | tf_op jit(solution)/shard_map/ppermute | solution.py:443
  122.0 14.9 %all_to_all.25.in_ref = f32[16,8,1024]{2,1,0:T(8,128)S(1)} all-to-all(f32[16,8,1024]{2,1,0:T(8,128)S(1)} %shard_map.131), channel_id=1, replica_groups=mesh['dom'=16,'feat'=16] {'dom'}, dimensions={0} | all-to-all | bytes 1048576 | tf_op jit(solution)/shard_map/all_to_all | solution.py:445
  137.0 14.0 %all_to_all.26 = f32[16,8,1024]{2,1,0:T(8,128)S(1)} all-to-all(f32[16,8,1024]{2,1,0:T(8,128)S(1)} %shard_map.132), channel_id=1, replica_groups=mesh['dom'=16,'feat'=16] {'dom'}, dimensions={0} | all-to-all | bytes 1048576 | tf_op jit(solution)/shard_map/all_to_all | solution.py:447
  (57 shorter events, 10.9 us)
Async XLA Ops:
  8.5 14.5 %all-to-all-start = ((s32[16,1,128]{2,1,0:T(1,128)}), s32[16,1,128]{2,1,0:T(1,128)S(1)}, u32[]{:S(2)}, u32[]{:S(2)}) async-start(s32[16,1,128]{2,1,0:T(1,128)} %shard_map.121), calls=%async_computation | async-start | bytes 16384 | tf_op jit(solution)/shard_map/all_to_all | solution.py:342
  15.6 70.9 %all-gather.3.cloned.1.call-start = ((), (), s32[]{:S(2)}) async-start(), calls=%async_computation.5 | async-start | bytes 6684672 | tf_op jit(solution)/shard_map/all_gather | solution.py:383
  28.1 6.0 %copy-start.11 = (f32[8,64,128]{2,1,0:T(8,128)S(1)}, f32[8,64,128]{2,1,0:T(8,128)}, u32[]{:S(2)}) copy-start(f32[8,64,128]{2,1,0:T(8,128)} %get-tuple-element.28) | copy-start | bytes 786436
  28.1 25.6 %copy-start.9 = (s32[15,1024]{1,0:T(8,128)S(1)}, s32[15,1024]{1,0:T(8,128)}, u32[]{:S(2)}) copy-start(s32[15,1024]{1,0:T(8,128)} %param.12) | copy-start | bytes 184324
  28.1 36.2 %copy-start.6 = (s32[64,1]{0,1:T(1,128)S(1)}, s32[64,1]{0,1:T(1,128)}, u32[]{:S(2)}) copy-start(s32[64,1]{0,1:T(1,128)} %param.13) | copy-start | bytes 772
  28.2 36.2 %all-to-all-start.1 = ((bf16[16,512,128]{2,1,0:T(8,128)(2,1)}), bf16[16,512,128]{2,1,0:T(8,128)(2,1)S(1)}, u32[]{:S(2)}, u32[]{:S(2)}) async-start(bf16[16,512,128]{2,1,0:T(8,128)(2,1)} %bitcast.20), calls=%async_computation.1 | async-start | bytes 4194304 | tf_op jit(solution)/shard_map/all_to_all | solution.py:384
  34.1 1.6 %collective-permute-start = (f32[8,64,128]{2,1,0:T(8,128)S(1)}, f32[8,64,128]{2,1,0:T(8,128)S(1)}, u32[]{:S(2)}, u32[]{:S(2)}) collective-permute-start(f32[8,64,128]{2,1,0:T(8,128)S(1)} %copy-done.11), channel_id=1, source_target_pairs={{0,1},{1,0},{2,3},{3,2},{4,5},{5,4},{6,7},{7,6},{8,9},{9,8},{10,11... | collective-permute-start | bytes 786440 | tf_op jit(solution)/shard_map/ppermute | solution.py:392
  38.3 11.2 %collective-permute-start.1 = (f32[64,128]{1,0:T(8,128)}, f32[64,128]{1,0:T(8,128)S(1)}, u32[]{:S(2)}, u32[]{:S(2)}) collective-permute-start(f32[64,128]{1,0:T(8,128)} %get-tuple-element.29), channel_id=1, source_target_pairs={{0,2},{1,3},{2,4},{3,5},{4,6},{5,7},{6,8},{7,9},{8,10},{9,11},{10,... | collective-permute-start | bytes 98312 | tf_op jit(solution)/shard_map/ppermute | solution.py:333
  40.3 10.8 %collective-permute-start.2 = (f32[64,128]{1,0:T(8,128)}, f32[64,128]{1,0:T(8,128)S(1)}, u32[]{:S(2)}, u32[]{:S(2)}) collective-permute-start(f32[64,128]{1,0:T(8,128)} %get-tuple-element.30), channel_id=1, source_target_pairs={{0,14},{1,15},{2,0},{3,1},{4,2},{5,3},{6,4},{7,5},{8,6},{9,7},{10,... | collective-permute-start | bytes 98312 | tf_op jit(solution)/shard_map/ppermute | solution.py:333
  40.4 13.9 %collective-permute-start.3 = (f32[64,128]{1,0:T(8,128)}, f32[64,128]{1,0:T(8,128)S(1)}, u32[]{:S(2)}, u32[]{:S(2)}) collective-permute-start(f32[64,128]{1,0:T(8,128)} %get-tuple-element.31), channel_id=1, source_target_pairs={{0,4},{1,5},{2,6},{3,7},{4,8},{5,9},{6,10},{7,11},{8,12},{9,13},{1... | collective-permute-start | bytes 98312 | tf_op jit(solution)/shard_map/ppermute | solution.py:333
  46.1 8.2 %collective-permute-start.4 = (f32[64,128]{1,0:T(8,128)}, f32[64,128]{1,0:T(8,128)S(1)}, u32[]{:S(2)}, u32[]{:S(2)}) collective-permute-start(f32[64,128]{1,0:T(8,128)} %get-tuple-element.32), channel_id=1, source_target_pairs={{0,12},{1,13},{2,14},{3,15},{4,0},{5,1},{6,2},{7,3},{8,4},{9,5},{1... | collective-permute-start | bytes 98312 | tf_op jit(solution)/shard_map/ppermute | solution.py:333
  46.1 8.3 %collective-permute-start.5 = (f32[64,128]{1,0:T(8,128)}, f32[64,128]{1,0:T(8,128)S(1)}, u32[]{:S(2)}, u32[]{:S(2)}) collective-permute-start(f32[64,128]{1,0:T(8,128)} %get-tuple-element.33), channel_id=1, source_target_pairs={{0,6},{1,7},{2,8},{3,9},{4,10},{5,11},{6,12},{7,13},{8,14},{9,15},... | collective-permute-start | bytes 98312 | tf_op jit(solution)/shard_map/ppermute | solution.py:333
  49.5 8.7 %collective-permute-start.6 = (f32[64,128]{1,0:T(8,128)}, f32[64,128]{1,0:T(8,128)S(1)}, u32[]{:S(2)}, u32[]{:S(2)}) collective-permute-start(f32[64,128]{1,0:T(8,128)} %get-tuple-element.34), channel_id=1, source_target_pairs={{0,10},{1,11},{2,12},{3,13},{4,14},{5,15},{6,0},{7,1},{8,2},{9,3},... | collective-permute-start | bytes 98312 | tf_op jit(solution)/shard_map/ppermute | solution.py:333
  51.2 8.8 %collective-permute-start.7 = (f32[64,128]{1,0:T(8,128)}, f32[64,128]{1,0:T(8,128)S(1)}, u32[]{:S(2)}, u32[]{:S(2)}) collective-permute-start(f32[64,128]{1,0:T(8,128)} %get-tuple-element.35), channel_id=1, source_target_pairs={{0,8},{1,9},{2,10},{3,11},{4,12},{5,13},{6,14},{7,15},{8,0},{9,1},... | collective-permute-start | bytes 98312 | tf_op jit(solution)/shard_map/ppermute | solution.py:333
  54.0 14.0 %copy-start.7 = (s32[64]{0:T(128)S(1)}, s32[64]{0:T(128)}, u32[]{:S(2)}) copy-start(s32[64]{0:T(128)} %count_ref.1) | copy-start | bytes 772
  65.2 21.2 %copy-start.3 = (f32[64,128]{1,0:T(8,128)S(1)}, f32[64,128]{1,0:T(8,128)}, u32[]{:S(2)}) copy-start(f32[64,128]{1,0:T(8,128)} %get-tuple-element.37.rest_0_) | copy-start | bytes 98308
  65.2 21.2 %copy-start.4 = (s32[2]{0:T(128)S(1)}, s32[2]{0:T(128)}, u32[]{:S(2)}) copy-start(s32[2]{0:T(128)} %pad_add_fusion.place_ref) | copy-start | bytes 28
  65.2 21.2 %copy-start.5 = (f32[1024]{0:T(1024)S(1)}, f32[1024]{0:T(1024)}, u32[]{:S(2)}) copy-start(f32[1024]{0:T(1024)} %param.18) | copy-start | bytes 12292
  65.3 2.8 %collective-permute-start.8 = (bf16[64,64,128]{2,1,0:T(8,128)(2,1)S(1)}, bf16[64,64,128]{2,1,0:T(8,128)(2,1)S(1)}, u32[]{:S(2)}, u32[]{:S(2)}) collective-permute-start(bf16[64,64,128]{2,1,0:T(8,128)(2,1)S(1)} %shard_map.125.own_ref), channel_id=1, source_target_pairs={{0,1},{1,0},{2,3},{3,2},{4,5},{5,4},{6,7},{7,6},{8,9},{9,8},{10,11... | collective-permute-start | bytes 3145736 | tf_op jit(solution)/shard_map/ppermute | solution.py:406
  78.3 17.2 %all-to-all-start.2 = ((f32[8,64,128]{2,1,0:T(8,128)}), f32[8,64,128]{2,1,0:T(8,128)S(1)}, u32[]{:S(2)}, u32[]{:S(2)}) async-start(f32[8,64,128]{2,1,0:T(8,128)} %shard_map.126.mean_ref), calls=%async_computation.2 | async-start | bytes 524288 | tf_op jit(solution)/shard_map/all_to_all | solution.py:420
  86.5 2.8 %copy-start = (bf16[48,64,1024]{2,1,0:T(8,128)(2,1)S(1)}, bf16[48,64,1024]{2,1,0:T(8,128)(2,1)}, u32[]{:S(2)}) copy-start(bf16[48,64,1024]{2,1,0:T(8,128)(2,1)} %all-gather.3.cloned.1.call-done) | copy-start | bytes 18874372
  89.2 6.3 %copy-start.2 = (bf16[64,1024]{1,0:T(8,128)(2,1)S(1)}, bf16[64,1024]{1,0:T(8,128)(2,1)}, u32[]{:S(2)}) copy-start(bf16[64,1024]{1,0:T(8,128)(2,1)} %cotangent_ref.1) | copy-start | bytes 393220
  92.1 20.6 %copy-start.1 = (f32[8,64,128]{2,1,0:T(8,128)S(1)}, f32[8,64,128]{2,1,0:T(8,128)}, u32[]{:S(2)}) copy-start(f32[8,64,128]{2,1,0:T(8,128)} %get-tuple-element.41.self_ref) | copy-start | bytes 786436
  97.1 7.0 %collective-permute-start.11 = (bf16[64,1024]{1,0:T(8,128)(2,1)S(1)}, bf16[64,1024]{1,0:T(8,128)(2,1)S(1)}, u32[]{:S(2)}, u32[]{:S(2)}) collective-permute-start(bf16[64,1024]{1,0:T(8,128)(2,1)S(1)} %get-tuple-element.44.near_ref), channel_id=1, source_target_pairs={{0,4},{1,5},{2,6},{3,7},{4,8},{5,9},{6,10},{7,11},{8,12},{9,13},{1... | collective-permute-start | bytes 393224 | tf_op jit(solution)/shard_map/ppermute | solution.py:333
  98.4 9.7 %collective-permute-start.12 = (bf16[64,1024]{1,0:T(8,128)(2,1)S(1)}, bf16[64,1024]{1,0:T(8,128)(2,1)S(1)}, u32[]{:S(2)}, u32[]{:S(2)}) collective-permute-start(bf16[64,1024]{1,0:T(8,128)(2,1)S(1)} %get-tuple-element.44.near_ref), channel_id=1, source_target_pairs={{0,12},{1,13},{2,14},{3,15},{4,0},{5,1},{6,2},{7,3},{8,4},{9,5},{1... | collective-permute-start | bytes 393224 | tf_op jit(solution)/shard_map/ppermute | solution.py:333
  100.2 12.0 %collective-permute-start.10 = (bf16[64,1024]{1,0:T(8,128)(2,1)S(1)}, bf16[64,1024]{1,0:T(8,128)(2,1)S(1)}, u32[]{:S(2)}, u32[]{:S(2)}) collective-permute-start(bf16[64,1024]{1,0:T(8,128)(2,1)S(1)} %get-tuple-element.44.near_ref), channel_id=1, source_target_pairs={{0,14},{1,15},{2,0},{3,1},{4,2},{5,3},{6,4},{7,5},{8,6},{9,7},{10,... | collective-permute-start | bytes 393224 | tf_op jit(solution)/shard_map/ppermute | solution.py:333
  103.4 10.4 %collective-permute-start.9 = (bf16[64,1024]{1,0:T(8,128)(2,1)S(1)}, bf16[64,1024]{1,0:T(8,128)(2,1)S(1)}, u32[]{:S(2)}, u32[]{:S(2)}) collective-permute-start(bf16[64,1024]{1,0:T(8,128)(2,1)S(1)} %get-tuple-element.44.near_ref), channel_id=1, source_target_pairs={{0,2},{1,3},{2,4},{3,5},{4,6},{5,7},{6,8},{7,9},{8,10},{9,11},{10,... | collective-permute-start | bytes 393224 | tf_op jit(solution)/shard_map/ppermute | solution.py:333
  104.2 14.5 %collective-permute-start.13 = (bf16[64,1024]{1,0:T(8,128)(2,1)S(1)}, bf16[64,1024]{1,0:T(8,128)(2,1)S(1)}, u32[]{:S(2)}, u32[]{:S(2)}) collective-permute-start(bf16[64,1024]{1,0:T(8,128)(2,1)S(1)} %collective-permute-done.11.rest_2_), channel_id=1, source_target_pairs={{0,2},{1,3},{2,4},{3,5},{4,6},{5,7},{6,8},{7,9},{8,10},{9,11},{10,... | collective-permute-start | bytes 393224 | tf_op jit(solution)/shard_map/ppermute | solution.py:333
  108.1 10.6 %collective-permute-start.14 = (bf16[64,1024]{1,0:T(8,128)(2,1)S(1)}, bf16[64,1024]{1,0:T(8,128)(2,1)S(1)}, u32[]{:S(2)}, u32[]{:S(2)}) collective-permute-start(bf16[64,1024]{1,0:T(8,128)(2,1)S(1)} %collective-permute-done.12.rest_3_), channel_id=1, source_target_pairs={{0,14},{1,15},{2,0},{3,1},{4,2},{5,3},{6,4},{7,5},{8,6},{9,7},{10,... | collective-permute-start | bytes 393224 | tf_op jit(solution)/shard_map/ppermute | solution.py:333
  108.7 6.1 %collective-permute-start.15 = (bf16[32,1024]{1,0:T(8,128)(2,1)S(1)}, bf16[32,1024]{1,0:T(8,128)(2,1)S(1)}, u32[]{:S(2)}, u32[]{:S(2)}) collective-permute-start(bf16[32,1024]{1,0:T(8,128)(2,1)S(1)} %slice.24), channel_id=1, source_target_pairs={{0,4},{1,5},{2,6},{3,7},{4,8},{5,9},{6,10},{7,11},{8,12},{9,13},{1... | collective-permute-start | bytes 196616 | tf_op jit(solution)/shard_map/ppermute | solution.py:333
  112.2 6.5 %collective-permute-start.16 = (bf16[32,1024]{1,0:T(8,128)(2,1)S(1)}, bf16[32,1024]{1,0:T(8,128)(2,1)S(1)}, u32[]{:S(2)}, u32[]{:S(2)}) collective-permute-start(bf16[32,1024]{1,0:T(8,128)(2,1)S(1)} %slice.25), channel_id=1, source_target_pairs={{0,12},{1,13},{2,14},{3,15},{4,0},{5,1},{6,2},{7,3},{8,4},{9,5},{1... | collective-permute-start | bytes 196616 | tf_op jit(solution)/shard_map/ppermute | solution.py:333
  120.0 2.0 %collective-permute-start.17 = (f32[16,8,1024]{2,1,0:T(8,128)S(1)}, f32[16,8,1024]{2,1,0:T(8,128)S(1)}, u32[]{:S(2)}, u32[]{:S(2)}) collective-permute-start(f32[16,8,1024]{2,1,0:T(8,128)S(1)} %get-tuple-element.46), channel_id=1, source_target_pairs={{0,1},{1,0},{2,3},{3,2},{4,5},{5,4},{6,7},{7,6},{8,9},{9,8},{10,11... | collective-permute-start | bytes 1572872 | tf_op jit(solution)/shard_map/ppermute | solution.py:443
  (2 other events, 1.3 us)
Sparse Core Ops, SparseCore 0:
  28.2 51.9 all-gather.2

commit v4 on v3

--- a/solution.py
+++ b/solution.py
@@ -67,7 +67,7 @@
     outs = []
     for part in range(parts):
         fetch(part).wait()
-        lax.fori_loop(part * pairs, (part + 1) * pairs, turn, 0, unroll=2)
+        lax.fori_loop(part * pairs, (part + 1) * pairs, turn, 0, unroll=pairs)
         window = pl.ds(2 * pairs * part, 2 * pairs)
         outs.append(pltpu.make_async_copy(packed.at[window], packed_ref.at[window], out_sems.at[part]))
         outs[-1].start()
@@ -86,9 +86,11 @@
 
 
 def pack_kernel(
-    me_ref, request_ref, packed_hbm, self_hbm, neigh_hbm, out_hbm, weight_ref,
-    wanted, wanted_smem, packed_ref, both, out_ref, sem, in_sem, out_sems, weight_sems,
+    request_hbm, packed_hbm, self_hbm, neigh_hbm, out_hbm, weight_hbm,
+    wanted, packed_ref, both, weight_ref, out_ref, sem, in_sem, out_sems, weight_sems,
 ):
+    slots = pltpu.make_async_copy(request_hbm, wanted, sem)
+    slots.start()
     fetch = pltpu.make_async_copy(packed_hbm, packed_ref, in_sem)
     fetch.start()
     weights = [
@@ -97,34 +99,19 @@
     ]
     for copy in weights:
         copy.start()
-    me = me_ref[0]
-    request = request_ref[...]
-    parts = request.shape[0]
-    lane = lane_of(request.shape)
-    mine = jnp.logical_and(request == me, lane < HALF)
-    below = lax.broadcasted_iota(jnp.int32, (BLOCK, BLOCK), 0) <= lane_of((BLOCK, BLOCK))
-    rank = dot(mine.astype(BF16), below.astype(BF16))
-    block = pltpu.roll(request, HALF, 1).astype(F32)
-    result = jnp.zeros(request.shape, F32)
-    for slot in range(SLOTS):
-        hit = jnp.logical_and(mine, rank == slot + 1.0)
-        chosen = jnp.sum(jnp.where(hit, block, 0.0), axis=1, keepdims=True)
-        result = jnp.where(lane == slot, chosen, result)
-    wanted[...] = result.astype(jnp.int32)
-    copy = pltpu.make_async_copy(wanted, wanted_smem, sem)
-    copy.start()
     for held in weights:
         held.wait()
     high, low = split(both[0])
     weight_ref[0] = high
     weight_ref[1] = low
     weight_ref[2] = both[1].astype(BF16)
-    copy.wait()
+    copies = [pltpu.make_async_copy(weight_ref, weight_hbm, weight_sems.at[2])]
+    copies[0].start()
+    slots.wait()
     fetch.wait()
-    copies = []
-    for part in range(parts):
+    for part in range(out_ref.shape[0]):
         for slot in range(SLOTS):
-            out_ref[part, slot] = packed_ref[wanted_smem[part, slot]]
+            out_ref[part, slot] = packed_ref[wanted[part, 0, slot]]
         copies.append(pltpu.make_async_copy(out_ref.at[part], out_hbm.at[part], out_sems.at[part]))
         copies[-1].start()
     for copy in copies:
@@ -143,7 +130,7 @@
         out_ref[entry] = arrived_ref[owner * SLOTS + rank]
         return carry
 
-    lax.fori_loop(0, out_ref.shape[0], place, 0, unroll=4)
+    lax.fori_loop(0, out_ref.shape[0], place, 0, unroll=8)
 
 
 def gather_kernel(core_ref, count_ref, near_ref, own_ref, other_ref, out_ref, front):
@@ -163,22 +150,22 @@
         front[pl.ds(start + HALF, HALF), :] = jnp.where(row < count - HALF, lower, 0.0)
         return carry
 
-    lax.fori_loop(0, own_ref.shape[0], place, 0, unroll=4)
+    lax.fori_loop(0, own_ref.shape[0], place, 0, unroll=8)
 
     def average(step, carry):
-        group, part = lax.div(step, 4), lax.rem(step, 4)
-        base = ((2 * group + core) * 64 + part * 16) * FAN
-        for seed in range(16):
+        group, part = lax.div(step, 2), lax.rem(step, 2)
+        base = ((2 * group + core) * 64 + part * 32) * FAN
+        for seed in range(32):
             terms = [front[pl.ds(near_ref[base + seed * FAN + k], 1), :] for k in range(FAN)]
             while len(terms) > 1:
                 terms = [
                     terms[i] + terms[i + 1] if i + 1 < len(terms) else terms[i]
                     for i in range(0, len(terms), 2)
                 ]
-            out_ref[group, pl.ds(part * 16 + seed, 1), :] = terms[0] * (1.0 / FAN)
+            out_ref[group, pl.ds(part * 32 + seed, 1), :] = terms[0] * (1.0 / FAN)
         return carry
 
-    lax.fori_loop(0, 32, average, 0)
+    lax.fori_loop(0, 16, average, 0)
 
 
 def join_kernel(place_ref, own_ref, other_ref, *rest):
@@ -196,9 +183,23 @@
 
 
 def open_kernel(owner_ref, block_ref, request_ref):
-    request = jnp.concatenate([owner_ref[...], block_ref[...]], axis=1)
-    for part in range(request_ref.shape[0]):
-        request_ref[part] = request
+    parts = request_ref.shape[0]
+    wide = (parts, owner_ref.shape[1])
+    owner = jnp.broadcast_to(owner_ref[...], wide)
+    block = jnp.broadcast_to(block_ref[...], wide).astype(F32)
+    mine = owner == lax.broadcasted_iota(jnp.int32, wide, 0)
+    square = (wide[1], wide[1])
+    below = lax.broadcasted_iota(jnp.int32, square, 0) <= lane_of(square)
+    rank = dot(mine.astype(BF16), below.astype(BF16))
+    lane = lane_of((parts, BLOCK))
+    result = jnp.zeros((parts, BLOCK), F32)
+    for slot in range(SLOTS):
+        hit = jnp.logical_and(mine, rank == slot + 1.0)
+        chosen = jnp.sum(jnp.where(hit, block, 0.0), axis=1, keepdims=True)
+        result = jnp.where(lane == slot, chosen, result)
+    result = result.astype(jnp.int32)
+    for part in range(parts):
+        request_ref[part] = result[part : part + 1]
 
 
 def three(left, right_high, right_low):
@@ -322,7 +323,6 @@
     ring = n_feat // 2
     across = [(i, i ^ 1) for i in range(n_feat)]
     columns = [[2 * z + c for z in range(ring)] for c in range(2)]
-    dom = lax.axis_index("dom").astype(jnp.int32).reshape(1)
     feat = lax.axis_index("feat").astype(jnp.int32).reshape(1)
     core = feat % 2
     place = jnp.concatenate([core, feat // 2])
@@ -335,13 +335,10 @@
     owner_ids = owners[:, 0]
     shape = jax.ShapeDtypeStruct
 
-    entries_here = owner_ids.shape[0]
     request = call(
-        open_kernel, shape((n_dom, 1, 2 * entries_here), jnp.int32), [VMEM, VMEM], limit=60
+        open_kernel, shape((n_dom, 1, BLOCK), jnp.int32), [VMEM, VMEM], limit=60
     )(owner_ids[None, :], blocks[None, :])
-    requests = lax.all_to_all(request, "dom", split_axis=0, concat_axis=0, tiled=True).reshape(
-        n_dom, 2 * entries_here
-    )
+    requests = lax.all_to_all(request, "dom", split_axis=0, concat_axis=0, tiled=True)
     near = jnp.transpose(neighbours).reshape(-1)
     packed, kept, given = call(
         prepare_kernel,
@@ -366,20 +363,20 @@
     outgoing, weight = call(
         pack_kernel,
         (shape((n_dom, SLOTS, HALF, BLOCK), BF16), shape((3, 64, hidden_width), BF16)),
-        [SMEM, VMEM, ANY, ANY, ANY],
+        [ANY] * 4,
         [
-            pltpu.VMEM((n_dom, BLOCK), jnp.int32),
-            pltpu.SMEM((n_dom, BLOCK), jnp.int32),
+            pltpu.SMEM((n_dom, 1, BLOCK), jnp.int32),
             pltpu.VMEM(packed.shape, BF16),
             pltpu.VMEM((2, 64, hidden_width), F32),
+            pltpu.VMEM((3, 64, hidden_width), BF16),
             pltpu.VMEM((n_dom, SLOTS, HALF, BLOCK), BF16),
             pltpu.SemaphoreType.DMA,
             pltpu.SemaphoreType.DMA,
             pltpu.SemaphoreType.DMA((n_dom,)),
-            pltpu.SemaphoreType.DMA((2,)),
+            pltpu.SemaphoreType.DMA((3,)),
         ],
-        limit=59, outs=(ANY, VMEM),
-    )(dom, requests, packed, w_self, w_neigh)
+        limit=59, outs=(ANY, ANY),
+    )(requests, packed, w_self, w_neigh)
     weights = lax.all_gather(weight, "feat", axis=0, tiled=False)
     arrived = lax.all_to_all(
         outgoing.reshape(n_dom, SLOTS * HALF, BLOCK), "dom", split_axis=0, concat_axis=0, tiled=True

time: 159 us -> 156 us (0.981)
  Pallas kernels: 31.8 us -> 28.9 us
  transfers between devices with their start and end apart: 22 -> 22, of which waited for: 12 -> 12; matrix products, arithmetic and copies ran while one was open for 1% -> 1% of each run, Pallas kernels for 15% -> 14%
where the time goes in v4:
time: 156 us
  starting transfers between devices  49.3 us (32%)
  Pallas kernels  28.9 us (19%)
  blocking collectives  28.9 us (19%)
  waiting for transfers between devices  28.2 us (18%)
  between operations  14.3 us (9%)
  local copies, waits for them, and re-layouts  5.51 us (4%)
    ppermute x15, starting transfers between devices, climb(): return lax.ppermute(value, 'feat', pairs)  28.9 us
    all_to_all x1, blocking collectives, body(): lax.all_to_all(partial, 'dom', split_axis=0, concat_axis=0, tiled=True)  14.9 us
    all_to_all x1, blocking collectives, body(): lax.all_to_all(total, 'dom', split_axis=0, concat_axis=0, tiled=True)  14 us
    ppermute x15, waiting for transfers between devices, climb(): return lax.ppermute(value, 'feat', pairs)  12.5 us
    pallas_call x1, Pallas kernels, body(): call(gather_kernel, shape((ring, 64, BLOCK), F32), [SMEM, SMEM, SMEM, VME...  9.55 us
    all_to_all x1, starting transfers between devices, body(): lax.all_to_all(mean, 'feat', split_axis=0, concat_axis=0, tiled=True, axi...  8.01 us
    all_to_all x1, starting transfers between devices, body(): lax.all_to_all(request, 'dom', split_axis=0, concat_axis=0, tiled=True)  7.03 us
    pallas_call x1, Pallas kernels, body(): call(prepare_kernel, (shape((feature_table.shape[1] // BLOCK, HALF, BLOCK...  5.06 us
  transfers between devices with their start and end apart: 22, of which 12 were waited for; matrix products, arithmetic and copies ran while one was open for 1% of the time, Pallas kernels for 14%

profile of v4, /device:TPU:64, one launch (start us, length us, event | category | flops | bytes accessed | tf_op | source)
XLA Modules:
  0.0 155.7 jit_solution(10282910929046953110)
XLA Ops:
  7.2 1.5 shard_map.121
  8.7 7.0 %all-to-all-start = ((s32[16,1,128]{2,1,0:T(1,128)}), s32[16,1,128]{2,1,0:T(1,128)S(1)}, u32[]{:S(2)}, u32[]{:S(2)}) async-start(s32[16,1,128]{2,1,0:T(1,128)} %shard_map.121), calls=%async_computation | async-start | bytes 16384 | tf_op jit(solution)/shard_map/all_to_all | solution.py:341
  15.8 5.1 %shard_map.122 = (bf16[64,64,128]{2,1,0:T(8,128)(2,1)}, f32[8,64,128]{2,1,0:T(8,128)}, f32[8,64,128]{2,1,0:T(8,128)}) custom-call(s32[1]{0:T(128)S(6)} %select_n.12.core_ref, s32[1024]{0:T(1024)} %seed_hbm.1, f32[64,8192]{1,0:T(8,128)} %table_hbm.1), custom_call_target="tpu_custom_call" | custom-call | bytes 10485760 | tf_op jit(solution)/shard_map/pallas_call | solution.py:343
  20.8 2.4 %all-to-all-done.request_hbm = s32[16,1,128]{2,1,0:T(1,128)S(1)} async-done(((s32[16,1,128]{2,1,0:T(1,128)}), s32[16,1,128]{2,1,0:T(1,128)S(1)}, u32[]{:S(2)}, u32[]{:S(2)}) %all-to-all-start) | async-done | bytes 8224 | tf_op jit(solution)/shard_map/all_to_all | solution.py:341
  23.8 3.1 %shard_map.123 = (bf16[16,8,64,128]{3,2,1,0:T(8,128)(2,1)}, bf16[3,64,1024]{2,1,0:T(8,128)(2,1)}) custom-call(s32[16,1,128]{2,1,0:T(1,128)} %copy-done.10, bf16[64,64,128]{2,1,0:T(8,128)(2,1)} %get-tuple-element.25.packed_hbm, f32[64,1024]{1,0:T(8,128)} %self_hbm.1, f32[64,1024]{1,0:T(8,128)} %neigh_hbm.1), custom_call_target="tpu_custom_call" | custom-call | tf_op jit(solution)/shard_map/pallas_call | solution.py:363
  26.9 5.0 %all-to-all-start.1 = ((bf16[16,512,128]{2,1,0:T(8,128)(2,1)}), bf16[16,512,128]{2,1,0:T(8,128)(2,1)S(1)}, u32[]{:S(2)}, u32[]{:S(2)}) async-start(bf16[16,512,128]{2,1,0:T(8,128)(2,1)} %bitcast.18), calls=%async_computation.1 | async-start | bytes 4194304 | tf_op jit(solution)/shard_map/all_to_all | solution.py:381
  34.3 1.9 %shard_map.124 = (f32[8,64,128]{2,1,0:T(8,128)}, f32[64,128]{1,0:T(8,128)}, f32[64,128]{1,0:T(8,128)}, f32[64,128]{1,0:T(8,128)}, f32[64,128]{1,0:T(8,128)}, /*i...) custom-call(s32[2]{0:T(128)} %pad_add_fusion.place_ref, ...), custom_call_target="tpu_custom_call" | custom-call | bytes 1048576 | tf_op jit(solution)/shard_map/pallas_call | solution.py:384
  36.2 2.0 %collective-permute-start.1 = (f32[64,128]{1,0:T(8,128)}, f32[64,128]{1,0:T(8,128)S(1)}, u32[]{:S(2)}, u32[]{:S(2)}) collective-permute-start(f32[64,128]{1,0:T(8,128)} %get-tuple-element.29), channel_id=1, source_target_pairs={{0,2},{1,3},{2,4},{3,5},{4,6},{5,7},{6,8},{7,9},{8,10},{9,11},{10,... | collective-permute-start | bytes 98312 | tf_op jit(solution)/shard_map/ppermute | solution.py:333
  38.3 5.7 %collective-permute-start.3 = (f32[64,128]{1,0:T(8,128)}, f32[64,128]{1,0:T(8,128)S(1)}, u32[]{:S(2)}, u32[]{:S(2)}) collective-permute-start(f32[64,128]{1,0:T(8,128)} %get-tuple-element.31), channel_id=1, source_target_pairs={{0,4},{1,5},{2,6},{3,7},{4,8},{5,9},{6,10},{7,11},{8,12},{9,13},{1... | collective-permute-start | bytes 98312 | tf_op jit(solution)/shard_map/ppermute | solution.py:333
  44.0 3.4 %collective-permute-start.5 = (f32[64,128]{1,0:T(8,128)}, f32[64,128]{1,0:T(8,128)S(1)}, u32[]{:S(2)}, u32[]{:S(2)}) collective-permute-start(f32[64,128]{1,0:T(8,128)} %get-tuple-element.33), channel_id=1, source_target_pairs={{0,6},{1,7},{2,8},{3,9},{4,10},{5,11},{6,12},{7,13},{8,14},{9,15},... | collective-permute-start | bytes 98312 | tf_op jit(solution)/shard_map/ppermute | solution.py:333
  47.4 1.7 %collective-permute-start.6 = (f32[64,128]{1,0:T(8,128)}, f32[64,128]{1,0:T(8,128)S(1)}, u32[]{:S(2)}, u32[]{:S(2)}) collective-permute-start(f32[64,128]{1,0:T(8,128)} %get-tuple-element.34), channel_id=1, source_target_pairs={{0,10},{1,11},{2,12},{3,13},{4,14},{5,15},{6,0},{7,1},{8,2},{9,3},... | collective-permute-start | bytes 98312 | tf_op jit(solution)/shard_map/ppermute | solution.py:333
  49.0 2.6 %collective-permute-start.7 = (f32[64,128]{1,0:T(8,128)}, f32[64,128]{1,0:T(8,128)S(1)}, u32[]{:S(2)}, u32[]{:S(2)}) collective-permute-start(f32[64,128]{1,0:T(8,128)} %get-tuple-element.35), channel_id=1, source_target_pairs={{0,8},{1,9},{2,10},{3,11},{4,12},{5,13},{6,14},{7,15},{8,0},{9,1},... | collective-permute-start | bytes 98312 | tf_op jit(solution)/shard_map/ppermute | solution.py:333
  52.3 3.8 %collective-permute-done.6.rest_5_.rest_6_ = f32[64,128]{1,0:T(8,128)S(1)} collective-permute-done((f32[64,128]{1,0:T(8,128)}, f32[64,128]{1,0:T(8,128)S(1)}, u32[]{:S(2)}, u32[]{:S(2)}) %collective-permute-start.6) | collective-permute-done | bytes 32800 | tf_op jit(solution)/shard_map/ppermute | solution.py:333
  56.1 1.8 %collective-permute-done.7.rest_6_.rest_7_ = f32[64,128]{1,0:T(8,128)S(1)} collective-permute-done((f32[64,128]{1,0:T(8,128)}, f32[64,128]{1,0:T(8,128)S(1)}, u32[]{:S(2)}, u32[]{:S(2)}) %collective-permute-start.7) | collective-permute-done | bytes 32800 | tf_op jit(solution)/shard_map/ppermute | solution.py:333
  57.9 4.4 %all-to-all-done.1 = bf16[16,512,128]{2,1,0:T(8,128)(2,1)S(1)} async-done(((bf16[16,512,128]{2,1,0:T(8,128)(2,1)}), bf16[16,512,128]{2,1,0:T(8,128)(2,1)S(1)}, u32[]{:S(2)}, u32[]{:S(2)}) %all-to-all-start.1) | async-done | bytes 2097184 | tf_op jit(solution)/shard_map/all_to_all | solution.py:381
  63.2 2.8 %collective-permute-done.8.other_ref = bf16[64,64,128]{2,1,0:T(8,128)(2,1)S(1)} collective-permute-done((bf16[64,64,128]{2,1,0:T(8,128)(2,1)S(1)}, bf16[64,64,128]{2,1,0:T(8,128)(2,1)S(1)}, u32[]{:S(2)}, u32[]{:S(2)}) %collective-permute-start.8) | collective-permute-done | bytes 1048608 | tf_op jit(solution)/shard_map/ppermute | solution.py:403
  66.0 9.6 %shard_map.126.mean_ref = f32[8,64,128]{2,1,0:T(8,128)} custom-call(s32[1]{0:T(128)S(6)} %select_n.12.core_ref, s32[64]{0:T(128)S(1)} %copy-done.7, s32[15360]{0:T(1024)S(1)} %reshape.26.rest_7_.near_ref, bf16[64,64,128]{2,1,0:T(8,128)(2,1)S(1)} %shard_map.125.own_ref, bf16[64,64,128]{2,1,0:T(8,128)(2,1)S(1)} %collective-permute-done.8.other_ref), custom_call_target="tpu_custom_call" | custom-call | bytes 31457280 | tf_op jit(solution)/shard_map/pallas_call | solution.py:397
  75.5 8.0 %all-to-all-start.2 = ((f32[8,64,128]{2,1,0:T(8,128)}), f32[8,64,128]{2,1,0:T(8,128)S(1)}, u32[]{:S(2)}, u32[]{:S(2)}) async-start(f32[8,64,128]{2,1,0:T(8,128)} %shard_map.126.mean_ref), calls=%async_computation.2 | async-start | bytes 524288 | tf_op jit(solution)/shard_map/all_to_all | solution.py:417
  83.6 2.8 %copy-done = bf16[48,64,1024]{2,1,0:T(8,128)(2,1)S(1)} copy-done((bf16[48,64,1024]{2,1,0:T(8,128)(2,1)S(1)}, bf16[48,64,1024]{2,1,0:T(8,128)(2,1)}, u32[]{:S(2)}) %copy-start) | copy-done | bytes 6291480
  86.4 2.8 %shard_map.127 = (f32[64,1024]{1,0:T(8,128)S(1)}, bf16[16,64,1024]{2,1,0:T(8,128)(2,1)S(1)}) custom-call(s32[2]{0:T(128)S(1)} %copy-done.4, f32[1,1024]{1,0:T(1,128)S(1)} %bitcast.15, bf16[16,3,64,1024]{3,2,1,0:T(8,128)(2,1)S(1)} %bitcast.14, f32[64,128]{1,0:T(8,128)S(1)} %copy-done.3, f32[64,128]{1,0:T(8,128)S(1)} %collective-permute-done.1.rest_0_.rest_1_, ...), custom_call_target="tpu_custom_call" | custom-call | flops 402653184 | bytes 9437184 | tf_op jit(solution)/shard_map/pallas_call | solution.py:405
  89.2 3.5 %all-to-all-done.2.mean_ref = f32[8,64,128]{2,1,0:T(8,128)S(1)} async-done(((f32[8,64,128]{2,1,0:T(8,128)}), f32[8,64,128]{2,1,0:T(8,128)S(1)}, u32[]{:S(2)}, u32[]{:S(2)}) %all-to-all-start.2) | async-done | bytes 262176 | tf_op jit(solution)/shard_map/all_to_all | solution.py:417
  92.7 1.6 %shard_map.128 = (bf16[64,1024]{1,0:T(8,128)(2,1)}, bf16[64,1024]{1,0:T(8,128)(2,1)S(1)}) custom-call(f32[8,64,128]{2,1,0:T(8,128)S(1)} %all-to-all-done.2.mean_ref, f32[64,1024]{1,0:T(8,128)S(1)} %get-tuple-element.38.part_ref, bf16[16,64,1024]{2,1,0:T(8,128)(2,1)S(1)} %get-tuple-element.39.weight_ref, bf16[64,1024]{1,0:T(8,128)(2,1)S(1)} %copy-done.2), custom_call_target="tpu_custom_call" | custom-call | flops 268435456 | bytes 4194304 | tf_op jit(solution)/shard_map/pallas_call | solution.py:421
  95.5 1.8 %collective-permute-start.12 = (bf16[64,1024]{1,0:T(8,128)(2,1)S(1)}, bf16[64,1024]{1,0:T(8,128)(2,1)S(1)}, u32[]{:S(2)}, u32[]{:S(2)}) collective-permute-start(bf16[64,1024]{1,0:T(8,128)(2,1)S(1)} %get-tuple-element.44.near_ref), channel_id=1, source_target_pairs={{0,12},{1,13},{2,14},{3,15},{4,0},{5,1},{6,2},{7,3},{8,4},{9,5},{1... | collective-permute-start | bytes 393224 | tf_op jit(solution)/shard_map/ppermute | solution.py:333
  97.3 3.2 %collective-permute-start.10 = (bf16[64,1024]{1,0:T(8,128)(2,1)S(1)}, bf16[64,1024]{1,0:T(8,128)(2,1)S(1)}, u32[]{:S(2)}, u32[]{:S(2)}) collective-permute-start(bf16[64,1024]{1,0:T(8,128)(2,1)S(1)} %get-tuple-element.44.near_ref), channel_id=1, source_target_pairs={{0,14},{1,15},{2,0},{3,1},{4,2},{5,3},{6,4},{7,5},{8,6},{9,7},{10,... | collective-permute-start | bytes 393224 | tf_op jit(solution)/shard_map/ppermute | solution.py:333
  101.3 2.7 %collective-permute-start.13 = (bf16[64,1024]{1,0:T(8,128)(2,1)S(1)}, bf16[64,1024]{1,0:T(8,128)(2,1)S(1)}, u32[]{:S(2)}, u32[]{:S(2)}) collective-permute-start(bf16[64,1024]{1,0:T(8,128)(2,1)S(1)} %collective-permute-done.11.rest_2_), channel_id=1, source_target_pairs={{0,2},{1,3},{2,4},{3,5},{4,6},{5,7},{6,8},{7,9},{8,10},{9,11},{10,... | collective-permute-start | bytes 393224 | tf_op jit(solution)/shard_map/ppermute | solution.py:333
  104.0 1.3 collective-permute-done.12.rest_3_
  105.8 3.5 %collective-permute-start.15 = (bf16[32,1024]{1,0:T(8,128)(2,1)S(1)}, bf16[32,1024]{1,0:T(8,128)(2,1)S(1)}, u32[]{:S(2)}, u32[]{:S(2)}) collective-permute-start(bf16[32,1024]{1,0:T(8,128)(2,1)S(1)} %slice.24), channel_id=1, source_target_pairs={{0,4},{1,5},{2,6},{3,7},{4,8},{5,9},{6,10},{7,11},{8,12},{9,13},{1... | collective-permute-start | bytes 196616 | tf_op jit(solution)/shard_map/ppermute | solution.py:333
  111.9 3.9 %collective-permute-done.16.rest_7_ = bf16[32,1024]{1,0:T(8,128)(2,1)S(1)} collective-permute-done((bf16[32,1024]{1,0:T(8,128)(2,1)S(1)}, bf16[32,1024]{1,0:T(8,128)(2,1)S(1)}, u32[]{:S(2)}, u32[]{:S(2)}) %collective-permute-start.16) | collective-permute-done | bytes 65568 | tf_op jit(solution)/shard_map/ppermute | solution.py:333
  115.8 1.3 shard_map.130
  117.2 1.9 %collective-permute-done.17.right_ref = f32[16,8,1024]{2,1,0:T(8,128)S(1)} collective-permute-done((f32[16,8,1024]{2,1,0:T(8,128)S(1)}, f32[16,8,1024]{2,1,0:T(8,128)S(1)}, u32[]{:S(2)}, u32[]{:S(2)}) %collective-permute-start.17) | collective-permute-done | bytes 524320 | tf_op jit(solution)/shard_map/ppermute | solution.py:440
  119.1 14.9 %all_to_all.25.in_ref = f32[16,8,1024]{2,1,0:T(8,128)S(1)} all-to-all(f32[16,8,1024]{2,1,0:T(8,128)S(1)} %shard_map.131), channel_id=1, replica_groups=mesh['dom'=16,'feat'=16] {'dom'}, dimensions={0} | all-to-all | bytes 1048576 | tf_op jit(solution)/shard_map/all_to_all | solution.py:442
  134.1 14.0 %all_to_all.26 = f32[16,8,1024]{2,1,0:T(8,128)S(1)} all-to-all(f32[16,8,1024]{2,1,0:T(8,128)S(1)} %shard_map.132), channel_id=1, replica_groups=mesh['dom'=16,'feat'=16] {'dom'}, dimensions={0} | all-to-all | bytes 1048576 | tf_op jit(solution)/shard_map/all_to_all | solution.py:444
  (57 shorter events, 10.8 us)
Async XLA Ops:
  8.7 14.5 %all-to-all-start = ((s32[16,1,128]{2,1,0:T(1,128)}), s32[16,1,128]{2,1,0:T(1,128)S(1)}, u32[]{:S(2)}, u32[]{:S(2)}) async-start(s32[16,1,128]{2,1,0:T(1,128)} %shard_map.121), calls=%async_computation | async-start | bytes 16384 | tf_op jit(solution)/shard_map/all_to_all | solution.py:341
  15.7 67.9 %all-gather.3.cloned.1.call-start = ((), (), s32[]{:S(2)}) async-start(), calls=%async_computation.5 | async-start | bytes 6684672 | tf_op jit(solution)/shard_map/all_gather | solution.py:380
  26.9 5.1 %copy-start.11 = (f32[8,64,128]{2,1,0:T(8,128)S(1)}, f32[8,64,128]{2,1,0:T(8,128)}, u32[]{:S(2)}) copy-start(f32[8,64,128]{2,1,0:T(8,128)} %get-tuple-element.28) | copy-start | bytes 786436
  26.9 24.7 %copy-start.9 = (s32[15,1024]{1,0:T(8,128)S(1)}, s32[15,1024]{1,0:T(8,128)}, u32[]{:S(2)}) copy-start(s32[15,1024]{1,0:T(8,128)} %param.12) | copy-start | bytes 184324
  26.9 35.3 %copy-start.6 = (s32[64,1]{0,1:T(1,128)S(1)}, s32[64,1]{0,1:T(1,128)}, u32[]{:S(2)}) copy-start(s32[64,1]{0,1:T(1,128)} %param.13) | copy-start | bytes 772
  26.9 35.3 %all-to-all-start.1 = ((bf16[16,512,128]{2,1,0:T(8,128)(2,1)}), bf16[16,512,128]{2,1,0:T(8,128)(2,1)S(1)}, u32[]{:S(2)}, u32[]{:S(2)}) async-start(bf16[16,512,128]{2,1,0:T(8,128)(2,1)} %bitcast.18), calls=%async_computation.1 | async-start | bytes 4194304 | tf_op jit(solution)/shard_map/all_to_all | solution.py:381
  32.0 1.6 %collective-permute-start = (f32[8,64,128]{2,1,0:T(8,128)S(1)}, f32[8,64,128]{2,1,0:T(8,128)S(1)}, u32[]{:S(2)}, u32[]{:S(2)}) collective-permute-start(f32[8,64,128]{2,1,0:T(8,128)S(1)} %copy-done.11), channel_id=1, source_target_pairs={{0,1},{1,0},{2,3},{3,2},{4,5},{5,4},{6,7},{7,6},{8,9},{9,8},{10,11... | collective-permute-start | bytes 786440 | tf_op jit(solution)/shard_map/ppermute | solution.py:389
  36.2 11.2 %collective-permute-start.1 = (f32[64,128]{1,0:T(8,128)}, f32[64,128]{1,0:T(8,128)S(1)}, u32[]{:S(2)}, u32[]{:S(2)}) collective-permute-start(f32[64,128]{1,0:T(8,128)} %get-tuple-element.29), channel_id=1, source_target_pairs={{0,2},{1,3},{2,4},{3,5},{4,6},{5,7},{6,8},{7,9},{8,10},{9,11},{10,... | collective-permute-start | bytes 98312 | tf_op jit(solution)/shard_map/ppermute | solution.py:333
  38.2 10.8 %collective-permute-start.2 = (f32[64,128]{1,0:T(8,128)}, f32[64,128]{1,0:T(8,128)S(1)}, u32[]{:S(2)}, u32[]{:S(2)}) collective-permute-start(f32[64,128]{1,0:T(8,128)} %get-tuple-element.30), channel_id=1, source_target_pairs={{0,14},{1,15},{2,0},{3,1},{4,2},{5,3},{6,4},{7,5},{8,6},{9,7},{10,... | collective-permute-start | bytes 98312 | tf_op jit(solution)/shard_map/ppermute | solution.py:333
  38.3 13.9 %collective-permute-start.3 = (f32[64,128]{1,0:T(8,128)}, f32[64,128]{1,0:T(8,128)S(1)}, u32[]{:S(2)}, u32[]{:S(2)}) collective-permute-start(f32[64,128]{1,0:T(8,128)} %get-tuple-element.31), channel_id=1, source_target_pairs={{0,4},{1,5},{2,6},{3,7},{4,8},{5,9},{6,10},{7,11},{8,12},{9,13},{1... | collective-permute-start | bytes 98312 | tf_op jit(solution)/shard_map/ppermute | solution.py:333
  44.0 8.2 %collective-permute-start.4 = (f32[64,128]{1,0:T(8,128)}, f32[64,128]{1,0:T(8,128)S(1)}, u32[]{:S(2)}, u32[]{:S(2)}) collective-permute-start(f32[64,128]{1,0:T(8,128)} %get-tuple-element.32), channel_id=1, source_target_pairs={{0,12},{1,13},{2,14},{3,15},{4,0},{5,1},{6,2},{7,3},{8,4},{9,5},{1... | collective-permute-start | bytes 98312 | tf_op jit(solution)/shard_map/ppermute | solution.py:333
  44.0 8.3 %collective-permute-start.5 = (f32[64,128]{1,0:T(8,128)}, f32[64,128]{1,0:T(8,128)S(1)}, u32[]{:S(2)}, u32[]{:S(2)}) collective-permute-start(f32[64,128]{1,0:T(8,128)} %get-tuple-element.33), channel_id=1, source_target_pairs={{0,6},{1,7},{2,8},{3,9},{4,10},{5,11},{6,12},{7,13},{8,14},{9,15},... | collective-permute-start | bytes 98312 | tf_op jit(solution)/shard_map/ppermute | solution.py:333
  47.4 8.7 %collective-permute-start.6 = (f32[64,128]{1,0:T(8,128)}, f32[64,128]{1,0:T(8,128)S(1)}, u32[]{:S(2)}, u32[]{:S(2)}) collective-permute-start(f32[64,128]{1,0:T(8,128)} %get-tuple-element.34), channel_id=1, source_target_pairs={{0,10},{1,11},{2,12},{3,13},{4,14},{5,15},{6,0},{7,1},{8,2},{9,3},... | collective-permute-start | bytes 98312 | tf_op jit(solution)/shard_map/ppermute | solution.py:333
  49.0 8.8 %collective-permute-start.7 = (f32[64,128]{1,0:T(8,128)}, f32[64,128]{1,0:T(8,128)S(1)}, u32[]{:S(2)}, u32[]{:S(2)}) collective-permute-start(f32[64,128]{1,0:T(8,128)} %get-tuple-element.35), channel_id=1, source_target_pairs={{0,8},{1,9},{2,10},{3,11},{4,12},{5,13},{6,14},{7,15},{8,0},{9,1},... | collective-permute-start | bytes 98312 | tf_op jit(solution)/shard_map/ppermute | solution.py:333
  51.9 14.1 %copy-start.7 = (s32[64]{0:T(128)S(1)}, s32[64]{0:T(128)}, u32[]{:S(2)}) copy-start(s32[64]{0:T(128)} %count_ref.1) | copy-start | bytes 772
  63.1 20.5 %copy-start.3 = (f32[64,128]{1,0:T(8,128)S(1)}, f32[64,128]{1,0:T(8,128)}, u32[]{:S(2)}) copy-start(f32[64,128]{1,0:T(8,128)} %get-tuple-element.37.rest_0_) | copy-start | bytes 98308
  63.1 20.5 %copy-start.4 = (s32[2]{0:T(128)S(1)}, s32[2]{0:T(128)}, u32[]{:S(2)}) copy-start(s32[2]{0:T(128)} %pad_add_fusion.place_ref) | copy-start | bytes 28
  63.1 20.5 %copy-start.5 = (f32[1024]{0:T(1024)S(1)}, f32[1024]{0:T(1024)}, u32[]{:S(2)}) copy-start(f32[1024]{0:T(1024)} %param.18) | copy-start | bytes 12292
  63.1 2.9 %collective-permute-start.8 = (bf16[64,64,128]{2,1,0:T(8,128)(2,1)S(1)}, bf16[64,64,128]{2,1,0:T(8,128)(2,1)S(1)}, u32[]{:S(2)}, u32[]{:S(2)}) collective-permute-start(bf16[64,64,128]{2,1,0:T(8,128)(2,1)S(1)} %shard_map.125.own_ref), channel_id=1, source_target_pairs={{0,1},{1,0},{2,3},{3,2},{4,5},{5,4},{6,7},{7,6},{8,9},{9,8},{10,11... | collective-permute-start | bytes 3145736 | tf_op jit(solution)/shard_map/ppermute | solution.py:403
  75.5 17.1 %all-to-all-start.2 = ((f32[8,64,128]{2,1,0:T(8,128)}), f32[8,64,128]{2,1,0:T(8,128)S(1)}, u32[]{:S(2)}, u32[]{:S(2)}) async-start(f32[8,64,128]{2,1,0:T(8,128)} %shard_map.126.mean_ref), calls=%async_computation.2 | async-start | bytes 524288 | tf_op jit(solution)/shard_map/all_to_all | solution.py:417
  83.6 2.8 %copy-start = (bf16[48,64,1024]{2,1,0:T(8,128)(2,1)S(1)}, bf16[48,64,1024]{2,1,0:T(8,128)(2,1)}, u32[]{:S(2)}) copy-start(bf16[48,64,1024]{2,1,0:T(8,128)(2,1)} %all-gather.3.cloned.1.call-done) | copy-start | bytes 18874372
  86.4 6.3 %copy-start.2 = (bf16[64,1024]{1,0:T(8,128)(2,1)S(1)}, bf16[64,1024]{1,0:T(8,128)(2,1)}, u32[]{:S(2)}) copy-start(bf16[64,1024]{1,0:T(8,128)(2,1)} %cotangent_ref.1) | copy-start | bytes 393220
  89.2 20.6 %copy-start.1 = (f32[8,64,128]{2,1,0:T(8,128)S(1)}, f32[8,64,128]{2,1,0:T(8,128)}, u32[]{:S(2)}) copy-start(f32[8,64,128]{2,1,0:T(8,128)} %get-tuple-element.41.self_ref) | copy-start | bytes 786436
  94.3 7.0 %collective-permute-start.11 = (bf16[64,1024]{1,0:T(8,128)(2,1)S(1)}, bf16[64,1024]{1,0:T(8,128)(2,1)S(1)}, u32[]{:S(2)}, u32[]{:S(2)}) collective-permute-start(bf16[64,1024]{1,0:T(8,128)(2,1)S(1)} %get-tuple-element.44.near_ref), channel_id=1, source_target_pairs={{0,4},{1,5},{2,6},{3,7},{4,8},{5,9},{6,10},{7,11},{8,12},{9,13},{1... | collective-permute-start | bytes 393224 | tf_op jit(solution)/shard_map/ppermute | solution.py:333
  95.5 9.7 %collective-permute-start.12 = (bf16[64,1024]{1,0:T(8,128)(2,1)S(1)}, bf16[64,1024]{1,0:T(8,128)(2,1)S(1)}, u32[]{:S(2)}, u32[]{:S(2)}) collective-permute-start(bf16[64,1024]{1,0:T(8,128)(2,1)S(1)} %get-tuple-element.44.near_ref), channel_id=1, source_target_pairs={{0,12},{1,13},{2,14},{3,15},{4,0},{5,1},{6,2},{7,3},{8,4},{9,5},{1... | collective-permute-start | bytes 393224 | tf_op jit(solution)/shard_map/ppermute | solution.py:333
  97.3 12.0 %collective-permute-start.10 = (bf16[64,1024]{1,0:T(8,128)(2,1)S(1)}, bf16[64,1024]{1,0:T(8,128)(2,1)S(1)}, u32[]{:S(2)}, u32[]{:S(2)}) collective-permute-start(bf16[64,1024]{1,0:T(8,128)(2,1)S(1)} %get-tuple-element.44.near_ref), channel_id=1, source_target_pairs={{0,14},{1,15},{2,0},{3,1},{4,2},{5,3},{6,4},{7,5},{8,6},{9,7},{10,... | collective-permute-start | bytes 393224 | tf_op jit(solution)/shard_map/ppermute | solution.py:333
  100.6 10.4 %collective-permute-start.9 = (bf16[64,1024]{1,0:T(8,128)(2,1)S(1)}, bf16[64,1024]{1,0:T(8,128)(2,1)S(1)}, u32[]{:S(2)}, u32[]{:S(2)}) collective-permute-start(bf16[64,1024]{1,0:T(8,128)(2,1)S(1)} %get-tuple-element.44.near_ref), channel_id=1, source_target_pairs={{0,2},{1,3},{2,4},{3,5},{4,6},{5,7},{6,8},{7,9},{8,10},{9,11},{10,... | collective-permute-start | bytes 393224 | tf_op jit(solution)/shard_map/ppermute | solution.py:333
  101.3 14.5 %collective-permute-start.13 = (bf16[64,1024]{1,0:T(8,128)(2,1)S(1)}, bf16[64,1024]{1,0:T(8,128)(2,1)S(1)}, u32[]{:S(2)}, u32[]{:S(2)}) collective-permute-start(bf16[64,1024]{1,0:T(8,128)(2,1)S(1)} %collective-permute-done.11.rest_2_), channel_id=1, source_target_pairs={{0,2},{1,3},{2,4},{3,5},{4,6},{5,7},{6,8},{7,9},{8,10},{9,11},{10,... | collective-permute-start | bytes 393224 | tf_op jit(solution)/shard_map/ppermute | solution.py:333
  105.2 10.6 %collective-permute-start.14 = (bf16[64,1024]{1,0:T(8,128)(2,1)S(1)}, bf16[64,1024]{1,0:T(8,128)(2,1)S(1)}, u32[]{:S(2)}, u32[]{:S(2)}) collective-permute-start(bf16[64,1024]{1,0:T(8,128)(2,1)S(1)} %collective-permute-done.12.rest_3_), channel_id=1, source_target_pairs={{0,14},{1,15},{2,0},{3,1},{4,2},{5,3},{6,4},{7,5},{8,6},{9,7},{10,... | collective-permute-start | bytes 393224 | tf_op jit(solution)/shard_map/ppermute | solution.py:333
  105.8 6.1 %collective-permute-start.15 = (bf16[32,1024]{1,0:T(8,128)(2,1)S(1)}, bf16[32,1024]{1,0:T(8,128)(2,1)S(1)}, u32[]{:S(2)}, u32[]{:S(2)}) collective-permute-start(bf16[32,1024]{1,0:T(8,128)(2,1)S(1)} %slice.24), channel_id=1, source_target_pairs={{0,4},{1,5},{2,6},{3,7},{4,8},{5,9},{6,10},{7,11},{8,12},{9,13},{1... | collective-permute-start | bytes 196616 | tf_op jit(solution)/shard_map/ppermute | solution.py:333
  109.3 6.5 %collective-permute-start.16 = (bf16[32,1024]{1,0:T(8,128)(2,1)S(1)}, bf16[32,1024]{1,0:T(8,128)(2,1)S(1)}, u32[]{:S(2)}, u32[]{:S(2)}) collective-permute-start(bf16[32,1024]{1,0:T(8,128)(2,1)S(1)} %slice.25), channel_id=1, source_target_pairs={{0,12},{1,13},{2,14},{3,15},{4,0},{5,1},{6,2},{7,3},{8,4},{9,5},{1... | collective-permute-start | bytes 196616 | tf_op jit(solution)/shard_map/ppermute | solution.py:333
  117.1 2.0 %collective-permute-start.17 = (f32[16,8,1024]{2,1,0:T(8,128)S(1)}, f32[16,8,1024]{2,1,0:T(8,128)S(1)}, u32[]{:S(2)}, u32[]{:S(2)}) collective-permute-start(f32[16,8,1024]{2,1,0:T(8,128)S(1)} %get-tuple-element.46), channel_id=1, source_target_pairs={{0,1},{1,0},{2,3},{3,2},{4,5},{5,4},{6,7},{7,6},{8,9},{9,8},{10,11... | collective-permute-start | bytes 1572872 | tf_op jit(solution)/shard_map/ppermute | solution.py:440
  (2 other events, 1.3 us)
Sparse Core Ops, SparseCore 0:
  27.0 51.0 all-gather.2

commit v5 on v4

--- a/solution.py
+++ b/solution.py
@@ -375,7 +375,7 @@
             pltpu.SemaphoreType.DMA((n_dom,)),
             pltpu.SemaphoreType.DMA((3,)),
         ],
-        limit=59, outs=(ANY, ANY),
+        limit=53.8, outs=(ANY, ANY),
     )(requests, packed, w_self, w_neigh)
     weights = lax.all_gather(weight, "feat", axis=0, tiled=False)
     arrived = lax.all_to_all(
@@ -385,7 +385,7 @@
         join_kernel,
         (shape((ring, 64, BLOCK), F32),) + (shape((64, BLOCK), F32),) * ring,
         [SMEM, VMEM, VMEM],
-        limit=60, cost=cost(0, 1 << 20),
+        limit=53.55, cost=cost(0, 1 << 20),
     )(place, kept, lax.ppermute(given, "feat", across))
     moved = [climb(sends[k % ring], k) for k in DISTANCES[1:]]
     pieces = [sends[0]] + moved
@@ -412,7 +412,7 @@
             pltpu.SemaphoreType.DMA((12,)),
             pltpu.SemaphoreType.DMA((ring,)),
         ],
-        limit=24, cost=cost(3 << 27, 9 << 20),
+        limit=51.4, cost=cost(3 << 27, 9 << 20),
     )(place, out_bias[None, :], weights, *pieces)
     mean_seeds = lax.all_to_all(
         mean, "feat", split_axis=0, concat_axis=0, tiled=True, axis_index_groups=columns

time: 156 us -> 156 us (level)
  local copies, waits for them, and re-layouts: 5.51 us -> 2.12 us
  waiting for transfers between devices: 28.2 us -> 30.7 us
    unnamed x24 -> x16, local copies, waits for them, and re-layouts: 4.13 us -> 0.74 us
    all_to_all x1, waiting for transfers between devices: 3.48 us -> 5.46 us  [body(): lax.all_to_all(mean, 'feat', split_axis=0, concat_axis=0, tiled=True, axi...]
  transfers between devices with their start and end apart: 22 -> 22, of which waited for: 12 -> 12; matrix products, arithmetic and copies ran while one was open for 1% -> 0% of each run, Pallas kernels for 14% -> 14%
where the time goes in v5:
time: 156 us; the launch traced here: 155 us
  starting transfers between devices  49.4 us (32%)
  waiting for transfers between devices  30.7 us (20%)
  Pallas kernels  29.7 us (19%)
  blocking collectives  28.8 us (18%)
  between operations  14.3 us (9%)
  local copies, waits for them, and re-layouts  2.12 us (1%)
    ppermute x15, starting transfers between devices, climb(): return lax.ppermute(value, 'feat', pairs)  28.9 us
    all_to_all x1, blocking collectives, body(): lax.all_to_all(partial, 'dom', split_axis=0, concat_axis=0, tiled=True)  14.8 us
    all_to_all x1, blocking collectives, body(): lax.all_to_all(total, 'dom', split_axis=0, concat_axis=0, tiled=True)  14 us
    ppermute x15, waiting for transfers between devices, climb(): return lax.ppermute(value, 'feat', pairs)  12.2 us
    pallas_call x1, Pallas kernels, body(): call(gather_kernel, shape((ring, 64, BLOCK), F32), [SMEM, SMEM, SMEM, VME...  9.55 us
    all_to_all x1, starting transfers between devices, body(): lax.all_to_all(mean, 'feat', split_axis=0, concat_axis=0, tiled=True, axi...  8.12 us
    all_to_all x1, starting transfers between devices, body(): lax.all_to_all(request, 'dom', split_axis=0, concat_axis=0, tiled=True)  7.03 us
    all_to_all x1, waiting for transfers between devices, body(): lax.all_to_all(mean, 'feat', split_axis=0, concat_axis=0, tiled=True, axi...  5.46 us
  transfers between devices with their start and end apart: 22, of which 12 were waited for; matrix products, arithmetic and copies ran while one was open for 0% of the time, Pallas kernels for 14%

profile of v5, /device:TPU:64, one launch (start us, length us, event | category | flops | bytes accessed | tf_op | source)
XLA Modules:
  0.0 155.1 jit_solution(6538235731466193008)
XLA Ops:
  7.2 1.5 shard_map.121
  8.7 7.0 %all-to-all-start = ((s32[16,1,128]{2,1,0:T(1,128)}), s32[16,1,128]{2,1,0:T(1,128)S(1)}, u32[]{:S(2)}, u32[]{:S(2)}) async-start(s32[16,1,128]{2,1,0:T(1,128)} %shard_map.121), calls=%async_computation | async-start | bytes 16384 | tf_op jit(solution)/shard_map/all_to_all | solution.py:341
  15.8 5.1 %shard_map.122 = (bf16[64,64,128]{2,1,0:T(8,128)(2,1)}, f32[8,64,128]{2,1,0:T(8,128)}, f32[8,64,128]{2,1,0:T(8,128)}) custom-call(s32[1]{0:T(128)S(6)} %select_n.12.core_ref, s32[1024]{0:T(1024)} %seed_hbm.1, f32[64,8192]{1,0:T(8,128)} %table_hbm.1), custom_call_target="tpu_custom_call" | custom-call | bytes 10485760 | tf_op jit(solution)/shard_map/pallas_call | solution.py:343
  20.8 2.4 %all-to-all-done.request_hbm = s32[16,1,128]{2,1,0:T(1,128)S(1)} async-done(((s32[16,1,128]{2,1,0:T(1,128)}), s32[16,1,128]{2,1,0:T(1,128)S(1)}, u32[]{:S(2)}, u32[]{:S(2)}) %all-to-all-start) | async-done | bytes 8224 | tf_op jit(solution)/shard_map/all_to_all | solution.py:341
  23.2 3.1 %shard_map.123 = (bf16[16,8,64,128]{3,2,1,0:T(8,128)(2,1)}, bf16[3,64,1024]{2,1,0:T(8,128)(2,1)}) custom-call(s32[16,1,128]{2,1,0:T(1,128)S(1)} %all-to-all-done.request_hbm, bf16[64,64,128]{2,1,0:T(8,128)(2,1)} %get-tuple-element.25.packed_hbm, f32[64,1024]{1,0:T(8,128)} %self_hbm.1, f32[64,1024]{1,0:T(8,128)} %neigh_hbm.1), custom_call_target="tpu_custom_call" | custom-call | tf_op jit(solution)/shard_map/pallas_call | solution.py:363
  26.3 5.0 %all-to-all-start.1 = ((bf16[16,512,128]{2,1,0:T(8,128)(2,1)}), bf16[16,512,128]{2,1,0:T(8,128)(2,1)S(1)}, u32[]{:S(2)}, u32[]{:S(2)}) async-start(bf16[16,512,128]{2,1,0:T(8,128)(2,1)} %bitcast.18), calls=%async_computation.1 | async-start | bytes 4194304 | tf_op jit(solution)/shard_map/all_to_all | solution.py:381
  31.6 1.4 collective-permute-done.other_ref
  33.7 1.9 %shard_map.124 = (f32[8,64,128]{2,1,0:T(8,128)}, f32[64,128]{1,0:T(8,128)S(1)}, f32[64,128]{1,0:T(8,128)S(1)}, f32[64,128]{1,0:T(8,128)S(1)}, f32[64,128]{1,0:T(...) custom-call(s32[2]{0:T(128)S(1)} %pad_add_fusion.place_ref, ...), custom_call_target="tpu_custom_call" | custom-call | bytes 1048576 | tf_op jit(solution)/shard_map/pallas_call | solution.py:384
  35.6 1.9 %collective-permute-start.1 = (f32[64,128]{1,0:T(8,128)S(1)}, f32[64,128]{1,0:T(8,128)S(1)}, u32[]{:S(2)}, u32[]{:S(2)}) collective-permute-start(f32[64,128]{1,0:T(8,128)S(1)} %get-tuple-element.29), channel_id=1, source_target_pairs={{0,2},{1,3},{2,4},{3,5},{4,6},{5,7},{6,8},{7,9},{8,10},{9,11},{10,... | collective-permute-start | bytes 98312 | tf_op jit(solution)/shard_map/ppermute | solution.py:333
  37.6 5.7 %collective-permute-start.3 = (f32[64,128]{1,0:T(8,128)S(1)}, f32[64,128]{1,0:T(8,128)S(1)}, u32[]{:S(2)}, u32[]{:S(2)}) collective-permute-start(f32[64,128]{1,0:T(8,128)S(1)} %get-tuple-element.31), channel_id=1, source_target_pairs={{0,4},{1,5},{2,6},{3,7},{4,8},{5,9},{6,10},{7,11},{8,12},{9,13},{1... | collective-permute-start | bytes 98312 | tf_op jit(solution)/shard_map/ppermute | solution.py:333
  43.3 3.4 %collective-permute-start.5 = (f32[64,128]{1,0:T(8,128)S(1)}, f32[64,128]{1,0:T(8,128)S(1)}, u32[]{:S(2)}, u32[]{:S(2)}) collective-permute-start(f32[64,128]{1,0:T(8,128)S(1)} %get-tuple-element.33), channel_id=1, source_target_pairs={{0,6},{1,7},{2,8},{3,9},{4,10},{5,11},{6,12},{7,13},{8,14},{9,15},... | collective-permute-start | bytes 98312 | tf_op jit(solution)/shard_map/ppermute | solution.py:333
  46.7 1.7 %collective-permute-start.6 = (f32[64,128]{1,0:T(8,128)S(1)}, f32[64,128]{1,0:T(8,128)S(1)}, u32[]{:S(2)}, u32[]{:S(2)}) collective-permute-start(f32[64,128]{1,0:T(8,128)S(1)} %get-tuple-element.34), channel_id=1, source_target_pairs={{0,10},{1,11},{2,12},{3,13},{4,14},{5,15},{6,0},{7,1},{8,2},{9,3},... | collective-permute-start | bytes 98312 | tf_op jit(solution)/shard_map/ppermute | solution.py:333
  48.4 2.6 %collective-permute-start.7 = (f32[64,128]{1,0:T(8,128)S(1)}, f32[64,128]{1,0:T(8,128)S(1)}, u32[]{:S(2)}, u32[]{:S(2)}) collective-permute-start(f32[64,128]{1,0:T(8,128)S(1)} %get-tuple-element.35), channel_id=1, source_target_pairs={{0,8},{1,9},{2,10},{3,11},{4,12},{5,13},{6,14},{7,15},{8,0},{9,1},... | collective-permute-start | bytes 98312 | tf_op jit(solution)/shard_map/ppermute | solution.py:333
  51.6 3.7 %collective-permute-done.6.rest_5_.rest_6_ = f32[64,128]{1,0:T(8,128)S(1)} collective-permute-done((f32[64,128]{1,0:T(8,128)S(1)}, f32[64,128]{1,0:T(8,128)S(1)}, u32[]{:S(2)}, u32[]{:S(2)}) %collective-permute-start.6) | collective-permute-done | bytes 32800 | tf_op jit(solution)/shard_map/ppermute | solution.py:333
  55.3 1.7 %collective-permute-done.7.rest_6_.rest_7_ = f32[64,128]{1,0:T(8,128)S(1)} collective-permute-done((f32[64,128]{1,0:T(8,128)S(1)}, f32[64,128]{1,0:T(8,128)S(1)}, u32[]{:S(2)}, u32[]{:S(2)}) %collective-permute-start.7) | collective-permute-done | bytes 32800 | tf_op jit(solution)/shard_map/ppermute | solution.py:333
  56.9 4.7 %all-to-all-done.1 = bf16[16,512,128]{2,1,0:T(8,128)(2,1)S(1)} async-done(((bf16[16,512,128]{2,1,0:T(8,128)(2,1)}), bf16[16,512,128]{2,1,0:T(8,128)(2,1)S(1)}, u32[]{:S(2)}, u32[]{:S(2)}) %all-to-all-start.1) | async-done | bytes 2097184 | tf_op jit(solution)/shard_map/all_to_all | solution.py:381
  62.6 2.6 %collective-permute-done.8.other_ref = bf16[64,64,128]{2,1,0:T(8,128)(2,1)S(1)} collective-permute-done((bf16[64,64,128]{2,1,0:T(8,128)(2,1)S(1)}, bf16[64,64,128]{2,1,0:T(8,128)(2,1)S(1)}, u32[]{:S(2)}, u32[]{:S(2)}) %collective-permute-start.8) | collective-permute-done | bytes 1048608 | tf_op jit(solution)/shard_map/ppermute | solution.py:403
  65.3 9.6 %shard_map.126.mean_ref = f32[8,64,128]{2,1,0:T(8,128)} custom-call(s32[1]{0:T(128)S(6)} %select_n.12.core_ref, s32[64]{0:T(128)S(1)} %copy-done.4, s32[15360]{0:T(1024)S(1)} %reshape.26.rest_7_.near_ref, bf16[64,64,128]{2,1,0:T(8,128)(2,1)S(1)} %shard_map.125.own_ref, bf16[64,64,128]{2,1,0:T(8,128)(2,1)S(1)} %collective-permute-done.8.other_ref), custom_call_target="tpu_custom_call" | custom-call | bytes 31457280 | tf_op jit(solution)/shard_map/pallas_call | solution.py:397
  74.8 8.1 %all-to-all-start.2 = ((f32[8,64,128]{2,1,0:T(8,128)}), f32[8,64,128]{2,1,0:T(8,128)S(1)}, u32[]{:S(2)}, u32[]{:S(2)}) async-start(f32[8,64,128]{2,1,0:T(8,128)} %shard_map.126.mean_ref), calls=%async_computation.2 | async-start | bytes 524288 | tf_op jit(solution)/shard_map/all_to_all | solution.py:417
  83.0 3.6 %shard_map.127 = (f32[64,1024]{1,0:T(8,128)S(1)}, bf16[16,64,1024]{2,1,0:T(8,128)(2,1)S(1)}) custom-call(s32[2]{0:T(128)S(1)} %pad_add_fusion.place_ref, f32[1,1024]{1,0:T(1,128)S(1)} %bitcast.14, bf16[16,3,64,1024]{3,2,1,0:T(8,128)(2,1)} %bitcast.17, f32[64,128]{1,0:T(8,128)S(1)} %get-tuple-element.37.rest_0_, ...), custom_call_target="tpu_custom_call" | custom-call | flops 402653184 | bytes 9437184 | tf_op jit(solution)/shard_map/pallas_call | solution.py:405
  86.6 5.5 %all-to-all-done.2.mean_ref = f32[8,64,128]{2,1,0:T(8,128)S(1)} async-done(((f32[8,64,128]{2,1,0:T(8,128)}), f32[8,64,128]{2,1,0:T(8,128)S(1)}, u32[]{:S(2)}, u32[]{:S(2)}) %all-to-all-start.2) | async-done | bytes 262176 | tf_op jit(solution)/shard_map/all_to_all | solution.py:417
  92.1 1.6 %shard_map.128 = (bf16[64,1024]{1,0:T(8,128)(2,1)}, bf16[64,1024]{1,0:T(8,128)(2,1)S(1)}) custom-call(f32[8,64,128]{2,1,0:T(8,128)S(1)} %all-to-all-done.2.mean_ref, f32[64,1024]{1,0:T(8,128)S(1)} %get-tuple-element.38.part_ref, bf16[16,64,1024]{2,1,0:T(8,128)(2,1)S(1)} %get-tuple-element.39.weight_ref, bf16[64,1024]{1,0:T(8,128)(2,1)S(1)} %copy-done.1), custom_call_target="tpu_custom_call" | custom-call | flops 268435456 | bytes 4194304 | tf_op jit(solution)/shard_map/pallas_call | solution.py:421
  94.9 1.8 %collective-permute-start.12 = (bf16[64,1024]{1,0:T(8,128)(2,1)S(1)}, bf16[64,1024]{1,0:T(8,128)(2,1)S(1)}, u32[]{:S(2)}, u32[]{:S(2)}) collective-permute-start(bf16[64,1024]{1,0:T(8,128)(2,1)S(1)} %get-tuple-element.44.near_ref), channel_id=1, source_target_pairs={{0,12},{1,13},{2,14},{3,15},{4,0},{5,1},{6,2},{7,3},{8,4},{9,5},{1... | collective-permute-start | bytes 393224 | tf_op jit(solution)/shard_map/ppermute | solution.py:333
  96.7 3.2 %collective-permute-start.10 = (bf16[64,1024]{1,0:T(8,128)(2,1)S(1)}, bf16[64,1024]{1,0:T(8,128)(2,1)S(1)}, u32[]{:S(2)}, u32[]{:S(2)}) collective-permute-start(bf16[64,1024]{1,0:T(8,128)(2,1)S(1)} %get-tuple-element.44.near_ref), channel_id=1, source_target_pairs={{0,14},{1,15},{2,0},{3,1},{4,2},{5,3},{6,4},{7,5},{8,6},{9,7},{10,... | collective-permute-start | bytes 393224 | tf_op jit(solution)/shard_map/ppermute | solution.py:333
  100.7 2.7 %collective-permute-start.13 = (bf16[64,1024]{1,0:T(8,128)(2,1)S(1)}, bf16[64,1024]{1,0:T(8,128)(2,1)S(1)}, u32[]{:S(2)}, u32[]{:S(2)}) collective-permute-start(bf16[64,1024]{1,0:T(8,128)(2,1)S(1)} %collective-permute-done.11.rest_2_), channel_id=1, source_target_pairs={{0,2},{1,3},{2,4},{3,5},{4,6},{5,7},{6,8},{7,9},{8,10},{9,11},{10,... | collective-permute-start | bytes 393224 | tf_op jit(solution)/shard_map/ppermute | solution.py:333
  103.4 1.3 collective-permute-done.12.rest_3_
  105.2 3.5 %collective-permute-start.15 = (bf16[32,1024]{1,0:T(8,128)(2,1)S(1)}, bf16[32,1024]{1,0:T(8,128)(2,1)S(1)}, u32[]{:S(2)}, u32[]{:S(2)}) collective-permute-start(bf16[32,1024]{1,0:T(8,128)(2,1)S(1)} %slice.24), channel_id=1, source_target_pairs={{0,4},{1,5},{2,6},{3,7},{4,8},{5,9},{6,10},{7,11},{8,12},{9,13},{1... | collective-permute-start | bytes 196616 | tf_op jit(solution)/shard_map/ppermute | solution.py:333
  111.3 3.9 %collective-permute-done.16.rest_7_ = bf16[32,1024]{1,0:T(8,128)(2,1)S(1)} collective-permute-done((bf16[32,1024]{1,0:T(8,128)(2,1)S(1)}, bf16[32,1024]{1,0:T(8,128)(2,1)S(1)}, u32[]{:S(2)}, u32[]{:S(2)}) %collective-permute-start.16) | collective-permute-done | bytes 65568 | tf_op jit(solution)/shard_map/ppermute | solution.py:333
  115.2 1.3 shard_map.130
  116.6 1.9 %collective-permute-done.17.right_ref = f32[16,8,1024]{2,1,0:T(8,128)S(1)} collective-permute-done((f32[16,8,1024]{2,1,0:T(8,128)S(1)}, f32[16,8,1024]{2,1,0:T(8,128)S(1)}, u32[]{:S(2)}, u32[]{:S(2)}) %collective-permute-start.17) | collective-permute-done | bytes 524320 | tf_op jit(solution)/shard_map/ppermute | solution.py:440
  118.5 14.8 %all_to_all.25.in_ref = f32[16,8,1024]{2,1,0:T(8,128)S(1)} all-to-all(f32[16,8,1024]{2,1,0:T(8,128)S(1)} %shard_map.131), channel_id=1, replica_groups=mesh['dom'=16,'feat'=16] {'dom'}, dimensions={0} | all-to-all | bytes 1048576 | tf_op jit(solution)/shard_map/all_to_all | solution.py:442
  133.4 14.0 %all_to_all.26 = f32[16,8,1024]{2,1,0:T(8,128)S(1)} all-to-all(f32[16,8,1024]{2,1,0:T(8,128)S(1)} %shard_map.132), channel_id=1, replica_groups=mesh['dom'=16,'feat'=16] {'dom'}, dimensions={0} | all-to-all | bytes 1048576 | tf_op jit(solution)/shard_map/all_to_all | solution.py:444
  (49 shorter events, 8.8 us)
Async XLA Ops:
  8.7 14.5 %all-to-all-start = ((s32[16,1,128]{2,1,0:T(1,128)}), s32[16,1,128]{2,1,0:T(1,128)S(1)}, u32[]{:S(2)}, u32[]{:S(2)}) async-start(s32[16,1,128]{2,1,0:T(1,128)} %shard_map.121), calls=%async_computation | async-start | bytes 16384 | tf_op jit(solution)/shard_map/all_to_all | solution.py:341
  15.7 67.3 %all-gather.3.cloned.1.call-start = ((), (), s32[]{:S(2)}) async-start(), calls=%async_computation.5 | async-start | bytes 6684672 | tf_op jit(solution)/shard_map/all_gather | solution.py:380
  26.3 5.1 %copy-start.7 = (f32[8,64,128]{2,1,0:T(8,128)S(1)}, f32[8,64,128]{2,1,0:T(8,128)}, u32[]{:S(2)}) copy-start(f32[8,64,128]{2,1,0:T(8,128)} %get-tuple-element.28) | copy-start | bytes 786436
  26.3 24.7 %copy-start.6 = (s32[15,1024]{1,0:T(8,128)S(1)}, s32[15,1024]{1,0:T(8,128)}, u32[]{:S(2)}) copy-start(s32[15,1024]{1,0:T(8,128)} %param.12) | copy-start | bytes 184324
  26.3 35.3 %copy-start.3 = (s32[64,1]{0,1:T(1,128)S(1)}, s32[64,1]{0,1:T(1,128)}, u32[]{:S(2)}) copy-start(s32[64,1]{0,1:T(1,128)} %param.13) | copy-start | bytes 772
  26.3 35.3 %all-to-all-start.1 = ((bf16[16,512,128]{2,1,0:T(8,128)(2,1)}), bf16[16,512,128]{2,1,0:T(8,128)(2,1)S(1)}, u32[]{:S(2)}, u32[]{:S(2)}) async-start(bf16[16,512,128]{2,1,0:T(8,128)(2,1)} %bitcast.18), calls=%async_computation.1 | async-start | bytes 4194304 | tf_op jit(solution)/shard_map/all_to_all | solution.py:381
  31.4 1.6 %collective-permute-start = (f32[8,64,128]{2,1,0:T(8,128)S(1)}, f32[8,64,128]{2,1,0:T(8,128)S(1)}, u32[]{:S(2)}, u32[]{:S(2)}) collective-permute-start(f32[8,64,128]{2,1,0:T(8,128)S(1)} %copy-done.7), channel_id=1, source_target_pairs={{0,1},{1,0},{2,3},{3,2},{4,5},{5,4},{6,7},{7,6},{8,9},{9,8},{10,11... | collective-permute-start | bytes 786440 | tf_op jit(solution)/shard_map/ppermute | solution.py:389
  33.0 0.7 copy-start.5
  35.6 11.1 %collective-permute-start.1 = (f32[64,128]{1,0:T(8,128)S(1)}, f32[64,128]{1,0:T(8,128)S(1)}, u32[]{:S(2)}, u32[]{:S(2)}) collective-permute-start(f32[64,128]{1,0:T(8,128)S(1)} %get-tuple-element.29), channel_id=1, source_target_pairs={{0,2},{1,3},{2,4},{3,5},{4,6},{5,7},{6,8},{7,9},{8,10},{9,11},{10,... | collective-permute-start | bytes 98312 | tf_op jit(solution)/shard_map/ppermute | solution.py:333
  37.5 10.8 %collective-permute-start.2 = (f32[64,128]{1,0:T(8,128)S(1)}, f32[64,128]{1,0:T(8,128)S(1)}, u32[]{:S(2)}, u32[]{:S(2)}) collective-permute-start(f32[64,128]{1,0:T(8,128)S(1)} %get-tuple-element.30), channel_id=1, source_target_pairs={{0,14},{1,15},{2,0},{3,1},{4,2},{5,3},{6,4},{7,5},{8,6},{9,7},{10,... | collective-permute-start | bytes 98312 | tf_op jit(solution)/shard_map/ppermute | solution.py:333
  37.6 13.9 %collective-permute-start.3 = (f32[64,128]{1,0:T(8,128)S(1)}, f32[64,128]{1,0:T(8,128)S(1)}, u32[]{:S(2)}, u32[]{:S(2)}) collective-permute-start(f32[64,128]{1,0:T(8,128)S(1)} %get-tuple-element.31), channel_id=1, source_target_pairs={{0,4},{1,5},{2,6},{3,7},{4,8},{5,9},{6,10},{7,11},{8,12},{9,13},{1... | collective-permute-start | bytes 98312 | tf_op jit(solution)/shard_map/ppermute | solution.py:333
  43.3 8.2 %collective-permute-start.4 = (f32[64,128]{1,0:T(8,128)S(1)}, f32[64,128]{1,0:T(8,128)S(1)}, u32[]{:S(2)}, u32[]{:S(2)}) collective-permute-start(f32[64,128]{1,0:T(8,128)S(1)} %get-tuple-element.32), channel_id=1, source_target_pairs={{0,12},{1,13},{2,14},{3,15},{4,0},{5,1},{6,2},{7,3},{8,4},{9,5},{1... | collective-permute-start | bytes 98312 | tf_op jit(solution)/shard_map/ppermute | solution.py:333
  43.3 8.2 %collective-permute-start.5 = (f32[64,128]{1,0:T(8,128)S(1)}, f32[64,128]{1,0:T(8,128)S(1)}, u32[]{:S(2)}, u32[]{:S(2)}) collective-permute-start(f32[64,128]{1,0:T(8,128)S(1)} %get-tuple-element.33), channel_id=1, source_target_pairs={{0,6},{1,7},{2,8},{3,9},{4,10},{5,11},{6,12},{7,13},{8,14},{9,15},... | collective-permute-start | bytes 98312 | tf_op jit(solution)/shard_map/ppermute | solution.py:333
  46.7 8.6 %collective-permute-start.6 = (f32[64,128]{1,0:T(8,128)S(1)}, f32[64,128]{1,0:T(8,128)S(1)}, u32[]{:S(2)}, u32[]{:S(2)}) collective-permute-start(f32[64,128]{1,0:T(8,128)S(1)} %get-tuple-element.34), channel_id=1, source_target_pairs={{0,10},{1,11},{2,12},{3,13},{4,14},{5,15},{6,0},{7,1},{8,2},{9,3},... | collective-permute-start | bytes 98312 | tf_op jit(solution)/shard_map/ppermute | solution.py:333
  48.4 8.6 %collective-permute-start.7 = (f32[64,128]{1,0:T(8,128)S(1)}, f32[64,128]{1,0:T(8,128)S(1)}, u32[]{:S(2)}, u32[]{:S(2)}) collective-permute-start(f32[64,128]{1,0:T(8,128)S(1)} %get-tuple-element.35), channel_id=1, source_target_pairs={{0,8},{1,9},{2,10},{3,11},{4,12},{5,13},{6,14},{7,15},{8,0},{9,1},... | collective-permute-start | bytes 98312 | tf_op jit(solution)/shard_map/ppermute | solution.py:333
  51.2 14.1 %copy-start.4 = (s32[64]{0:T(128)S(1)}, s32[64]{0:T(128)}, u32[]{:S(2)}) copy-start(s32[64]{0:T(128)} %count_ref.1) | copy-start | bytes 772
  62.5 20.4 %copy-start.2 = (f32[1024]{0:T(1024)S(1)}, f32[1024]{0:T(1024)}, u32[]{:S(2)}) copy-start(f32[1024]{0:T(1024)} %param.18) | copy-start | bytes 12292
  62.5 2.7 %collective-permute-start.8 = (bf16[64,64,128]{2,1,0:T(8,128)(2,1)S(1)}, bf16[64,64,128]{2,1,0:T(8,128)(2,1)S(1)}, u32[]{:S(2)}, u32[]{:S(2)}) collective-permute-start(bf16[64,64,128]{2,1,0:T(8,128)(2,1)S(1)} %shard_map.125.own_ref), channel_id=1, source_target_pairs={{0,1},{1,0},{2,3},{3,2},{4,5},{5,4},{6,7},{7,6},{8,9},{9,8},{10,11... | collective-permute-start | bytes 3145736 | tf_op jit(solution)/shard_map/ppermute | solution.py:403
  74.8 17.2 %all-to-all-start.2 = ((f32[8,64,128]{2,1,0:T(8,128)}), f32[8,64,128]{2,1,0:T(8,128)S(1)}, u32[]{:S(2)}, u32[]{:S(2)}) async-start(f32[8,64,128]{2,1,0:T(8,128)} %shard_map.126.mean_ref), calls=%async_computation.2 | async-start | bytes 524288 | tf_op jit(solution)/shard_map/all_to_all | solution.py:417
  83.0 9.1 %copy-start.1 = (bf16[64,1024]{1,0:T(8,128)(2,1)S(1)}, bf16[64,1024]{1,0:T(8,128)(2,1)}, u32[]{:S(2)}) copy-start(bf16[64,1024]{1,0:T(8,128)(2,1)} %cotangent_ref.1) | copy-start | bytes 393220
  86.6 22.6 %copy-start = (f32[8,64,128]{2,1,0:T(8,128)S(1)}, f32[8,64,128]{2,1,0:T(8,128)}, u32[]{:S(2)}) copy-start(f32[8,64,128]{2,1,0:T(8,128)} %get-tuple-element.41.self_ref) | copy-start | bytes 786436
  93.7 7.0 %collective-permute-start.11 = (bf16[64,1024]{1,0:T(8,128)(2,1)S(1)}, bf16[64,1024]{1,0:T(8,128)(2,1)S(1)}, u32[]{:S(2)}, u32[]{:S(2)}) collective-permute-start(bf16[64,1024]{1,0:T(8,128)(2,1)S(1)} %get-tuple-element.44.near_ref), channel_id=1, source_target_pairs={{0,4},{1,5},{2,6},{3,7},{4,8},{5,9},{6,10},{7,11},{8,12},{9,13},{1... | collective-permute-start | bytes 393224 | tf_op jit(solution)/shard_map/ppermute | solution.py:333
  94.9 9.7 %collective-permute-start.12 = (bf16[64,1024]{1,0:T(8,128)(2,1)S(1)}, bf16[64,1024]{1,0:T(8,128)(2,1)S(1)}, u32[]{:S(2)}, u32[]{:S(2)}) collective-permute-start(bf16[64,1024]{1,0:T(8,128)(2,1)S(1)} %get-tuple-element.44.near_ref), channel_id=1, source_target_pairs={{0,12},{1,13},{2,14},{3,15},{4,0},{5,1},{6,2},{7,3},{8,4},{9,5},{1... | collective-permute-start | bytes 393224 | tf_op jit(solution)/shard_map/ppermute | solution.py:333
  96.7 12.0 %collective-permute-start.10 = (bf16[64,1024]{1,0:T(8,128)(2,1)S(1)}, bf16[64,1024]{1,0:T(8,128)(2,1)S(1)}, u32[]{:S(2)}, u32[]{:S(2)}) collective-permute-start(bf16[64,1024]{1,0:T(8,128)(2,1)S(1)} %get-tuple-element.44.near_ref), channel_id=1, source_target_pairs={{0,14},{1,15},{2,0},{3,1},{4,2},{5,3},{6,4},{7,5},{8,6},{9,7},{10,... | collective-permute-start | bytes 393224 | tf_op jit(solution)/shard_map/ppermute | solution.py:333
  100.0 10.4 %collective-permute-start.9 = (bf16[64,1024]{1,0:T(8,128)(2,1)S(1)}, bf16[64,1024]{1,0:T(8,128)(2,1)S(1)}, u32[]{:S(2)}, u32[]{:S(2)}) collective-permute-start(bf16[64,1024]{1,0:T(8,128)(2,1)S(1)} %get-tuple-element.44.near_ref), channel_id=1, source_target_pairs={{0,2},{1,3},{2,4},{3,5},{4,6},{5,7},{6,8},{7,9},{8,10},{9,11},{10,... | collective-permute-start | bytes 393224 | tf_op jit(solution)/shard_map/ppermute | solution.py:333
  100.7 14.5 %collective-permute-start.13 = (bf16[64,1024]{1,0:T(8,128)(2,1)S(1)}, bf16[64,1024]{1,0:T(8,128)(2,1)S(1)}, u32[]{:S(2)}, u32[]{:S(2)}) collective-permute-start(bf16[64,1024]{1,0:T(8,128)(2,1)S(1)} %collective-permute-done.11.rest_2_), channel_id=1, source_target_pairs={{0,2},{1,3},{2,4},{3,5},{4,6},{5,7},{6,8},{7,9},{8,10},{9,11},{10,... | collective-permute-start | bytes 393224 | tf_op jit(solution)/shard_map/ppermute | solution.py:333
  104.6 10.6 %collective-permute-start.14 = (bf16[64,1024]{1,0:T(8,128)(2,1)S(1)}, bf16[64,1024]{1,0:T(8,128)(2,1)S(1)}, u32[]{:S(2)}, u32[]{:S(2)}) collective-permute-start(bf16[64,1024]{1,0:T(8,128)(2,1)S(1)} %collective-permute-done.12.rest_3_), channel_id=1, source_target_pairs={{0,14},{1,15},{2,0},{3,1},{4,2},{5,3},{6,4},{7,5},{8,6},{9,7},{10,... | collective-permute-start | bytes 393224 | tf_op jit(solution)/shard_map/ppermute | solution.py:333
  105.2 6.1 %collective-permute-start.15 = (bf16[32,1024]{1,0:T(8,128)(2,1)S(1)}, bf16[32,1024]{1,0:T(8,128)(2,1)S(1)}, u32[]{:S(2)}, u32[]{:S(2)}) collective-permute-start(bf16[32,1024]{1,0:T(8,128)(2,1)S(1)} %slice.24), channel_id=1, source_target_pairs={{0,4},{1,5},{2,6},{3,7},{4,8},{5,9},{6,10},{7,11},{8,12},{9,13},{1... | collective-permute-start | bytes 196616 | tf_op jit(solution)/shard_map/ppermute | solution.py:333
  108.7 6.5 %collective-permute-start.16 = (bf16[32,1024]{1,0:T(8,128)(2,1)S(1)}, bf16[32,1024]{1,0:T(8,128)(2,1)S(1)}, u32[]{:S(2)}, u32[]{:S(2)}) collective-permute-start(bf16[32,1024]{1,0:T(8,128)(2,1)S(1)} %slice.25), channel_id=1, source_target_pairs={{0,12},{1,13},{2,14},{3,15},{4,0},{5,1},{6,2},{7,3},{8,4},{9,5},{1... | collective-permute-start | bytes 196616 | tf_op jit(solution)/shard_map/ppermute | solution.py:333
  116.5 2.0 %collective-permute-start.17 = (f32[16,8,1024]{2,1,0:T(8,128)S(1)}, f32[16,8,1024]{2,1,0:T(8,128)S(1)}, u32[]{:S(2)}, u32[]{:S(2)}) collective-permute-start(f32[16,8,1024]{2,1,0:T(8,128)S(1)} %get-tuple-element.46), channel_id=1, source_target_pairs={{0,1},{1,0},{2,3},{3,2},{4,5},{5,4},{6,7},{7,6},{8,9},{9,8},{10,11... | collective-permute-start | bytes 1572872 | tf_op jit(solution)/shard_map/ppermute | solution.py:440
Sparse Core Ops, SparseCore 0:
  26.4 51.0 all-gather.2

commit v6 on v5

--- a/solution.py
+++ b/solution.py
@@ -133,8 +133,10 @@
     lax.fori_loop(0, out_ref.shape[0], place, 0, unroll=8)
 
 
-def gather_kernel(core_ref, count_ref, near_ref, own_ref, other_ref, out_ref, front):
+def gather_kernel(core_ref, count_ref, near_hbm, own_ref, other_ref, out_ref, front, near_ref, sem):
     core = core_ref[0]
+    fetch = pltpu.make_async_copy(near_hbm, near_ref, sem)
+    fetch.start()
     lane = lane_of((HALF, BLOCK))
     row = lax.broadcasted_iota(jnp.int32, (HALF, BLOCK), 0)
     straight = (lane < HALF) == (core == 0)
@@ -151,6 +153,7 @@
         return carry
 
     lax.fori_loop(0, own_ref.shape[0], place, 0, unroll=8)
+    fetch.wait()
 
     def average(step, carry):
         group, part = lax.div(step, 2), lax.rem(step, 2)
@@ -397,8 +400,12 @@
     mean = call(
         gather_kernel,
         shape((ring, 64, BLOCK), F32),
-        [SMEM, SMEM, SMEM, VMEM, VMEM],
-        [pltpu.VMEM((owner_ids.shape[0] * BLOCK, BLOCK), F32)],
+        [SMEM, SMEM, ANY, VMEM, VMEM],
+        [
+            pltpu.VMEM((owner_ids.shape[0] * BLOCK, BLOCK), F32),
+            pltpu.SMEM(near.shape, jnp.int32),
+            pltpu.SemaphoreType.DMA,
+        ],
         cost=cost(0, 30 << 20),
     )(core, counts, near, entries, lax.ppermute(entries, "feat", across))
 

time: 156 us -> 155 us (level)
  no operation moved by 1% of the time
where the time goes in v6:
time: 155 us
  starting transfers between devices  49.4 us (32%)
  waiting for transfers between devices  30.8 us (20%)
  Pallas kernels  29.2 us (19%)
  blocking collectives  28.8 us (19%)
  between operations  14.3 us (9%)
  local copies, waits for them, and re-layouts  2.12 us (1%)
    ppermute x15, starting transfers between devices, climb(): return lax.ppermute(value, 'feat', pairs)  28.9 us
    all_to_all x1, blocking collectives, body(): lax.all_to_all(partial, 'dom', split_axis=0, concat_axis=0, tiled=True)  14.8 us
    all_to_all x1, blocking collectives, body(): lax.all_to_all(total, 'dom', split_axis=0, concat_axis=0, tiled=True)  14 us
    ppermute x15, waiting for transfers between devices, climb(): return lax.ppermute(value, 'feat', pairs)  12.2 us
    pallas_call x1, Pallas kernels, body(): call(gather_kernel, shape((ring, 64, BLOCK), F32), [SMEM, SMEM, ANY, VMEM...  9.06 us
    all_to_all x1, starting transfers between devices, body(): lax.all_to_all(mean, 'feat', split_axis=0, concat_axis=0, tiled=True, axi...  8.13 us
    all_to_all x1, starting transfers between devices, body(): lax.all_to_all(request, 'dom', split_axis=0, concat_axis=0, tiled=True)  7.03 us
    all_to_all x1, waiting for transfers between devices, body(): lax.all_to_all(mean, 'feat', split_axis=0, concat_axis=0, tiled=True, axi...  5.46 us
  transfers between devices with their start and end apart: 22, of which 12 were waited for; matrix products, arithmetic and copies ran while one was open for 0% of the time, Pallas kernels for 14%

profile of v6, /device:TPU:64, one launch (start us, length us, event | category | flops | bytes accessed | tf_op | source)
XLA Modules:
  0.0 154.6 jit_solution(3554802360753251416)
XLA Ops:
  7.2 1.5 shard_map.121
  8.7 7.0 %all-to-all-start = ((s32[16,1,128]{2,1,0:T(1,128)}), s32[16,1,128]{2,1,0:T(1,128)S(1)}, u32[]{:S(2)}, u32[]{:S(2)}) async-start(s32[16,1,128]{2,1,0:T(1,128)} %shard_map.121), calls=%async_computation | async-start | bytes 16384 | tf_op jit(solution)/shard_map/all_to_all | solution.py:344
  15.8 5.1 %shard_map.122 = (bf16[64,64,128]{2,1,0:T(8,128)(2,1)}, f32[8,64,128]{2,1,0:T(8,128)}, f32[8,64,128]{2,1,0:T(8,128)}) custom-call(s32[1]{0:T(128)S(6)} %select_n.12.core_ref, s32[1024]{0:T(1024)} %seed_hbm.1, f32[64,8192]{1,0:T(8,128)} %table_hbm.1), custom_call_target="tpu_custom_call" | custom-call | bytes 10485760 | tf_op jit(solution)/shard_map/pallas_call | solution.py:346
  20.8 2.4 %all-to-all-done.request_hbm = s32[16,1,128]{2,1,0:T(1,128)S(1)} async-done(((s32[16,1,128]{2,1,0:T(1,128)}), s32[16,1,128]{2,1,0:T(1,128)S(1)}, u32[]{:S(2)}, u32[]{:S(2)}) %all-to-all-start) | async-done | bytes 8224 | tf_op jit(solution)/shard_map/all_to_all | solution.py:344
  23.2 3.1 %shard_map.123 = (bf16[16,8,64,128]{3,2,1,0:T(8,128)(2,1)}, bf16[3,64,1024]{2,1,0:T(8,128)(2,1)}) custom-call(s32[16,1,128]{2,1,0:T(1,128)S(1)} %all-to-all-done.request_hbm, bf16[64,64,128]{2,1,0:T(8,128)(2,1)} %get-tuple-element.25.packed_hbm, f32[64,1024]{1,0:T(8,128)} %self_hbm.1, f32[64,1024]{1,0:T(8,128)} %neigh_hbm.1), custom_call_target="tpu_custom_call" | custom-call | tf_op jit(solution)/shard_map/pallas_call | solution.py:366
  26.3 5.0 %all-to-all-start.1 = ((bf16[16,512,128]{2,1,0:T(8,128)(2,1)}), bf16[16,512,128]{2,1,0:T(8,128)(2,1)S(1)}, u32[]{:S(2)}, u32[]{:S(2)}) async-start(bf16[16,512,128]{2,1,0:T(8,128)(2,1)} %bitcast.18), calls=%async_computation.1 | async-start | bytes 4194304 | tf_op jit(solution)/shard_map/all_to_all | solution.py:384
  31.6 1.4 collective-permute-done.other_ref
  33.7 1.9 %shard_map.124 = (f32[8,64,128]{2,1,0:T(8,128)}, f32[64,128]{1,0:T(8,128)S(1)}, f32[64,128]{1,0:T(8,128)S(1)}, f32[64,128]{1,0:T(8,128)S(1)}, f32[64,128]{1,0:T(...) custom-call(s32[2]{0:T(128)S(1)} %pad_add_fusion.place_ref, ...), custom_call_target="tpu_custom_call" | custom-call | bytes 1048576 | tf_op jit(solution)/shard_map/pallas_call | solution.py:387
  35.6 1.9 %collective-permute-start.1 = (f32[64,128]{1,0:T(8,128)S(1)}, f32[64,128]{1,0:T(8,128)S(1)}, u32[]{:S(2)}, u32[]{:S(2)}) collective-permute-start(f32[64,128]{1,0:T(8,128)S(1)} %get-tuple-element.29), channel_id=1, source_target_pairs={{0,2},{1,3},{2,4},{3,5},{4,6},{5,7},{6,8},{7,9},{8,10},{9,11},{10,... | collective-permute-start | bytes 98312 | tf_op jit(solution)/shard_map/ppermute | solution.py:336
  37.6 5.7 %collective-permute-start.3 = (f32[64,128]{1,0:T(8,128)S(1)}, f32[64,128]{1,0:T(8,128)S(1)}, u32[]{:S(2)}, u32[]{:S(2)}) collective-permute-start(f32[64,128]{1,0:T(8,128)S(1)} %get-tuple-element.31), channel_id=1, source_target_pairs={{0,4},{1,5},{2,6},{3,7},{4,8},{5,9},{6,10},{7,11},{8,12},{9,13},{1... | collective-permute-start | bytes 98312 | tf_op jit(solution)/shard_map/ppermute | solution.py:336
  43.3 3.4 %collective-permute-start.5 = (f32[64,128]{1,0:T(8,128)S(1)}, f32[64,128]{1,0:T(8,128)S(1)}, u32[]{:S(2)}, u32[]{:S(2)}) collective-permute-start(f32[64,128]{1,0:T(8,128)S(1)} %get-tuple-element.33), channel_id=1, source_target_pairs={{0,6},{1,7},{2,8},{3,9},{4,10},{5,11},{6,12},{7,13},{8,14},{9,15},... | collective-permute-start | bytes 98312 | tf_op jit(solution)/shard_map/ppermute | solution.py:336
  46.7 1.7 %collective-permute-start.6 = (f32[64,128]{1,0:T(8,128)S(1)}, f32[64,128]{1,0:T(8,128)S(1)}, u32[]{:S(2)}, u32[]{:S(2)}) collective-permute-start(f32[64,128]{1,0:T(8,128)S(1)} %get-tuple-element.34), channel_id=1, source_target_pairs={{0,10},{1,11},{2,12},{3,13},{4,14},{5,15},{6,0},{7,1},{8,2},{9,3},... | collective-permute-start | bytes 98312 | tf_op jit(solution)/shard_map/ppermute | solution.py:336
  48.4 2.6 %collective-permute-start.7 = (f32[64,128]{1,0:T(8,128)S(1)}, f32[64,128]{1,0:T(8,128)S(1)}, u32[]{:S(2)}, u32[]{:S(2)}) collective-permute-start(f32[64,128]{1,0:T(8,128)S(1)} %get-tuple-element.35), channel_id=1, source_target_pairs={{0,8},{1,9},{2,10},{3,11},{4,12},{5,13},{6,14},{7,15},{8,0},{9,1},... | collective-permute-start | bytes 98312 | tf_op jit(solution)/shard_map/ppermute | solution.py:336
  51.6 3.7 %collective-permute-done.6.rest_5_.rest_6_ = f32[64,128]{1,0:T(8,128)S(1)} collective-permute-done((f32[64,128]{1,0:T(8,128)S(1)}, f32[64,128]{1,0:T(8,128)S(1)}, u32[]{:S(2)}, u32[]{:S(2)}) %collective-permute-start.6) | collective-permute-done | bytes 32800 | tf_op jit(solution)/shard_map/ppermute | solution.py:336
  55.3 1.7 %collective-permute-done.7.rest_6_.rest_7_ = f32[64,128]{1,0:T(8,128)S(1)} collective-permute-done((f32[64,128]{1,0:T(8,128)S(1)}, f32[64,128]{1,0:T(8,128)S(1)}, u32[]{:S(2)}, u32[]{:S(2)}) %collective-permute-start.7) | collective-permute-done | bytes 32800 | tf_op jit(solution)/shard_map/ppermute | solution.py:336
  56.9 4.7 %all-to-all-done.1 = bf16[16,512,128]{2,1,0:T(8,128)(2,1)S(1)} async-done(((bf16[16,512,128]{2,1,0:T(8,128)(2,1)}), bf16[16,512,128]{2,1,0:T(8,128)(2,1)S(1)}, u32[]{:S(2)}, u32[]{:S(2)}) %all-to-all-start.1) | async-done | bytes 2097184 | tf_op jit(solution)/shard_map/all_to_all | solution.py:384
  62.6 2.6 %collective-permute-done.8.other_ref = bf16[64,64,128]{2,1,0:T(8,128)(2,1)S(1)} collective-permute-done((bf16[64,64,128]{2,1,0:T(8,128)(2,1)S(1)}, bf16[64,64,128]{2,1,0:T(8,128)(2,1)S(1)}, u32[]{:S(2)}, u32[]{:S(2)}) %collective-permute-start.8) | collective-permute-done | bytes 1048608 | tf_op jit(solution)/shard_map/ppermute | solution.py:410
  65.3 9.1 %shard_map.126.mean_ref = f32[8,64,128]{2,1,0:T(8,128)} custom-call(s32[1]{0:T(128)S(6)} %select_n.12.core_ref, s32[64]{0:T(128)S(1)} %copy-done.4, s32[15360]{0:T(1024)S(1)} %reshape.26.rest_7_.near_hbm, bf16[64,64,128]{2,1,0:T(8,128)(2,1)S(1)} %shard_map.125.own_ref, bf16[64,64,128]{2,1,0:T(8,128)(2,1)S(1)} %collective-permute-done.8.other_ref), custom_call_target="tpu_custom_call" | custom-call | bytes 31457280 | tf_op jit(solution)/shard_map/pallas_call | solution.py:400
  74.4 8.1 %all-to-all-start.2 = ((f32[8,64,128]{2,1,0:T(8,128)}), f32[8,64,128]{2,1,0:T(8,128)S(1)}, u32[]{:S(2)}, u32[]{:S(2)}) async-start(f32[8,64,128]{2,1,0:T(8,128)} %shard_map.126.mean_ref), calls=%async_computation.2 | async-start | bytes 524288 | tf_op jit(solution)/shard_map/all_to_all | solution.py:424
  82.5 3.6 %shard_map.127 = (f32[64,1024]{1,0:T(8,128)S(1)}, bf16[16,64,1024]{2,1,0:T(8,128)(2,1)S(1)}) custom-call(s32[2]{0:T(128)S(1)} %pad_add_fusion.place_ref, f32[1,1024]{1,0:T(1,128)S(1)} %bitcast.14, bf16[16,3,64,1024]{3,2,1,0:T(8,128)(2,1)} %bitcast.17, f32[64,128]{1,0:T(8,128)S(1)} %get-tuple-element.37.rest_0_, ...), custom_call_target="tpu_custom_call" | custom-call | flops 402653184 | bytes 9437184 | tf_op jit(solution)/shard_map/pallas_call | solution.py:412
  86.1 5.5 %all-to-all-done.2.mean_ref = f32[8,64,128]{2,1,0:T(8,128)S(1)} async-done(((f32[8,64,128]{2,1,0:T(8,128)}), f32[8,64,128]{2,1,0:T(8,128)S(1)}, u32[]{:S(2)}, u32[]{:S(2)}) %all-to-all-start.2) | async-done | bytes 262176 | tf_op jit(solution)/shard_map/all_to_all | solution.py:424
  91.6 1.6 %shard_map.128 = (bf16[64,1024]{1,0:T(8,128)(2,1)}, bf16[64,1024]{1,0:T(8,128)(2,1)S(1)}) custom-call(f32[8,64,128]{2,1,0:T(8,128)S(1)} %all-to-all-done.2.mean_ref, f32[64,1024]{1,0:T(8,128)S(1)} %get-tuple-element.38.part_ref, bf16[16,64,1024]{2,1,0:T(8,128)(2,1)S(1)} %get-tuple-element.39.weight_ref, bf16[64,1024]{1,0:T(8,128)(2,1)S(1)} %copy-done.1), custom_call_target="tpu_custom_call" | custom-call | flops 268435456 | bytes 4194304 | tf_op jit(solution)/shard_map/pallas_call | solution.py:428
  94.4 1.8 %collective-permute-start.12 = (bf16[64,1024]{1,0:T(8,128)(2,1)S(1)}, bf16[64,1024]{1,0:T(8,128)(2,1)S(1)}, u32[]{:S(2)}, u32[]{:S(2)}) collective-permute-start(bf16[64,1024]{1,0:T(8,128)(2,1)S(1)} %get-tuple-element.44.near_ref), channel_id=1, source_target_pairs={{0,12},{1,13},{2,14},{3,15},{4,0},{5,1},{6,2},{7,3},{8,4},{9,5},{1... | collective-permute-start | bytes 393224 | tf_op jit(solution)/shard_map/ppermute | solution.py:336
  96.2 3.2 %collective-permute-start.10 = (bf16[64,1024]{1,0:T(8,128)(2,1)S(1)}, bf16[64,1024]{1,0:T(8,128)(2,1)S(1)}, u32[]{:S(2)}, u32[]{:S(2)}) collective-permute-start(bf16[64,1024]{1,0:T(8,128)(2,1)S(1)} %get-tuple-element.44.near_ref), channel_id=1, source_target_pairs={{0,14},{1,15},{2,0},{3,1},{4,2},{5,3},{6,4},{7,5},{8,6},{9,7},{10,... | collective-permute-start | bytes 393224 | tf_op jit(solution)/shard_map/ppermute | solution.py:336
  100.2 2.7 %collective-permute-start.13 = (bf16[64,1024]{1,0:T(8,128)(2,1)S(1)}, bf16[64,1024]{1,0:T(8,128)(2,1)S(1)}, u32[]{:S(2)}, u32[]{:S(2)}) collective-permute-start(bf16[64,1024]{1,0:T(8,128)(2,1)S(1)} %collective-permute-done.11.rest_2_), channel_id=1, source_target_pairs={{0,2},{1,3},{2,4},{3,5},{4,6},{5,7},{6,8},{7,9},{8,10},{9,11},{10,... | collective-permute-start | bytes 393224 | tf_op jit(solution)/shard_map/ppermute | solution.py:336
  102.9 1.3 collective-permute-done.12.rest_3_
  104.7 3.5 %collective-permute-start.15 = (bf16[32,1024]{1,0:T(8,128)(2,1)S(1)}, bf16[32,1024]{1,0:T(8,128)(2,1)S(1)}, u32[]{:S(2)}, u32[]{:S(2)}) collective-permute-start(bf16[32,1024]{1,0:T(8,128)(2,1)S(1)} %slice.24), channel_id=1, source_target_pairs={{0,4},{1,5},{2,6},{3,7},{4,8},{5,9},{6,10},{7,11},{8,12},{9,13},{1... | collective-permute-start | bytes 196616 | tf_op jit(solution)/shard_map/ppermute | solution.py:336
  110.9 3.9 %collective-permute-done.16.rest_7_ = bf16[32,1024]{1,0:T(8,128)(2,1)S(1)} collective-permute-done((bf16[32,1024]{1,0:T(8,128)(2,1)S(1)}, bf16[32,1024]{1,0:T(8,128)(2,1)S(1)}, u32[]{:S(2)}, u32[]{:S(2)}) %collective-permute-start.16) | collective-permute-done | bytes 65568 | tf_op jit(solution)/shard_map/ppermute | solution.py:336
  114.7 1.3 shard_map.130
  116.1 1.9 %collective-permute-done.17.right_ref = f32[16,8,1024]{2,1,0:T(8,128)S(1)} collective-permute-done((f32[16,8,1024]{2,1,0:T(8,128)S(1)}, f32[16,8,1024]{2,1,0:T(8,128)S(1)}, u32[]{:S(2)}, u32[]{:S(2)}) %collective-permute-start.17) | collective-permute-done | bytes 524320 | tf_op jit(solution)/shard_map/ppermute | solution.py:447
  118.1 14.8 %all_to_all.25.in_ref = f32[16,8,1024]{2,1,0:T(8,128)S(1)} all-to-all(f32[16,8,1024]{2,1,0:T(8,128)S(1)} %shard_map.131), channel_id=1, replica_groups=mesh['dom'=16,'feat'=16] {'dom'}, dimensions={0} | all-to-all | bytes 1048576 | tf_op jit(solution)/shard_map/all_to_all | solution.py:449
  132.9 14.0 %all_to_all.26 = f32[16,8,1024]{2,1,0:T(8,128)S(1)} all-to-all(f32[16,8,1024]{2,1,0:T(8,128)S(1)} %shard_map.132), channel_id=1, replica_groups=mesh['dom'=16,'feat'=16] {'dom'}, dimensions={0} | all-to-all | bytes 1048576 | tf_op jit(solution)/shard_map/all_to_all | solution.py:451
  (49 shorter events, 8.8 us)
Async XLA Ops:
  8.7 14.5 %all-to-all-start = ((s32[16,1,128]{2,1,0:T(1,128)}), s32[16,1,128]{2,1,0:T(1,128)S(1)}, u32[]{:S(2)}, u32[]{:S(2)}) async-start(s32[16,1,128]{2,1,0:T(1,128)} %shard_map.121), calls=%async_computation | async-start | bytes 16384 | tf_op jit(solution)/shard_map/all_to_all | solution.py:344
  15.7 66.8 %all-gather.3.cloned.1.call-start = ((), (), s32[]{:S(2)}) async-start(), calls=%async_computation.5 | async-start | bytes 6684672 | tf_op jit(solution)/shard_map/all_gather | solution.py:383
  26.3 5.1 %copy-start.7 = (f32[8,64,128]{2,1,0:T(8,128)S(1)}, f32[8,64,128]{2,1,0:T(8,128)}, u32[]{:S(2)}) copy-start(f32[8,64,128]{2,1,0:T(8,128)} %get-tuple-element.28) | copy-start | bytes 786436
  26.3 24.7 %copy-start.6 = (s32[15,1024]{1,0:T(8,128)S(1)}, s32[15,1024]{1,0:T(8,128)}, u32[]{:S(2)}) copy-start(s32[15,1024]{1,0:T(8,128)} %param.12) | copy-start | bytes 184324
  26.3 35.3 %copy-start.3 = (s32[64,1]{0,1:T(1,128)S(1)}, s32[64,1]{0,1:T(1,128)}, u32[]{:S(2)}) copy-start(s32[64,1]{0,1:T(1,128)} %param.13) | copy-start | bytes 772
  26.3 35.3 %all-to-all-start.1 = ((bf16[16,512,128]{2,1,0:T(8,128)(2,1)}), bf16[16,512,128]{2,1,0:T(8,128)(2,1)S(1)}, u32[]{:S(2)}, u32[]{:S(2)}) async-start(bf16[16,512,128]{2,1,0:T(8,128)(2,1)} %bitcast.18), calls=%async_computation.1 | async-start | bytes 4194304 | tf_op jit(solution)/shard_map/all_to_all | solution.py:384
  31.4 1.6 %collective-permute-start = (f32[8,64,128]{2,1,0:T(8,128)S(1)}, f32[8,64,128]{2,1,0:T(8,128)S(1)}, u32[]{:S(2)}, u32[]{:S(2)}) collective-permute-start(f32[8,64,128]{2,1,0:T(8,128)S(1)} %copy-done.7), channel_id=1, source_target_pairs={{0,1},{1,0},{2,3},{3,2},{4,5},{5,4},{6,7},{7,6},{8,9},{9,8},{10,11... | collective-permute-start | bytes 786440 | tf_op jit(solution)/shard_map/ppermute | solution.py:392
  33.0 0.7 copy-start.5
  35.6 11.1 %collective-permute-start.1 = (f32[64,128]{1,0:T(8,128)S(1)}, f32[64,128]{1,0:T(8,128)S(1)}, u32[]{:S(2)}, u32[]{:S(2)}) collective-permute-start(f32[64,128]{1,0:T(8,128)S(1)} %get-tuple-element.29), channel_id=1, source_target_pairs={{0,2},{1,3},{2,4},{3,5},{4,6},{5,7},{6,8},{7,9},{8,10},{9,11},{10,... | collective-permute-start | bytes 98312 | tf_op jit(solution)/shard_map/ppermute | solution.py:336
  37.5 10.8 %collective-permute-start.2 = (f32[64,128]{1,0:T(8,128)S(1)}, f32[64,128]{1,0:T(8,128)S(1)}, u32[]{:S(2)}, u32[]{:S(2)}) collective-permute-start(f32[64,128]{1,0:T(8,128)S(1)} %get-tuple-element.30), channel_id=1, source_target_pairs={{0,14},{1,15},{2,0},{3,1},{4,2},{5,3},{6,4},{7,5},{8,6},{9,7},{10,... | collective-permute-start | bytes 98312 | tf_op jit(solution)/shard_map/ppermute | solution.py:336
  37.6 13.9 %collective-permute-start.3 = (f32[64,128]{1,0:T(8,128)S(1)}, f32[64,128]{1,0:T(8,128)S(1)}, u32[]{:S(2)}, u32[]{:S(2)}) collective-permute-start(f32[64,128]{1,0:T(8,128)S(1)} %get-tuple-element.31), channel_id=1, source_target_pairs={{0,4},{1,5},{2,6},{3,7},{4,8},{5,9},{6,10},{7,11},{8,12},{9,13},{1... | collective-permute-start | bytes 98312 | tf_op jit(solution)/shard_map/ppermute | solution.py:336
  43.3 8.2 %collective-permute-start.4 = (f32[64,128]{1,0:T(8,128)S(1)}, f32[64,128]{1,0:T(8,128)S(1)}, u32[]{:S(2)}, u32[]{:S(2)}) collective-permute-start(f32[64,128]{1,0:T(8,128)S(1)} %get-tuple-element.32), channel_id=1, source_target_pairs={{0,12},{1,13},{2,14},{3,15},{4,0},{5,1},{6,2},{7,3},{8,4},{9,5},{1... | collective-permute-start | bytes 98312 | tf_op jit(solution)/shard_map/ppermute | solution.py:336
  43.3 8.2 %collective-permute-start.5 = (f32[64,128]{1,0:T(8,128)S(1)}, f32[64,128]{1,0:T(8,128)S(1)}, u32[]{:S(2)}, u32[]{:S(2)}) collective-permute-start(f32[64,128]{1,0:T(8,128)S(1)} %get-tuple-element.33), channel_id=1, source_target_pairs={{0,6},{1,7},{2,8},{3,9},{4,10},{5,11},{6,12},{7,13},{8,14},{9,15},... | collective-permute-start | bytes 98312 | tf_op jit(solution)/shard_map/ppermute | solution.py:336
  46.7 8.6 %collective-permute-start.6 = (f32[64,128]{1,0:T(8,128)S(1)}, f32[64,128]{1,0:T(8,128)S(1)}, u32[]{:S(2)}, u32[]{:S(2)}) collective-permute-start(f32[64,128]{1,0:T(8,128)S(1)} %get-tuple-element.34), channel_id=1, source_target_pairs={{0,10},{1,11},{2,12},{3,13},{4,14},{5,15},{6,0},{7,1},{8,2},{9,3},... | collective-permute-start | bytes 98312 | tf_op jit(solution)/shard_map/ppermute | solution.py:336
  48.4 8.6 %collective-permute-start.7 = (f32[64,128]{1,0:T(8,128)S(1)}, f32[64,128]{1,0:T(8,128)S(1)}, u32[]{:S(2)}, u32[]{:S(2)}) collective-permute-start(f32[64,128]{1,0:T(8,128)S(1)} %get-tuple-element.35), channel_id=1, source_target_pairs={{0,8},{1,9},{2,10},{3,11},{4,12},{5,13},{6,14},{7,15},{8,0},{9,1},... | collective-permute-start | bytes 98312 | tf_op jit(solution)/shard_map/ppermute | solution.py:336
  51.2 14.1 %copy-start.4 = (s32[64]{0:T(128)S(1)}, s32[64]{0:T(128)}, u32[]{:S(2)}) copy-start(s32[64]{0:T(128)} %count_ref.1) | copy-start | bytes 772
  62.5 20.0 %copy-start.2 = (f32[1024]{0:T(1024)S(1)}, f32[1024]{0:T(1024)}, u32[]{:S(2)}) copy-start(f32[1024]{0:T(1024)} %param.18) | copy-start | bytes 12292
  62.5 2.7 %collective-permute-start.8 = (bf16[64,64,128]{2,1,0:T(8,128)(2,1)S(1)}, bf16[64,64,128]{2,1,0:T(8,128)(2,1)S(1)}, u32[]{:S(2)}, u32[]{:S(2)}) collective-permute-start(bf16[64,64,128]{2,1,0:T(8,128)(2,1)S(1)} %shard_map.125.own_ref), channel_id=1, source_target_pairs={{0,1},{1,0},{2,3},{3,2},{4,5},{5,4},{6,7},{7,6},{8,9},{9,8},{10,11... | collective-permute-start | bytes 3145736 | tf_op jit(solution)/shard_map/ppermute | solution.py:410
  74.4 17.2 %all-to-all-start.2 = ((f32[8,64,128]{2,1,0:T(8,128)}), f32[8,64,128]{2,1,0:T(8,128)S(1)}, u32[]{:S(2)}, u32[]{:S(2)}) async-start(f32[8,64,128]{2,1,0:T(8,128)} %shard_map.126.mean_ref), calls=%async_computation.2 | async-start | bytes 524288 | tf_op jit(solution)/shard_map/all_to_all | solution.py:424
  82.5 9.1 %copy-start.1 = (bf16[64,1024]{1,0:T(8,128)(2,1)S(1)}, bf16[64,1024]{1,0:T(8,128)(2,1)}, u32[]{:S(2)}) copy-start(bf16[64,1024]{1,0:T(8,128)(2,1)} %cotangent_ref.1) | copy-start | bytes 393220
  86.1 22.6 %copy-start = (f32[8,64,128]{2,1,0:T(8,128)S(1)}, f32[8,64,128]{2,1,0:T(8,128)}, u32[]{:S(2)}) copy-start(f32[8,64,128]{2,1,0:T(8,128)} %get-tuple-element.41.self_ref) | copy-start | bytes 786436
  93.2 7.0 %collective-permute-start.11 = (bf16[64,1024]{1,0:T(8,128)(2,1)S(1)}, bf16[64,1024]{1,0:T(8,128)(2,1)S(1)}, u32[]{:S(2)}, u32[]{:S(2)}) collective-permute-start(bf16[64,1024]{1,0:T(8,128)(2,1)S(1)} %get-tuple-element.44.near_ref), channel_id=1, source_target_pairs={{0,4},{1,5},{2,6},{3,7},{4,8},{5,9},{6,10},{7,11},{8,12},{9,13},{1... | collective-permute-start | bytes 393224 | tf_op jit(solution)/shard_map/ppermute | solution.py:336
  94.4 9.7 %collective-permute-start.12 = (bf16[64,1024]{1,0:T(8,128)(2,1)S(1)}, bf16[64,1024]{1,0:T(8,128)(2,1)S(1)}, u32[]{:S(2)}, u32[]{:S(2)}) collective-permute-start(bf16[64,1024]{1,0:T(8,128)(2,1)S(1)} %get-tuple-element.44.near_ref), channel_id=1, source_target_pairs={{0,12},{1,13},{2,14},{3,15},{4,0},{5,1},{6,2},{7,3},{8,4},{9,5},{1... | collective-permute-start | bytes 393224 | tf_op jit(solution)/shard_map/ppermute | solution.py:336
  96.2 12.0 %collective-permute-start.10 = (bf16[64,1024]{1,0:T(8,128)(2,1)S(1)}, bf16[64,1024]{1,0:T(8,128)(2,1)S(1)}, u32[]{:S(2)}, u32[]{:S(2)}) collective-permute-start(bf16[64,1024]{1,0:T(8,128)(2,1)S(1)} %get-tuple-element.44.near_ref), channel_id=1, source_target_pairs={{0,14},{1,15},{2,0},{3,1},{4,2},{5,3},{6,4},{7,5},{8,6},{9,7},{10,... | collective-permute-start | bytes 393224 | tf_op jit(solution)/shard_map/ppermute | solution.py:336
  99.5 10.4 %collective-permute-start.9 = (bf16[64,1024]{1,0:T(8,128)(2,1)S(1)}, bf16[64,1024]{1,0:T(8,128)(2,1)S(1)}, u32[]{:S(2)}, u32[]{:S(2)}) collective-permute-start(bf16[64,1024]{1,0:T(8,128)(2,1)S(1)} %get-tuple-element.44.near_ref), channel_id=1, source_target_pairs={{0,2},{1,3},{2,4},{3,5},{4,6},{5,7},{6,8},{7,9},{8,10},{9,11},{10,... | collective-permute-start | bytes 393224 | tf_op jit(solution)/shard_map/ppermute | solution.py:336
  100.2 14.5 %collective-permute-start.13 = (bf16[64,1024]{1,0:T(8,128)(2,1)S(1)}, bf16[64,1024]{1,0:T(8,128)(2,1)S(1)}, u32[]{:S(2)}, u32[]{:S(2)}) collective-permute-start(bf16[64,1024]{1,0:T(8,128)(2,1)S(1)} %collective-permute-done.11.rest_2_), channel_id=1, source_target_pairs={{0,2},{1,3},{2,4},{3,5},{4,6},{5,7},{6,8},{7,9},{8,10},{9,11},{10,... | collective-permute-start | bytes 393224 | tf_op jit(solution)/shard_map/ppermute | solution.py:336
  104.2 10.6 %collective-permute-start.14 = (bf16[64,1024]{1,0:T(8,128)(2,1)S(1)}, bf16[64,1024]{1,0:T(8,128)(2,1)S(1)}, u32[]{:S(2)}, u32[]{:S(2)}) collective-permute-start(bf16[64,1024]{1,0:T(8,128)(2,1)S(1)} %collective-permute-done.12.rest_3_), channel_id=1, source_target_pairs={{0,14},{1,15},{2,0},{3,1},{4,2},{5,3},{6,4},{7,5},{8,6},{9,7},{10,... | collective-permute-start | bytes 393224 | tf_op jit(solution)/shard_map/ppermute | solution.py:336
  104.7 6.1 %collective-permute-start.15 = (bf16[32,1024]{1,0:T(8,128)(2,1)S(1)}, bf16[32,1024]{1,0:T(8,128)(2,1)S(1)}, u32[]{:S(2)}, u32[]{:S(2)}) collective-permute-start(bf16[32,1024]{1,0:T(8,128)(2,1)S(1)} %slice.24), channel_id=1, source_target_pairs={{0,4},{1,5},{2,6},{3,7},{4,8},{5,9},{6,10},{7,11},{8,12},{9,13},{1... | collective-permute-start | bytes 196616 | tf_op jit(solution)/shard_map/ppermute | solution.py:336
  108.3 6.5 %collective-permute-start.16 = (bf16[32,1024]{1,0:T(8,128)(2,1)S(1)}, bf16[32,1024]{1,0:T(8,128)(2,1)S(1)}, u32[]{:S(2)}, u32[]{:S(2)}) collective-permute-start(bf16[32,1024]{1,0:T(8,128)(2,1)S(1)} %slice.25), channel_id=1, source_target_pairs={{0,12},{1,13},{2,14},{3,15},{4,0},{5,1},{6,2},{7,3},{8,4},{9,5},{1... | collective-permute-start | bytes 196616 | tf_op jit(solution)/shard_map/ppermute | solution.py:336
  116.0 2.0 %collective-permute-start.17 = (f32[16,8,1024]{2,1,0:T(8,128)S(1)}, f32[16,8,1024]{2,1,0:T(8,128)S(1)}, u32[]{:S(2)}, u32[]{:S(2)}) collective-permute-start(f32[16,8,1024]{2,1,0:T(8,128)S(1)} %get-tuple-element.46), channel_id=1, source_target_pairs={{0,1},{1,0},{2,3},{3,2},{4,5},{5,4},{6,7},{7,6},{8,9},{9,8},{10,11... | collective-permute-start | bytes 1572872 | tf_op jit(solution)/shard_map/ppermute | solution.py:447
Sparse Core Ops, SparseCore 0:
  26.4 51.0 all-gather.2

commit v7 on v6

--- a/solution.py
+++ b/solution.py
@@ -1,3 +1,5 @@
+import functools
+
 import jax
 import jax.numpy as jnp
 from jax import lax
@@ -118,22 +120,29 @@
         copy.wait()
 
 
-def collect_kernel(owner_ref, arrived_ref, *rest):
+def collect_kernel(first, owner_ref, arrived_ref, *rest):
     out_ref, seen = rest[-2:]
     for owner in range(arrived_ref.shape[0] // SLOTS):
         seen[owner] = 0
 
+    def skip(entry, carry):
+        owner = owner_ref[entry]
+        seen[owner] = seen[owner] + 1
+        return carry
+
     def place(entry, carry):
-        owner = owner_ref[entry]
+        owner = owner_ref[first + entry]
         rank = seen[owner]
         seen[owner] = rank + 1
         out_ref[entry] = arrived_ref[owner * SLOTS + rank]
         return carry
 
+    if first:
+        lax.fori_loop(0, first, skip, 0, unroll=8)
     lax.fori_loop(0, out_ref.shape[0], place, 0, unroll=8)
 
 
-def gather_kernel(core_ref, count_ref, near_hbm, own_ref, other_ref, out_ref, front, near_ref, sem):
+def gather_kernel(core_ref, count_ref, near_hbm, own_a, own_b, other_a, other_b, out_ref, front, near_ref, sem):
     core = core_ref[0]
     fetch = pltpu.make_async_copy(near_hbm, near_ref, sem)
     fetch.start()
@@ -141,9 +150,10 @@
     row = lax.broadcasted_iota(jnp.int32, (HALF, BLOCK), 0)
     straight = (lane < HALF) == (core == 0)
 
-    def place(entry, carry):
-        own = own_ref[entry].astype(F32)
-        other = other_ref[entry].astype(F32)
+    def place(first, own_ref, other_ref, step, carry):
+        entry = first + step
+        own = own_ref[step].astype(F32)
+        other = other_ref[step].astype(F32)
         count = count_ref[entry]
         upper = jnp.where(straight, own, other)
         lower = pltpu.roll(jnp.where(straight, other, own), HALF, 1)
@@ -152,7 +162,9 @@
         front[pl.ds(start + HALF, HALF), :] = jnp.where(row < count - HALF, lower, 0.0)
         return carry
 
-    lax.fori_loop(0, own_ref.shape[0], place, 0, unroll=8)
+    half = own_a.shape[0]
+    for first, pair in ((0, (own_a, other_a)), (half, (own_b, other_b))):
+        lax.fori_loop(0, half, functools.partial(place, first, *pair), 0, unroll=8)
     fetch.wait()
 
     def average(step, carry):
@@ -393,21 +405,27 @@
     moved = [climb(sends[k % ring], k) for k in DISTANCES[1:]]
     pieces = [sends[0]] + moved
 
-    entries = call(
-        collect_kernel, shape((owner_ids.shape[0], HALF, BLOCK), BF16),
-        [SMEM, VMEM] + [ANY] * 8, [pltpu.SMEM((n_dom,), jnp.int32)], limit=2, cost=cost(0, 2 << 20),
-    )(owner_ids, arrived.reshape(n_dom * SLOTS, HALF, BLOCK), *moved, near)
+    half = owner_ids.shape[0] // 2
+    blocks_here = arrived.reshape(n_dom * SLOTS, HALF, BLOCK)
+    entries = [
+        call(
+            functools.partial(collect_kernel, first), shape((half, HALF, BLOCK), BF16),
+            [SMEM, VMEM] + [ANY] * 8, [pltpu.SMEM((n_dom,), jnp.int32)], limit=2, cost=cost(0, 1 << 20),
+        )(owner_ids, blocks_here, *moved, near)
+        for first in (0, half)
+    ]
+    swapped = [lax.ppermute(value, "feat", across) for value in entries]
     mean = call(
         gather_kernel,
         shape((ring, 64, BLOCK), F32),
-        [SMEM, SMEM, ANY, VMEM, VMEM],
+        [SMEM, SMEM, ANY] + [VMEM] * 4,
         [
             pltpu.VMEM((owner_ids.shape[0] * BLOCK, BLOCK), F32),
             pltpu.SMEM(near.shape, jnp.int32),
             pltpu.SemaphoreType.DMA,
         ],
         cost=cost(0, 30 << 20),
-    )(core, counts, near, entries, lax.ppermute(entries, "feat", across))
+    )(core, counts, near, *entries, *swapped)
 
     part, neigh_weight = call(
         self_kernel,

time: 155 us -> 157 us (1.013)
    ppermute x15, waiting for transfers between devices: 12.2 us -> 13.9 us  [climb(): return lax.ppermute(value, 'feat', pairs)]
    pallas_call x2 -> x3, Pallas kernels: 9.92 us -> 10.6 us  [the longest x1 9.06 us: body(): call(gather_kernel, shape((ring, 64, BLOCK), F32), [SMEM, SMEM, ANY] + [V...]
  transfers between devices with their start and end apart: 22 -> 23, of which waited for: 12 -> 13; matrix products, arithmetic and copies ran while one was open for 0% -> 0% of each run, Pallas kernels for 14% -> 14%
where the time goes in v7:
time: 157 us; the launch traced here: 156 us
  starting transfers between devices  49.4 us (31%)
  waiting for transfers between devices  31.5 us (20%)
  Pallas kernels  29.9 us (19%)
  blocking collectives  28.8 us (18%)
  between operations  14.3 us (9%)
  local copies, waits for them, and re-layouts  2.12 us (1%)
    ppermute x15, starting transfers between devices, climb(): return lax.ppermute(value, 'feat', pairs)  28.3 us
    all_to_all x1, blocking collectives, body(): lax.all_to_all(partial, 'dom', split_axis=0, concat_axis=0, tiled=True)  14.8 us
    all_to_all x1, blocking collectives, body(): lax.all_to_all(total, 'dom', split_axis=0, concat_axis=0, tiled=True)  14 us
    ppermute x15, waiting for transfers between devices, climb(): return lax.ppermute(value, 'feat', pairs)  13.9 us
    pallas_call x1, Pallas kernels, body(): call(gather_kernel, shape((ring, 64, BLOCK), F32), [SMEM, SMEM, ANY] + [V...  9.06 us
    all_to_all x1, starting transfers between devices, body(): lax.all_to_all(mean, 'feat', split_axis=0, concat_axis=0, tiled=True, axi...  8.14 us
    all_to_all x1, starting transfers between devices, body(): lax.all_to_all(request, 'dom', split_axis=0, concat_axis=0, tiled=True)  7.03 us
    all_to_all x1, waiting for transfers between devices, body(): lax.all_to_all(mean, 'feat', split_axis=0, concat_axis=0, tiled=True, axi...  5.68 us
  transfers between devices with their start and end apart: 23, of which 13 were waited for; matrix products, arithmetic and copies ran while one was open for 0% of the time, Pallas kernels for 14%

profile of v7, /device:TPU:64, one launch (start us, length us, event | category | flops | bytes accessed | tf_op | source)
XLA Modules:
  0.0 156.1 jit_solution(4040854752047804278)
XLA Ops:
  7.2 1.5 shard_map.121
  8.7 7.0 %all-to-all-start = ((s32[16,1,128]{2,1,0:T(1,128)}), s32[16,1,128]{2,1,0:T(1,128)S(1)}, u32[]{:S(2)}, u32[]{:S(2)}) async-start(s32[16,1,128]{2,1,0:T(1,128)} %shard_map.121), calls=%async_computation | async-start | bytes 16384 | tf_op jit(solution)/shard_map/all_to_all | solution.py:356
  15.8 5.1 %shard_map.122 = (bf16[64,64,128]{2,1,0:T(8,128)(2,1)}, f32[8,64,128]{2,1,0:T(8,128)}, f32[8,64,128]{2,1,0:T(8,128)}) custom-call(s32[1]{0:T(128)S(6)} %select_n.12.core_ref, s32[1024]{0:T(1024)} %seed_hbm.1, f32[64,8192]{1,0:T(8,128)} %table_hbm.1), custom_call_target="tpu_custom_call" | custom-call | bytes 10485760 | tf_op jit(solution)/shard_map/pallas_call | solution.py:358
  20.8 2.4 %all-to-all-done.request_hbm = s32[16,1,128]{2,1,0:T(1,128)S(1)} async-done(((s32[16,1,128]{2,1,0:T(1,128)}), s32[16,1,128]{2,1,0:T(1,128)S(1)}, u32[]{:S(2)}, u32[]{:S(2)}) %all-to-all-start) | async-done | bytes 8224 | tf_op jit(solution)/shard_map/all_to_all | solution.py:356
  23.2 3.1 %shard_map.123 = (bf16[16,8,64,128]{3,2,1,0:T(8,128)(2,1)}, bf16[3,64,1024]{2,1,0:T(8,128)(2,1)}) custom-call(s32[16,1,128]{2,1,0:T(1,128)S(1)} %all-to-all-done.request_hbm, bf16[64,64,128]{2,1,0:T(8,128)(2,1)} %get-tuple-element.25.packed_hbm, f32[64,1024]{1,0:T(8,128)} %self_hbm.1, f32[64,1024]{1,0:T(8,128)} %neigh_hbm.1), custom_call_target="tpu_custom_call" | custom-call | tf_op jit(solution)/shard_map/pallas_call | solution.py:378
  26.3 5.0 %all-to-all-start.1 = ((bf16[16,512,128]{2,1,0:T(8,128)(2,1)}), bf16[16,512,128]{2,1,0:T(8,128)(2,1)S(1)}, u32[]{:S(2)}, u32[]{:S(2)}) async-start(bf16[16,512,128]{2,1,0:T(8,128)(2,1)} %bitcast.20), calls=%async_computation.1 | async-start | bytes 4194304 | tf_op jit(solution)/shard_map/all_to_all | solution.py:396
  31.6 1.4 collective-permute-done.other_ref
  33.7 1.9 %shard_map.124 = (f32[8,64,128]{2,1,0:T(8,128)}, f32[64,128]{1,0:T(8,128)S(1)}, f32[64,128]{1,0:T(8,128)S(1)}, f32[64,128]{1,0:T(8,128)S(1)}, f32[64,128]{1,0:T(...) custom-call(s32[2]{0:T(128)S(1)} %pad_add_fusion.place_ref, ...), custom_call_target="tpu_custom_call" | custom-call | bytes 1048576 | tf_op jit(solution)/shard_map/pallas_call | solution.py:399
  35.6 1.9 %collective-permute-start.1 = (f32[64,128]{1,0:T(8,128)S(1)}, f32[64,128]{1,0:T(8,128)S(1)}, u32[]{:S(2)}, u32[]{:S(2)}) collective-permute-start(f32[64,128]{1,0:T(8,128)S(1)} %get-tuple-element.29), channel_id=1, source_target_pairs={{0,2},{1,3},{2,4},{3,5},{4,6},{5,7},{6,8},{7,9},{8,10},{9,11},{10,... | collective-permute-start | bytes 98312 | tf_op jit(solution)/shard_map/ppermute | solution.py:348
  37.6 5.7 %collective-permute-start.3 = (f32[64,128]{1,0:T(8,128)S(1)}, f32[64,128]{1,0:T(8,128)S(1)}, u32[]{:S(2)}, u32[]{:S(2)}) collective-permute-start(f32[64,128]{1,0:T(8,128)S(1)} %get-tuple-element.31), channel_id=1, source_target_pairs={{0,4},{1,5},{2,6},{3,7},{4,8},{5,9},{6,10},{7,11},{8,12},{9,13},{1... | collective-permute-start | bytes 98312 | tf_op jit(solution)/shard_map/ppermute | solution.py:348
  43.3 3.4 %collective-permute-start.5 = (f32[64,128]{1,0:T(8,128)S(1)}, f32[64,128]{1,0:T(8,128)S(1)}, u32[]{:S(2)}, u32[]{:S(2)}) collective-permute-start(f32[64,128]{1,0:T(8,128)S(1)} %get-tuple-element.33), channel_id=1, source_target_pairs={{0,6},{1,7},{2,8},{3,9},{4,10},{5,11},{6,12},{7,13},{8,14},{9,15},... | collective-permute-start | bytes 98312 | tf_op jit(solution)/shard_map/ppermute | solution.py:348
  46.7 1.7 %collective-permute-start.6 = (f32[64,128]{1,0:T(8,128)S(1)}, f32[64,128]{1,0:T(8,128)S(1)}, u32[]{:S(2)}, u32[]{:S(2)}) collective-permute-start(f32[64,128]{1,0:T(8,128)S(1)} %get-tuple-element.34), channel_id=1, source_target_pairs={{0,10},{1,11},{2,12},{3,13},{4,14},{5,15},{6,0},{7,1},{8,2},{9,3},... | collective-permute-start | bytes 98312 | tf_op jit(solution)/shard_map/ppermute | solution.py:348
  48.3 2.6 %collective-permute-start.7 = (f32[64,128]{1,0:T(8,128)S(1)}, f32[64,128]{1,0:T(8,128)S(1)}, u32[]{:S(2)}, u32[]{:S(2)}) collective-permute-start(f32[64,128]{1,0:T(8,128)S(1)} %get-tuple-element.35), channel_id=1, source_target_pairs={{0,8},{1,9},{2,10},{3,11},{4,12},{5,13},{6,14},{7,15},{8,0},{9,1},... | collective-permute-start | bytes 98312 | tf_op jit(solution)/shard_map/ppermute | solution.py:348
  51.5 3.7 %collective-permute-done.6.rest_5_.rest_6_ = f32[64,128]{1,0:T(8,128)S(1)} collective-permute-done((f32[64,128]{1,0:T(8,128)S(1)}, f32[64,128]{1,0:T(8,128)S(1)}, u32[]{:S(2)}, u32[]{:S(2)}) %collective-permute-start.6) | collective-permute-done | bytes 32800 | tf_op jit(solution)/shard_map/ppermute | solution.py:348
  55.2 1.7 %collective-permute-done.7.rest_6_.rest_7_ = f32[64,128]{1,0:T(8,128)S(1)} collective-permute-done((f32[64,128]{1,0:T(8,128)S(1)}, f32[64,128]{1,0:T(8,128)S(1)}, u32[]{:S(2)}, u32[]{:S(2)}) %collective-permute-start.7) | collective-permute-done | bytes 32800 | tf_op jit(solution)/shard_map/ppermute | solution.py:348
  56.9 4.7 %all-to-all-done.1 = bf16[16,512,128]{2,1,0:T(8,128)(2,1)S(1)} async-done(((bf16[16,512,128]{2,1,0:T(8,128)(2,1)}), bf16[16,512,128]{2,1,0:T(8,128)(2,1)S(1)}, u32[]{:S(2)}, u32[]{:S(2)}) %all-to-all-start.1) | async-done | bytes 2097184 | tf_op jit(solution)/shard_map/all_to_all | solution.py:396
  65.5 9.1 %shard_map.127.mean_ref = f32[8,64,128]{2,1,0:T(8,128)} custom-call(s32[1]{0:T(128)S(6)} %select_n.12.core_ref, s32[64]{0:T(128)S(1)} %copy-done.4, s32[15360]{0:T(1024)S(1)} %reshape.26.rest_7_.near_hbm, bf16[32,64,128]{2,1,0:T(8,128)(2,1)S(1)} %shard_map.125.own_a, bf16[32,64,128]{2,1,0:T(8,128)(2,1)S(1)} %shard_map.126.own_b, ...), custom_call_target="tpu_custom_call" | custom-call | bytes 31457280 | tf_op jit(solution)/shard_map/pallas_call | solution.py:418
  74.5 8.1 %all-to-all-start.2 = ((f32[8,64,128]{2,1,0:T(8,128)}), f32[8,64,128]{2,1,0:T(8,128)S(1)}, u32[]{:S(2)}, u32[]{:S(2)}) async-start(f32[8,64,128]{2,1,0:T(8,128)} %shard_map.127.mean_ref), calls=%async_computation.2 | async-start | bytes 524288 | tf_op jit(solution)/shard_map/all_to_all | solution.py:442
  82.7 3.6 %shard_map.128 = (f32[64,1024]{1,0:T(8,128)S(1)}, bf16[16,64,1024]{2,1,0:T(8,128)(2,1)S(1)}) custom-call(s32[2]{0:T(128)S(1)} %pad_add_fusion.place_ref, f32[1,1024]{1,0:T(1,128)S(1)} %bitcast.18, bf16[16,3,64,1024]{3,2,1,0:T(8,128)(2,1)} %bitcast.19, f32[64,128]{1,0:T(8,128)S(1)} %get-tuple-element.37.rest_0_, ...), custom_call_target="tpu_custom_call" | custom-call | flops 402653184 | bytes 9437184 | tf_op jit(solution)/shard_map/pallas_call | solution.py:430
  86.3 5.7 %all-to-all-done.2.mean_ref = f32[8,64,128]{2,1,0:T(8,128)S(1)} async-done(((f32[8,64,128]{2,1,0:T(8,128)}), f32[8,64,128]{2,1,0:T(8,128)S(1)}, u32[]{:S(2)}, u32[]{:S(2)}) %all-to-all-start.2) | async-done | bytes 262176 | tf_op jit(solution)/shard_map/all_to_all | solution.py:442
  92.0 1.6 %shard_map.129 = (bf16[64,1024]{1,0:T(8,128)(2,1)}, bf16[64,1024]{1,0:T(8,128)(2,1)S(1)}) custom-call(f32[8,64,128]{2,1,0:T(8,128)S(1)} %all-to-all-done.2.mean_ref, f32[64,1024]{1,0:T(8,128)S(1)} %get-tuple-element.38.part_ref, bf16[16,64,1024]{2,1,0:T(8,128)(2,1)S(1)} %get-tuple-element.39.weight_ref, bf16[64,1024]{1,0:T(8,128)(2,1)S(1)} %copy-done.1), custom_call_target="tpu_custom_call" | custom-call | flops 268435456 | bytes 4194304 | tf_op jit(solution)/shard_map/pallas_call | solution.py:446
  93.6 1.3 collective-permute-start.12
  94.9 1.8 %collective-permute-start.13 = (bf16[64,1024]{1,0:T(8,128)(2,1)S(1)}, bf16[64,1024]{1,0:T(8,128)(2,1)S(1)}, u32[]{:S(2)}, u32[]{:S(2)}) collective-permute-start(bf16[64,1024]{1,0:T(8,128)(2,1)S(1)} %get-tuple-element.44.near_ref), channel_id=1, source_target_pairs={{0,12},{1,13},{2,14},{3,15},{4,0},{5,1},{6,2},{7,3},{8,4},{9,5},{1... | collective-permute-start | bytes 393224 | tf_op jit(solution)/shard_map/ppermute | solution.py:348
  97.5 2.5 %collective-permute-start.11 = (bf16[64,1024]{1,0:T(8,128)(2,1)S(1)}, bf16[64,1024]{1,0:T(8,128)(2,1)S(1)}, u32[]{:S(2)}, u32[]{:S(2)}) collective-permute-start(bf16[64,1024]{1,0:T(8,128)(2,1)S(1)} %get-tuple-element.44.near_ref), channel_id=1, source_target_pairs={{0,14},{1,15},{2,0},{3,1},{4,2},{5,3},{6,4},{7,5},{8,6},{9,7},{10,... | collective-permute-start | bytes 393224 | tf_op jit(solution)/shard_map/ppermute | solution.py:348
  99.9 2.3 %collective-permute-done.12.rest_2_ = bf16[64,1024]{1,0:T(8,128)(2,1)S(1)} collective-permute-done((bf16[64,1024]{1,0:T(8,128)(2,1)S(1)}, bf16[64,1024]{1,0:T(8,128)(2,1)S(1)}, u32[]{:S(2)}, u32[]{:S(2)}) %collective-permute-start.12) | collective-permute-done | bytes 131104 | tf_op jit(solution)/shard_map/ppermute | solution.py:348
  104.2 2.3 %collective-permute-start.15 = (bf16[64,1024]{1,0:T(8,128)(2,1)S(1)}, bf16[64,1024]{1,0:T(8,128)(2,1)S(1)}, u32[]{:S(2)}, u32[]{:S(2)}) collective-permute-start(bf16[64,1024]{1,0:T(8,128)(2,1)S(1)} %collective-permute-done.13.rest_3_), channel_id=1, source_target_pairs={{0,14},{1,15},{2,0},{3,1},{4,2},{5,3},{6,4},{7,5},{8,6},{9,7},{10,... | collective-permute-start | bytes 393224 | tf_op jit(solution)/shard_map/ppermute | solution.py:348
  106.4 3.3 %collective-permute-start.16 = (bf16[32,1024]{1,0:T(8,128)(2,1)S(1)}, bf16[32,1024]{1,0:T(8,128)(2,1)S(1)}, u32[]{:S(2)}, u32[]{:S(2)}) collective-permute-start(bf16[32,1024]{1,0:T(8,128)(2,1)S(1)} %slice.24), channel_id=1, source_target_pairs={{0,4},{1,5},{2,6},{3,7},{4,8},{5,9},{6,10},{7,11},{8,12},{9,13},{1... | collective-permute-start | bytes 196616 | tf_op jit(solution)/shard_map/ppermute | solution.py:348
  112.0 4.2 %collective-permute-done.17.rest_7_ = bf16[32,1024]{1,0:T(8,128)(2,1)S(1)} collective-permute-done((bf16[32,1024]{1,0:T(8,128)(2,1)S(1)}, bf16[32,1024]{1,0:T(8,128)(2,1)S(1)}, u32[]{:S(2)}, u32[]{:S(2)}) %collective-permute-start.17) | collective-permute-done | bytes 65568 | tf_op jit(solution)/shard_map/ppermute | solution.py:348
  116.2 1.3 shard_map.131
  117.6 1.9 %collective-permute-done.18.right_ref = f32[16,8,1024]{2,1,0:T(8,128)S(1)} collective-permute-done((f32[16,8,1024]{2,1,0:T(8,128)S(1)}, f32[16,8,1024]{2,1,0:T(8,128)S(1)}, u32[]{:S(2)}, u32[]{:S(2)}) %collective-permute-start.18) | collective-permute-done | bytes 524320 | tf_op jit(solution)/shard_map/ppermute | solution.py:465
  119.5 14.8 %all_to_all.25.in_ref = f32[16,8,1024]{2,1,0:T(8,128)S(1)} all-to-all(f32[16,8,1024]{2,1,0:T(8,128)S(1)} %shard_map.132), channel_id=1, replica_groups=mesh['dom'=16,'feat'=16] {'dom'}, dimensions={0} | all-to-all | bytes 1048576 | tf_op jit(solution)/shard_map/all_to_all | solution.py:467
  134.4 14.0 %all_to_all.26 = f32[16,8,1024]{2,1,0:T(8,128)S(1)} all-to-all(f32[16,8,1024]{2,1,0:T(8,128)S(1)} %shard_map.133), channel_id=1, replica_groups=mesh['dom'=16,'feat'=16] {'dom'}, dimensions={0} | all-to-all | bytes 1048576 | tf_op jit(solution)/shard_map/all_to_all | solution.py:469
  (52 shorter events, 11.4 us)
Async XLA Ops:
  8.7 14.5 %all-to-all-start = ((s32[16,1,128]{2,1,0:T(1,128)}), s32[16,1,128]{2,1,0:T(1,128)S(1)}, u32[]{:S(2)}, u32[]{:S(2)}) async-start(s32[16,1,128]{2,1,0:T(1,128)} %shard_map.121), calls=%async_computation | async-start | bytes 16384 | tf_op jit(solution)/shard_map/all_to_all | solution.py:356
  15.7 67.0 %all-gather.3.cloned.1.call-start = ((), (), s32[]{:S(2)}) async-start(), calls=%async_computation.5 | async-start | bytes 6684672 | tf_op jit(solution)/shard_map/all_gather | solution.py:395
  26.3 5.1 %copy-start.7 = (f32[8,64,128]{2,1,0:T(8,128)S(1)}, f32[8,64,128]{2,1,0:T(8,128)}, u32[]{:S(2)}) copy-start(f32[8,64,128]{2,1,0:T(8,128)} %get-tuple-element.28) | copy-start | bytes 786436
  26.3 24.6 %copy-start.6 = (s32[15,1024]{1,0:T(8,128)S(1)}, s32[15,1024]{1,0:T(8,128)}, u32[]{:S(2)}) copy-start(s32[15,1024]{1,0:T(8,128)} %param.12) | copy-start | bytes 184324
  26.3 35.3 %copy-start.2 = (s32[64,1]{0,1:T(1,128)S(1)}, s32[64,1]{0,1:T(1,128)}, u32[]{:S(2)}) copy-start(s32[64,1]{0,1:T(1,128)} %param.13) | copy-start | bytes 772
  26.3 35.3 %all-to-all-start.1 = ((bf16[16,512,128]{2,1,0:T(8,128)(2,1)}), bf16[16,512,128]{2,1,0:T(8,128)(2,1)S(1)}, u32[]{:S(2)}, u32[]{:S(2)}) async-start(bf16[16,512,128]{2,1,0:T(8,128)(2,1)} %bitcast.20), calls=%async_computation.1 | async-start | bytes 4194304 | tf_op jit(solution)/shard_map/all_to_all | solution.py:396
  31.4 1.6 %collective-permute-start = (f32[8,64,128]{2,1,0:T(8,128)S(1)}, f32[8,64,128]{2,1,0:T(8,128)S(1)}, u32[]{:S(2)}, u32[]{:S(2)}) collective-permute-start(f32[8,64,128]{2,1,0:T(8,128)S(1)} %copy-done.7), channel_id=1, source_target_pairs={{0,1},{1,0},{2,3},{3,2},{4,5},{5,4},{6,7},{7,6},{8,9},{9,8},{10,11... | collective-permute-start | bytes 786440 | tf_op jit(solution)/shard_map/ppermute | solution.py:404
  33.0 0.7 copy-start.5
  35.6 11.1 %collective-permute-start.1 = (f32[64,128]{1,0:T(8,128)S(1)}, f32[64,128]{1,0:T(8,128)S(1)}, u32[]{:S(2)}, u32[]{:S(2)}) collective-permute-start(f32[64,128]{1,0:T(8,128)S(1)} %get-tuple-element.29), channel_id=1, source_target_pairs={{0,2},{1,3},{2,4},{3,5},{4,6},{5,7},{6,8},{7,9},{8,10},{9,11},{10,... | collective-permute-start | bytes 98312 | tf_op jit(solution)/shard_map/ppermute | solution.py:348
  37.5 10.8 %collective-permute-start.2 = (f32[64,128]{1,0:T(8,128)S(1)}, f32[64,128]{1,0:T(8,128)S(1)}, u32[]{:S(2)}, u32[]{:S(2)}) collective-permute-start(f32[64,128]{1,0:T(8,128)S(1)} %get-tuple-element.30), channel_id=1, source_target_pairs={{0,14},{1,15},{2,0},{3,1},{4,2},{5,3},{6,4},{7,5},{8,6},{9,7},{10,... | collective-permute-start | bytes 98312 | tf_op jit(solution)/shard_map/ppermute | solution.py:348
  37.6 13.9 %collective-permute-start.3 = (f32[64,128]{1,0:T(8,128)S(1)}, f32[64,128]{1,0:T(8,128)S(1)}, u32[]{:S(2)}, u32[]{:S(2)}) collective-permute-start(f32[64,128]{1,0:T(8,128)S(1)} %get-tuple-element.31), channel_id=1, source_target_pairs={{0,4},{1,5},{2,6},{3,7},{4,8},{5,9},{6,10},{7,11},{8,12},{9,13},{1... | collective-permute-start | bytes 98312 | tf_op jit(solution)/shard_map/ppermute | solution.py:348
  43.3 8.2 %collective-permute-start.4 = (f32[64,128]{1,0:T(8,128)S(1)}, f32[64,128]{1,0:T(8,128)S(1)}, u32[]{:S(2)}, u32[]{:S(2)}) collective-permute-start(f32[64,128]{1,0:T(8,128)S(1)} %get-tuple-element.32), channel_id=1, source_target_pairs={{0,12},{1,13},{2,14},{3,15},{4,0},{5,1},{6,2},{7,3},{8,4},{9,5},{1... | collective-permute-start | bytes 98312 | tf_op jit(solution)/shard_map/ppermute | solution.py:348
  43.3 8.2 %collective-permute-start.5 = (f32[64,128]{1,0:T(8,128)S(1)}, f32[64,128]{1,0:T(8,128)S(1)}, u32[]{:S(2)}, u32[]{:S(2)}) collective-permute-start(f32[64,128]{1,0:T(8,128)S(1)} %get-tuple-element.33), channel_id=1, source_target_pairs={{0,6},{1,7},{2,8},{3,9},{4,10},{5,11},{6,12},{7,13},{8,14},{9,15},... | collective-permute-start | bytes 98312 | tf_op jit(solution)/shard_map/ppermute | solution.py:348
  46.7 8.6 %collective-permute-start.6 = (f32[64,128]{1,0:T(8,128)S(1)}, f32[64,128]{1,0:T(8,128)S(1)}, u32[]{:S(2)}, u32[]{:S(2)}) collective-permute-start(f32[64,128]{1,0:T(8,128)S(1)} %get-tuple-element.34), channel_id=1, source_target_pairs={{0,10},{1,11},{2,12},{3,13},{4,14},{5,15},{6,0},{7,1},{8,2},{9,3},... | collective-permute-start | bytes 98312 | tf_op jit(solution)/shard_map/ppermute | solution.py:348
  48.3 8.6 %collective-permute-start.7 = (f32[64,128]{1,0:T(8,128)S(1)}, f32[64,128]{1,0:T(8,128)S(1)}, u32[]{:S(2)}, u32[]{:S(2)}) collective-permute-start(f32[64,128]{1,0:T(8,128)S(1)} %get-tuple-element.35), channel_id=1, source_target_pairs={{0,8},{1,9},{2,10},{3,11},{4,12},{5,13},{6,14},{7,15},{8,0},{9,1},... | collective-permute-start | bytes 98312 | tf_op jit(solution)/shard_map/ppermute | solution.py:348
  62.5 3.0 %copy-start.4 = (s32[64]{0:T(128)S(1)}, s32[64]{0:T(128)}, u32[]{:S(2)}) copy-start(s32[64]{0:T(128)} %count_ref.1) | copy-start | bytes 772
  62.5 2.0 %collective-permute-start.9 = (bf16[32,64,128]{2,1,0:T(8,128)(2,1)S(1)}, bf16[32,64,128]{2,1,0:T(8,128)(2,1)S(1)}, u32[]{:S(2)}, u32[]{:S(2)}) collective-permute-start(bf16[32,64,128]{2,1,0:T(8,128)(2,1)S(1)} %shard_map.126.own_b), channel_id=1, source_target_pairs={{0,1},{1,0},{2,3},{3,2},{4,5},{5,4},{6,7},{7,6},{8,9},{9,8},{10,11... | collective-permute-start | bytes 1572872 | tf_op jit(solution)/shard_map/ppermute | solution.py:417
  63.3 19.3 %copy-start.3 = (f32[1024]{0:T(1024)S(1)}, f32[1024]{0:T(1024)}, u32[]{:S(2)}) copy-start(f32[1024]{0:T(1024)} %param.18) | copy-start | bytes 12292
  63.4 2.1 %collective-permute-start.8 = (bf16[32,64,128]{2,1,0:T(8,128)(2,1)S(1)}, bf16[32,64,128]{2,1,0:T(8,128)(2,1)S(1)}, u32[]{:S(2)}, u32[]{:S(2)}) collective-permute-start(bf16[32,64,128]{2,1,0:T(8,128)(2,1)S(1)} %shard_map.125.own_a), channel_id=1, source_target_pairs={{0,1},{1,0},{2,3},{3,2},{4,5},{5,4},{6,7},{7,6},{8,9},{9,8},{10,11... | collective-permute-start | bytes 1572872 | tf_op jit(solution)/shard_map/ppermute | solution.py:417
  74.5 17.5 %all-to-all-start.2 = ((f32[8,64,128]{2,1,0:T(8,128)}), f32[8,64,128]{2,1,0:T(8,128)S(1)}, u32[]{:S(2)}, u32[]{:S(2)}) async-start(f32[8,64,128]{2,1,0:T(8,128)} %shard_map.127.mean_ref), calls=%async_computation.2 | async-start | bytes 524288 | tf_op jit(solution)/shard_map/all_to_all | solution.py:442
  82.7 9.3 %copy-start.1 = (bf16[64,1024]{1,0:T(8,128)(2,1)S(1)}, bf16[64,1024]{1,0:T(8,128)(2,1)}, u32[]{:S(2)}) copy-start(bf16[64,1024]{1,0:T(8,128)(2,1)} %cotangent_ref.1) | copy-start | bytes 393220
  86.3 23.5 %copy-start = (f32[8,64,128]{2,1,0:T(8,128)S(1)}, f32[8,64,128]{2,1,0:T(8,128)}, u32[]{:S(2)}) copy-start(f32[8,64,128]{2,1,0:T(8,128)} %get-tuple-element.41.self_ref) | copy-start | bytes 786436
  93.6 8.6 %collective-permute-start.12 = (bf16[64,1024]{1,0:T(8,128)(2,1)S(1)}, bf16[64,1024]{1,0:T(8,128)(2,1)S(1)}, u32[]{:S(2)}, u32[]{:S(2)}) collective-permute-start(bf16[64,1024]{1,0:T(8,128)(2,1)S(1)} %get-tuple-element.44.near_ref), channel_id=1, source_target_pairs={{0,4},{1,5},{2,6},{3,7},{4,8},{5,9},{6,10},{7,11},{8,12},{9,13},{1... | collective-permute-start | bytes 393224 | tf_op jit(solution)/shard_map/ppermute | solution.py:348
  94.9 9.3 %collective-permute-start.13 = (bf16[64,1024]{1,0:T(8,128)(2,1)S(1)}, bf16[64,1024]{1,0:T(8,128)(2,1)S(1)}, u32[]{:S(2)}, u32[]{:S(2)}) collective-permute-start(bf16[64,1024]{1,0:T(8,128)(2,1)S(1)} %get-tuple-element.44.near_ref), channel_id=1, source_target_pairs={{0,12},{1,13},{2,14},{3,15},{4,0},{5,1},{6,2},{7,3},{8,4},{9,5},{1... | collective-permute-start | bytes 393224 | tf_op jit(solution)/shard_map/ppermute | solution.py:348
  96.7 13.1 %collective-permute-start.10 = (bf16[64,1024]{1,0:T(8,128)(2,1)S(1)}, bf16[64,1024]{1,0:T(8,128)(2,1)S(1)}, u32[]{:S(2)}, u32[]{:S(2)}) collective-permute-start(bf16[64,1024]{1,0:T(8,128)(2,1)S(1)} %get-tuple-element.44.near_ref), channel_id=1, source_target_pairs={{0,2},{1,3},{2,4},{3,5},{4,6},{5,7},{6,8},{7,9},{8,10},{9,11},{10,... | collective-permute-start | bytes 393224 | tf_op jit(solution)/shard_map/ppermute | solution.py:348
  97.5 13.6 %collective-permute-start.11 = (bf16[64,1024]{1,0:T(8,128)(2,1)S(1)}, bf16[64,1024]{1,0:T(8,128)(2,1)S(1)}, u32[]{:S(2)}, u32[]{:S(2)}) collective-permute-start(bf16[64,1024]{1,0:T(8,128)(2,1)S(1)} %get-tuple-element.44.near_ref), channel_id=1, source_target_pairs={{0,14},{1,15},{2,0},{3,1},{4,2},{5,3},{6,4},{7,5},{8,6},{9,7},{10,... | collective-permute-start | bytes 393224 | tf_op jit(solution)/shard_map/ppermute | solution.py:348
  102.2 14.0 %collective-permute-start.14 = (bf16[64,1024]{1,0:T(8,128)(2,1)S(1)}, bf16[64,1024]{1,0:T(8,128)(2,1)S(1)}, u32[]{:S(2)}, u32[]{:S(2)}) collective-permute-start(bf16[64,1024]{1,0:T(8,128)(2,1)S(1)} %collective-permute-done.12.rest_2_), channel_id=1, source_target_pairs={{0,2},{1,3},{2,4},{3,5},{4,6},{5,7},{6,8},{7,9},{8,10},{9,11},{10,... | collective-permute-start | bytes 393224 | tf_op jit(solution)/shard_map/ppermute | solution.py:348
  104.2 12.1 %collective-permute-start.15 = (bf16[64,1024]{1,0:T(8,128)(2,1)S(1)}, bf16[64,1024]{1,0:T(8,128)(2,1)S(1)}, u32[]{:S(2)}, u32[]{:S(2)}) collective-permute-start(bf16[64,1024]{1,0:T(8,128)(2,1)S(1)} %collective-permute-done.13.rest_3_), channel_id=1, source_target_pairs={{0,14},{1,15},{2,0},{3,1},{4,2},{5,3},{6,4},{7,5},{8,6},{9,7},{10,... | collective-permute-start | bytes 393224 | tf_op jit(solution)/shard_map/ppermute | solution.py:348
  106.4 5.6 %collective-permute-start.16 = (bf16[32,1024]{1,0:T(8,128)(2,1)S(1)}, bf16[32,1024]{1,0:T(8,128)(2,1)S(1)}, u32[]{:S(2)}, u32[]{:S(2)}) collective-permute-start(bf16[32,1024]{1,0:T(8,128)(2,1)S(1)} %slice.24), channel_id=1, source_target_pairs={{0,4},{1,5},{2,6},{3,7},{4,8},{5,9},{6,10},{7,11},{8,12},{9,13},{1... | collective-permute-start | bytes 196616 | tf_op jit(solution)/shard_map/ppermute | solution.py:348
  109.7 6.5 %collective-permute-start.17 = (bf16[32,1024]{1,0:T(8,128)(2,1)S(1)}, bf16[32,1024]{1,0:T(8,128)(2,1)S(1)}, u32[]{:S(2)}, u32[]{:S(2)}) collective-permute-start(bf16[32,1024]{1,0:T(8,128)(2,1)S(1)} %slice.25), channel_id=1, source_target_pairs={{0,12},{1,13},{2,14},{3,15},{4,0},{5,1},{6,2},{7,3},{8,4},{9,5},{1... | collective-permute-start | bytes 196616 | tf_op jit(solution)/shard_map/ppermute | solution.py:348
  117.5 2.0 %collective-permute-start.18 = (f32[16,8,1024]{2,1,0:T(8,128)S(1)}, f32[16,8,1024]{2,1,0:T(8,128)S(1)}, u32[]{:S(2)}, u32[]{:S(2)}) collective-permute-start(f32[16,8,1024]{2,1,0:T(8,128)S(1)} %get-tuple-element.46), channel_id=1, source_target_pairs={{0,1},{1,0},{2,3},{3,2},{4,5},{5,4},{6,7},{7,6},{8,9},{9,8},{10,11... | collective-permute-start | bytes 1572872 | tf_op jit(solution)/shard_map/ppermute | solution.py:465
Sparse Core Ops, SparseCore 0:
  26.4 51.0 all-gather.2
